TPU v7x, 128 devices: a whole 4x4x4 slice. The times are simulated.
128 devices in a mesh: patch: 32 (over z, y, core), dir: 4 (over x).
Axes of the slice: x: 4, y: 4, z: 4, core: 2. Of those that a mesh axis runs over, the one named last changes fastest.
Arguments:
- right_side: float32 [96, 768, 256], P('dir', 'patch'), may hold values from -6 to 6
- guess: float32 [96, 768, 256], P('dir', 'patch'), may hold values from -3 to 3
- mask_fine: int32 [96, 768, 2], P('dir', 'patch'), may hold values 0 or 1
- mask_next: int32 [48, 384, 1], P('dir', 'patch'), may hold values 0 or 1
Outputs:
- solution: float32 [96, 768, 256], P('dir', 'patch')
All inputs are finite; a program needn't handle non-finite values. No bound on the sum of `mask_fine` or of `mask_next` on one device may be relied on, other than what follows from the above.
Results may differ from a plain program's by a relative error of at most 0.00005.
Values sent between devices are 32-bit elements; how exact they have to be, the bound alone decides.
No kernel may reach another device: no remote copies, remote signals or barrier semaphores. Data moves between devices by JAX's collectives and lax.ppermute only.
A program may use at most 64 MiB of HBM per device.

v0:
```python
import jax
import jax.numpy as jnp
from jax import lax
from jax.sharding import PartitionSpec as P

TILE = 128
SWEEPS = 3
LEVELS = 4


MASS = (
    1.0 / 5040,
    120.0 / 5040,
    1191.0 / 5040,
    2416.0 / 5040,
    1191.0 / 5040,
    120.0 / 5040,
    1.0 / 5040,
)
STIFF = (-1.0 / 120, -0.2, -0.125, 2.0 / 3, -0.125, -0.2, -1.0 / 120)
SUBDIV = (0.125, 0.5, 0.75, 0.5, 0.125)
OMEGA = 0.5
HIGHEST = lax.Precision.HIGHEST


def padded(value, sides, width):
    for axis, dim in sides:
        devices, length = (lax.axis_size(axis), value.shape[dim])
        up = [(i, (i + 1) % devices) for i in range(devices)]
        down = [(j, i) for i, j in up]
        last = lax.slice_in_dim(value, length - width, length, axis=dim)
        leading = lax.slice_in_dim(value, 0, width, axis=dim)
        before = lax.ppermute(last, axis, up)
        after = lax.ppermute(leading, axis, down)
        value = jnp.concatenate([before, value, after], axis=dim)
    return value


def table(row_count, column_count, coeffs, row_step, column_step, offset):
    row_index = lax.broadcasted_iota(jnp.int32, (row_count, column_count), 0)
    column_index = lax.broadcasted_iota(jnp.int32, (row_count, column_count), 1)
    where_at = row_step * row_index + column_step * column_index + offset
    matrix = jnp.zeros((row_count, column_count), jnp.float32)
    for position, weight_value in enumerate(coeffs):
        matrix = matrix + jnp.where(where_at == position, weight_value, 0.0).astype(jnp.float32)
    return matrix


def along_last(values, matrix):
    return jnp.einsum("uvw,jw->uvj", values, matrix, precision=HIGHEST)


def along_middle(values, matrix):
    return jnp.einsum("ij,ujw->uiw", matrix, values, precision=HIGHEST)


def along_first(values, matrix):
    old_shape = values.shape
    flat = jnp.dot(
        matrix, values.reshape(old_shape[0], old_shape[1] * old_shape[2]), precision=HIGHEST
    )
    return flat.reshape(matrix.shape[0], old_shape[1], old_shape[2])


def clear_ends(extended, width):
    position = lax.axis_index("dir")
    last_index = lax.axis_size("dir") - 1
    extent_u = extended.shape[0]
    layer_index = lax.broadcasted_iota(jnp.int32, (extent_u, 1, 1), 0)
    lower_rim = jnp.logical_and(position == 0, layer_index < width)
    upper_rim = jnp.logical_and(position == last_index, layer_index >= extent_u - width)
    return jnp.where(jnp.logical_or(lower_rim, upper_rim), 0.0, extended)


def local_tables(extent_u, extent_v, extent_w):
    return (
        table(extent_w, extent_w, MASS, -1, 1, 3),
        table(extent_w, extent_w, STIFF, -1, 1, 3),
        table(extent_v, extent_v + 6, MASS, -1, 1, 0),
        table(extent_v, extent_v + 6, STIFF, -1, 1, 0),
        table(extent_u, extent_u + 6, MASS, -1, 1, 0),
        table(extent_u, extent_u + 6, STIFF, -1, 1, 0),
    )


def operate(current, scale_factor, tables):
    mass_w, stiff_w, mass_v, stiff_v, mass_u, stiff_u = tables
    extended = clear_ends(padded(current, (("patch", 1), ("dir", 0)), 3), 3)
    mass_side = along_last(extended, mass_w)
    stiff_side = along_last(extended, stiff_w)
    first_term = along_middle(mass_side, mass_v)
    second = along_middle(mass_side, stiff_v) + along_middle(stiff_side, mass_v)
    return scale_factor * (along_first(first_term, stiff_u) + along_first(second, mass_u))


def smooth(current, load, scale_factor, active, tables):
    update = OMEGA / scale_factor * (load - operate(current, scale_factor, tables))
    if active is not None:
        update = update * active
    return current + update


def cycle(load, current, level_index, actives):
    scale_factor = float(2**level_index)
    active = actives[level_index]
    extent_u, extent_v, extent_w = load.shape
    last_level = level_index == LEVELS - 1
    tables = local_tables(extent_u, extent_v, extent_w)
    for sweep_index in range(SWEEPS):
        current = smooth(current, load, scale_factor, active, tables)
    if not last_level:
        residual_field = load - operate(current, scale_factor, tables)
        if active is not None:
            residual_field = residual_field * active
        narrowed = along_last(residual_field, table(extent_w // 2, extent_w, SUBDIV, -2, 1, 2))
        widened = clear_ends(padded(narrowed, (("patch", 1), ("dir", 0)), 2), 2)
        coarse_load = along_first(
            along_middle(widened, table(extent_v // 2, extent_v + 4, SUBDIV, -2, 1, 0)),
            table(extent_u // 2, extent_u + 4, SUBDIV, -2, 1, 0),
        )
        correction = cycle(coarse_load, jnp.zeros_like(coarse_load), level_index + 1, actives)
        spread_out = clear_ends(padded(correction, (("patch", 1), ("dir", 0)), 1), 1)
        finer = along_last(spread_out, table(extent_w, extent_w // 2, SUBDIV, 1, -2, 2))
        finer = along_middle(finer, table(extent_v, extent_v // 2 + 2, SUBDIV, 1, -2, 4))
        finer = along_first(finer, table(extent_u, extent_u // 2 + 2, SUBDIV, 1, -2, 4))
        if active is not None:
            finer = finer * active
        current = current + finer
    for sweep_index in range(SWEEPS):
        current = smooth(current, load, scale_factor, active, tables)
    return current


def on_device(right_side, guess, mask_fine, mask_next):
    actives = [
        jnp.repeat(mask_fine.astype(jnp.float32), TILE, axis=2),
        jnp.repeat(mask_next.astype(jnp.float32), TILE, axis=2),
    ] + [None] * (LEVELS - 2)
    return cycle(right_side, guess * actives[0], 0, actives)


def solution(mesh):
    in_specs = (
        P("dir", "patch", None),
        P("dir", "patch", None),
        P("dir", "patch", None),
        P("dir", "patch", None),
    )
    out_specs = P("dir", "patch", None)
    return jax.shard_map(
        on_device, mesh=mesh, in_specs=in_specs, out_specs=out_specs, check_vma=False
    )
```

profile of v0, /device:TPU:6, one launch (start us, length us, event | category | flops | bytes accessed | tf_op | source)
XLA Modules:
  0.0 514.9 jit_solution(16386987670060652742)
XLA Ops:
  0.0 5.9 %collective-permute-start.61 = (f32[3,3,32]{2,0,1:T(4,128)S(1)}, f32[3,3,32]{2,0,1:T(4,128)S(1)}, u32[]{:S(2)}, u32[]{:S(2)}) collective-permute-start(f32[3,3,32]{2,0,1:T(4,128)S(1)} %broadcast_in_dim.1139), channel_id=1, source_target_pairs={{4,0},{8,4},{12,8},{16,12},{20,16},{24,20},{28,24},{32,28},{36,32}... | collective-permute-start | bytes 3464 | tf_op jit(solution)/shard_map/ppermute | solution.py:34
  5.9 5.1 collective-permute-start.41
  14.1 5.1 collective-permute-start.1
  21.2 5.1 collective-permute-start.21
  28.5 2.8 collective-permute-done.2
  43.1 5.0 collective-permute-start.5
  50.3 3.2 collective-permute-start.6
  56.0 4.2 collective-permute-done.7
  68.4 5.1 collective-permute-start.9
  90.1 5.1 collective-permute-start.13
  112.6 5.1 collective-permute-start.17
  119.3 2.4 collective-permute-start.19
  126.3 5.1 collective-permute-start.25
  133.6 2.6 collective-permute-start.26
  137.9 3.4 collective-permute-done.27
  144.3 5.1 collective-permute-start.29
  159.2 5.1 collective-permute-start.33
  174.5 5.1 collective-permute-start.37
  187.1 5.1 collective-permute-start.45
  193.0 2.5 collective-permute-start.62
  203.1 5.1 collective-permute-start.49
  217.2 5.1 collective-permute-start.53
  231.9 5.1 collective-permute-start.57
  244.9 3.6 collective-permute-start.65
  249.9 5.0 collective-permute-done.64
  255.1 3.2 collective-permute-start.66
  263.6 5.1 collective-permute-done.68
  268.8 3.3 collective-permute-start.70
  277.3 5.1 collective-permute-done.72
  291.3 5.1 collective-permute-done.76
  306.0 5.1 collective-permute-done.80
  318.5 5.1 collective-permute-start.85
  324.8 3.2 collective-permute-start.86
  329.4 3.5 collective-permute-done.87
  333.7 5.1 collective-permute-start.89
  347.8 5.1 collective-permute-start.93
  361.8 5.1 collective-permute-start.97
  375.9 5.1 collective-permute-start.101
  389.5 5.1 collective-permute-start.105
  404.4 5.1 collective-permute-start.109
  419.3 5.1 collective-permute-start.113
  434.1 5.1 collective-permute-start.117
  448.2 5.1 collective-permute-start.121
  457.6 2.7 collective-permute-done.122
  470.0 5.1 collective-permute-start.125
  479.4 2.7 collective-permute-done.126
  491.8 5.1 collective-permute-start.129
  501.3 2.6 collective-permute-done.130
  (684 shorter events, 297.9 us)
Async XLA Ops:
  0.0 192.2 %collective-permute-start.61 = (f32[3,3,32]{2,0,1:T(4,128)S(1)}, f32[3,3,32]{2,0,1:T(4,128)S(1)}, u32[]{:S(2)}, u32[]{:S(2)}) collective-permute-start(f32[3,3,32]{2,0,1:T(4,128)S(1)} %broadcast_in_dim.1139), channel_id=1, source_target_pairs={{4,0},{8,4},{12,8},{16,12},{20,16},{24,20},{28,24},{32,28},{36,32}... | collective-permute-start | bytes 3464 | tf_op jit(solution)/shard_map/ppermute | solution.py:34
  5.9 186.3 %collective-permute-start.60 = (f32[3,3,32]{2,0,1:T(4,128)S(1)}, f32[3,3,32]{2,0,1:T(4,128)S(1)}, u32[]{:S(2)}, u32[]{:S(2)}) collective-permute-start(f32[3,3,32]{2,0,1:T(4,128)S(1)} %broadcast_in_dim.1139), channel_id=1, source_target_pairs={{0,4},{4,8},{8,12},{12,16},{16,20},{20,24},{24,28},{28,32},{32,36}... | collective-permute-start | bytes 3464 | tf_op jit(solution)/shard_map/ppermute | solution.py:33
  5.9 20.4 %collective-permute-start.41 = (f32[6,3,64]{2,0,1:T(8,128)S(1)}, f32[6,3,64]{2,0,1:T(8,128)S(1)}, u32[]{:S(2)}, u32[]{:S(2)}) collective-permute-start(f32[6,3,64]{2,0,1:T(8,128)S(1)} %broadcast.740), channel_id=1, source_target_pairs={{4,0},{8,4},{12,8},{16,12},{20,16},{24,20},{28,24},{32,28},{36,32}... | collective-permute-start | bytes 13832 | tf_op jit(solution)/shard_map/ppermute | solution.py:34
  14.1 7.2 %collective-permute-start = (f32[24,3,256]{2,0,1:T(8,128)S(1)}, f32[24,3,256]{2,0,1:T(8,128)S(1)}, u32[]{:S(2)}, u32[]{:S(2)}) collective-permute-start(f32[24,3,256]{2,0,1:T(8,128)S(1)} %get-tuple-element.31), channel_id=1, source_target_pairs={{0,4},{4,8},{8,12},{12,16},{16,20},{20,24},{24,28},{28,32},{32,36}... | collective-permute-start | bytes 221192 | tf_op jit(solution)/shard_map/ppermute | solution.py:33
  14.1 7.1 %collective-permute-start.1 = (f32[24,3,256]{2,0,1:T(8,128)S(1)}, f32[24,3,256]{2,0,1:T(8,128)S(1)}, u32[]{:S(2)}, u32[]{:S(2)}) collective-permute-start(f32[24,3,256]{2,0,1:T(8,128)S(1)} %get-tuple-element.32), channel_id=1, source_target_pairs={{4,0},{8,4},{12,8},{16,12},{20,16},{24,20},{28,24},{32,28},{36,32}... | collective-permute-start | bytes 221192 | tf_op jit(solution)/shard_map/ppermute | solution.py:34
  21.2 21.8 %collective-permute-start.21 = (f32[12,3,128]{2,0,1:T(8,128)S(1)}, f32[12,3,128]{2,0,1:T(8,128)S(1)}, u32[]{:S(2)}, u32[]{:S(2)}) collective-permute-start(f32[12,3,128]{2,0,1:T(8,128)S(1)} %broadcast.703), channel_id=1, source_target_pairs={{4,0},{8,4},{12,8},{16,12},{20,16},{24,20},{28,24},{32,28},{36,32}... | collective-permute-start | bytes 55304 | tf_op jit(solution)/shard_map/ppermute | solution.py:34
  31.3 16.8 %collective-permute-start.20 = (f32[12,3,128]{2,0,1:T(8,128)S(1)}, f32[12,3,128]{2,0,1:T(8,128)S(1)}, u32[]{:S(2)}, u32[]{:S(2)}) collective-permute-start(f32[12,3,128]{2,0,1:T(8,128)S(1)} %broadcast.703), channel_id=1, source_target_pairs={{0,4},{4,8},{8,12},{12,16},{16,20},{20,24},{24,28},{28,32},{32,36}... | collective-permute-start | bytes 55304 | tf_op jit(solution)/shard_map/ppermute | solution.py:33
  43.0 7.2 %collective-permute-start.4 = (f32[24,3,256]{2,0,1:T(8,128)S(1)}, f32[24,3,256]{2,0,1:T(8,128)S(1)}, u32[]{:S(2)}, u32[]{:S(2)}) collective-permute-start(f32[24,3,256]{2,0,1:T(8,128)S(1)} %get-tuple-element.29), channel_id=1, source_target_pairs={{0,4},{4,8},{8,12},{12,16},{16,20},{20,24},{24,28},{28,32},{32,36}... | collective-permute-start | bytes 221192 | tf_op jit(solution)/shard_map/ppermute | solution.py:33
  43.1 7.2 %collective-permute-start.5 = (f32[24,3,256]{2,0,1:T(8,128)S(1)}, f32[24,3,256]{2,0,1:T(8,128)S(1)}, u32[]{:S(2)}, u32[]{:S(2)}) collective-permute-start(f32[24,3,256]{2,0,1:T(8,128)S(1)} %get-tuple-element.30), channel_id=1, source_target_pairs={{4,0},{8,4},{12,8},{16,12},{20,16},{24,20},{28,24},{32,28},{36,32}... | collective-permute-start | bytes 221192 | tf_op jit(solution)/shard_map/ppermute | solution.py:34
  53.5 6.6 %collective-permute-start.7 = (f32[3,30,256]{2,0,1:T(4,128)S(1)}, f32[3,30,256]{2,0,1:T(4,128)S(1)}, u32[]{:S(2)}, u32[]{:S(2)}) collective-permute-start(f32[3,30,256]{2,0,1:T(4,128)S(1)} %get-tuple-element.16), channel_id=1, source_target_pairs={{1,0},{2,1},{3,2},{0,3},{5,4},{6,5},{7,6},{4,7},{9,8},{10,9},{11,1... | collective-permute-start | bytes 276488 | tf_op jit(solution)/shard_map/ppermute | solution.py:34
  68.3 7.2 %collective-permute-start.8 = (f32[24,3,256]{2,0,1:T(8,128)S(1)}, f32[24,3,256]{2,0,1:T(8,128)S(1)}, u32[]{:S(2)}, u32[]{:S(2)}) collective-permute-start(f32[24,3,256]{2,0,1:T(8,128)S(1)} %get-tuple-element.27), channel_id=1, source_target_pairs={{0,4},{4,8},{8,12},{12,16},{16,20},{20,24},{24,28},{28,32},{32,36}... | collective-permute-start | bytes 221192 | tf_op jit(solution)/shard_map/ppermute | solution.py:33
  68.4 7.1 %collective-permute-start.9 = (f32[24,3,256]{2,0,1:T(8,128)S(1)}, f32[24,3,256]{2,0,1:T(8,128)S(1)}, u32[]{:S(2)}, u32[]{:S(2)}) collective-permute-start(f32[24,3,256]{2,0,1:T(8,128)S(1)} %get-tuple-element.28), channel_id=1, source_target_pairs={{4,0},{8,4},{12,8},{16,12},{20,16},{24,20},{28,24},{32,28},{36,32}... | collective-permute-start | bytes 221192 | tf_op jit(solution)/shard_map/ppermute | solution.py:34
  90.0 7.2 %collective-permute-start.12 = (f32[24,3,256]{2,0,1:T(8,128)S(1)}, f32[24,3,256]{2,0,1:T(8,128)S(1)}, u32[]{:S(2)}, u32[]{:S(2)}) collective-permute-start(f32[24,3,256]{2,0,1:T(8,128)S(1)} %get-tuple-element.25), channel_id=1, source_target_pairs={{0,4},{4,8},{8,12},{12,16},{16,20},{20,24},{24,28},{28,32},{32,36}... | collective-permute-start | bytes 221192 | tf_op jit(solution)/shard_map/ppermute | solution.py:33
  90.1 7.1 %collective-permute-start.13 = (f32[24,3,256]{2,0,1:T(8,128)S(1)}, f32[24,3,256]{2,0,1:T(8,128)S(1)}, u32[]{:S(2)}, u32[]{:S(2)}) collective-permute-start(f32[24,3,256]{2,0,1:T(8,128)S(1)} %get-tuple-element.26), channel_id=1, source_target_pairs={{4,0},{8,4},{12,8},{16,12},{20,16},{24,20},{28,24},{32,28},{36,32}... | collective-permute-start | bytes 221192 | tf_op jit(solution)/shard_map/ppermute | solution.py:34
  112.6 6.6 %collective-permute-start.16 = (f32[24,2,128]{2,1,0:T(2,128)S(1)}, f32[24,2,128]{2,1,0:T(2,128)S(1)}, u32[]{:S(2)}, u32[]{:S(2)}) collective-permute-start(f32[24,2,128]{2,1,0:T(2,128)S(1)} %get-tuple-element.35), channel_id=1, source_target_pairs={{0,4},{4,8},{8,12},{12,16},{16,20},{20,24},{24,28},{28,32},{32,36}... | collective-permute-start | bytes 73736 | tf_op jit(solution)/shard_map/ppermute | solution.py:33
  112.6 6.6 %collective-permute-start.17 = (f32[24,2,128]{2,1,0:T(2,128)S(1)}, f32[24,2,128]{2,1,0:T(2,128)S(1)}, u32[]{:S(2)}, u32[]{:S(2)}) collective-permute-start(f32[24,2,128]{2,1,0:T(2,128)S(1)} %get-tuple-element.36), channel_id=1, source_target_pairs={{4,0},{8,4},{12,8},{16,12},{20,16},{24,20},{28,24},{32,28},{36,32}... | collective-permute-start | bytes 73736 | tf_op jit(solution)/shard_map/ppermute | solution.py:34
  126.2 6.6 %collective-permute-start.24 = (f32[12,3,128]{2,0,1:T(8,128)S(1)}, f32[12,3,128]{2,0,1:T(8,128)S(1)}, u32[]{:S(2)}, u32[]{:S(2)}) collective-permute-start(f32[12,3,128]{2,0,1:T(8,128)S(1)} %get-tuple-element.69), channel_id=1, source_target_pairs={{0,4},{4,8},{8,12},{12,16},{16,20},{20,24},{24,28},{28,32},{32,36}... | collective-permute-start | bytes 55304 | tf_op jit(solution)/shard_map/ppermute | solution.py:33
  126.3 7.3 %collective-permute-start.25 = (f32[12,3,128]{2,0,1:T(8,128)S(1)}, f32[12,3,128]{2,0,1:T(8,128)S(1)}, u32[]{:S(2)}, u32[]{:S(2)}) collective-permute-start(f32[12,3,128]{2,0,1:T(8,128)S(1)} %get-tuple-element.70), channel_id=1, source_target_pairs={{4,0},{8,4},{12,8},{16,12},{20,16},{24,20},{28,24},{32,28},{36,32}... | collective-permute-start | bytes 55304 | tf_op jit(solution)/shard_map/ppermute | solution.py:34
  144.2 6.6 %collective-permute-start.28 = (f32[12,3,128]{2,0,1:T(8,128)S(1)}, f32[12,3,128]{2,0,1:T(8,128)S(1)}, u32[]{:S(2)}, u32[]{:S(2)}) collective-permute-start(f32[12,3,128]{2,0,1:T(8,128)S(1)} %get-tuple-element.67), channel_id=1, source_target_pairs={{0,4},{4,8},{8,12},{12,16},{16,20},{20,24},{24,28},{28,32},{32,36}... | collective-permute-start | bytes 55304 | tf_op jit(solution)/shard_map/ppermute | solution.py:33
  144.3 6.6 %collective-permute-start.29 = (f32[12,3,128]{2,0,1:T(8,128)S(1)}, f32[12,3,128]{2,0,1:T(8,128)S(1)}, u32[]{:S(2)}, u32[]{:S(2)}) collective-permute-start(f32[12,3,128]{2,0,1:T(8,128)S(1)} %get-tuple-element.68), channel_id=1, source_target_pairs={{4,0},{8,4},{12,8},{16,12},{20,16},{24,20},{28,24},{32,28},{36,32}... | collective-permute-start | bytes 55304 | tf_op jit(solution)/shard_map/ppermute | solution.py:34
  159.1 6.6 %collective-permute-start.32 = (f32[12,3,128]{2,0,1:T(8,128)S(1)}, f32[12,3,128]{2,0,1:T(8,128)S(1)}, u32[]{:S(2)}, u32[]{:S(2)}) collective-permute-start(f32[12,3,128]{2,0,1:T(8,128)S(1)} %get-tuple-element.65), channel_id=1, source_target_pairs={{0,4},{4,8},{8,12},{12,16},{16,20},{20,24},{24,28},{28,32},{32,36}... | collective-permute-start | bytes 55304 | tf_op jit(solution)/shard_map/ppermute | solution.py:33
  159.2 6.6 %collective-permute-start.33 = (f32[12,3,128]{2,0,1:T(8,128)S(1)}, f32[12,3,128]{2,0,1:T(8,128)S(1)}, u32[]{:S(2)}, u32[]{:S(2)}) collective-permute-start(f32[12,3,128]{2,0,1:T(8,128)S(1)} %get-tuple-element.66), channel_id=1, source_target_pairs={{4,0},{8,4},{12,8},{16,12},{20,16},{24,20},{28,24},{32,28},{36,32}... | collective-permute-start | bytes 55304 | tf_op jit(solution)/shard_map/ppermute | solution.py:34
  174.5 6.5 %collective-permute-start.36 = (f32[12,2,64]{2,1,0:T(2,128)S(1)}, f32[12,2,64]{2,1,0:T(2,128)S(1)}, u32[]{:S(2)}, u32[]{:S(2)}) collective-permute-start(f32[12,2,64]{2,1,0:T(2,128)S(1)} %get-tuple-element.63), channel_id=1, source_target_pairs={{0,4},{4,8},{8,12},{12,16},{16,20},{20,24},{24,28},{28,32},{32,36}... | collective-permute-start | bytes 18440 | tf_op jit(solution)/shard_map/ppermute | solution.py:33
  174.5 6.5 %collective-permute-start.37 = (f32[12,2,64]{2,1,0:T(2,128)S(1)}, f32[12,2,64]{2,1,0:T(2,128)S(1)}, u32[]{:S(2)}, u32[]{:S(2)}) collective-permute-start(f32[12,2,64]{2,1,0:T(2,128)S(1)} %get-tuple-element.64), channel_id=1, source_target_pairs={{4,0},{8,4},{12,8},{16,12},{20,16},{24,20},{28,24},{32,28},{36,32}... | collective-permute-start | bytes 18440 | tf_op jit(solution)/shard_map/ppermute | solution.py:34
  187.1 8.5 %collective-permute-start.44 = (f32[6,3,64]{2,0,1:T(8,128)S(1)}, f32[6,3,64]{2,0,1:T(8,128)S(1)}, u32[]{:S(2)}, u32[]{:S(2)}) collective-permute-start(f32[6,3,64]{2,0,1:T(8,128)S(1)} %get-tuple-element.103), channel_id=1, source_target_pairs={{0,4},{4,8},{8,12},{12,16},{16,20},{20,24},{24,28},{28,32},{32,36}... | collective-permute-start | bytes 13832 | tf_op jit(solution)/shard_map/ppermute | solution.py:33
  187.1 8.4 %collective-permute-start.45 = (f32[6,3,64]{2,0,1:T(8,128)S(1)}, f32[6,3,64]{2,0,1:T(8,128)S(1)}, u32[]{:S(2)}, u32[]{:S(2)}) collective-permute-start(f32[6,3,64]{2,0,1:T(8,128)S(1)} %get-tuple-element.104), channel_id=1, source_target_pairs={{4,0},{8,4},{12,8},{16,12},{20,16},{24,20},{28,24},{32,28},{36,32}... | collective-permute-start | bytes 13832 | tf_op jit(solution)/shard_map/ppermute | solution.py:34
  203.0 6.5 %collective-permute-start.48 = (f32[6,3,64]{2,0,1:T(8,128)S(1)}, f32[6,3,64]{2,0,1:T(8,128)S(1)}, u32[]{:S(2)}, u32[]{:S(2)}) collective-permute-start(f32[6,3,64]{2,0,1:T(8,128)S(1)} %get-tuple-element.101), channel_id=1, source_target_pairs={{0,4},{4,8},{8,12},{12,16},{16,20},{20,24},{24,28},{28,32},{32,36}... | collective-permute-start | bytes 13832 | tf_op jit(solution)/shard_map/ppermute | solution.py:33
  203.1 6.5 %collective-permute-start.49 = (f32[6,3,64]{2,0,1:T(8,128)S(1)}, f32[6,3,64]{2,0,1:T(8,128)S(1)}, u32[]{:S(2)}, u32[]{:S(2)}) collective-permute-start(f32[6,3,64]{2,0,1:T(8,128)S(1)} %get-tuple-element.102), channel_id=1, source_target_pairs={{4,0},{8,4},{12,8},{16,12},{20,16},{24,20},{28,24},{32,28},{36,32}... | collective-permute-start | bytes 13832 | tf_op jit(solution)/shard_map/ppermute | solution.py:34
  217.1 6.5 %collective-permute-start.52 = (f32[6,3,64]{2,0,1:T(8,128)S(1)}, f32[6,3,64]{2,0,1:T(8,128)S(1)}, u32[]{:S(2)}, u32[]{:S(2)}) collective-permute-start(f32[6,3,64]{2,0,1:T(8,128)S(1)} %get-tuple-element.99), channel_id=1, source_target_pairs={{0,4},{4,8},{8,12},{12,16},{16,20},{20,24},{24,28},{28,32},{32,36}... | collective-permute-start | bytes 13832 | tf_op jit(solution)/shard_map/ppermute | solution.py:33
  217.2 6.5 %collective-permute-start.53 = (f32[6,3,64]{2,0,1:T(8,128)S(1)}, f32[6,3,64]{2,0,1:T(8,128)S(1)}, u32[]{:S(2)}, u32[]{:S(2)}) collective-permute-start(f32[6,3,64]{2,0,1:T(8,128)S(1)} %get-tuple-element.100), channel_id=1, source_target_pairs={{4,0},{8,4},{12,8},{16,12},{20,16},{24,20},{28,24},{32,28},{36,32}... | collective-permute-start | bytes 13832 | tf_op jit(solution)/shard_map/ppermute | solution.py:34
  333.7 6.5 %collective-permute-start.88 = (f32[6,3,64]{2,0,1:T(8,128)S(1)}, f32[6,3,64]{2,0,1:T(8,128)S(1)}, u32[]{:S(2)}, u32[]{:S(2)}) collective-permute-start(f32[6,3,64]{2,0,1:T(8,128)S(1)} %get-tuple-element.95), channel_id=1, source_target_pairs={{0,4},{4,8},{8,12},{12,16},{16,20},{20,24},{24,28},{28,32},{32,36}... | collective-permute-start | bytes 13832 | tf_op jit(solution)/shard_map/ppermute | solution.py:33
  333.7 6.5 %collective-permute-start.89 = (f32[6,3,64]{2,0,1:T(8,128)S(1)}, f32[6,3,64]{2,0,1:T(8,128)S(1)}, u32[]{:S(2)}, u32[]{:S(2)}) collective-permute-start(f32[6,3,64]{2,0,1:T(8,128)S(1)} %get-tuple-element.96), channel_id=1, source_target_pairs={{4,0},{8,4},{12,8},{16,12},{20,16},{24,20},{28,24},{32,28},{36,32}... | collective-permute-start | bytes 13832 | tf_op jit(solution)/shard_map/ppermute | solution.py:34
  347.7 6.5 %collective-permute-start.92 = (f32[6,3,64]{2,0,1:T(8,128)S(1)}, f32[6,3,64]{2,0,1:T(8,128)S(1)}, u32[]{:S(2)}, u32[]{:S(2)}) collective-permute-start(f32[6,3,64]{2,0,1:T(8,128)S(1)} %get-tuple-element.93), channel_id=1, source_target_pairs={{0,4},{4,8},{8,12},{12,16},{16,20},{20,24},{24,28},{28,32},{32,36}... | collective-permute-start | bytes 13832 | tf_op jit(solution)/shard_map/ppermute | solution.py:33
  347.8 6.5 %collective-permute-start.93 = (f32[6,3,64]{2,0,1:T(8,128)S(1)}, f32[6,3,64]{2,0,1:T(8,128)S(1)}, u32[]{:S(2)}, u32[]{:S(2)}) collective-permute-start(f32[6,3,64]{2,0,1:T(8,128)S(1)} %get-tuple-element.94), channel_id=1, source_target_pairs={{4,0},{8,4},{12,8},{16,12},{20,16},{24,20},{28,24},{32,28},{36,32}... | collective-permute-start | bytes 13832 | tf_op jit(solution)/shard_map/ppermute | solution.py:34
  361.8 6.5 %collective-permute-start.96 = (f32[6,3,64]{2,0,1:T(8,128)S(1)}, f32[6,3,64]{2,0,1:T(8,128)S(1)}, u32[]{:S(2)}, u32[]{:S(2)}) collective-permute-start(f32[6,3,64]{2,0,1:T(8,128)S(1)} %get-tuple-element.91), channel_id=1, source_target_pairs={{0,4},{4,8},{8,12},{12,16},{16,20},{20,24},{24,28},{28,32},{32,36}... | collective-permute-start | bytes 13832 | tf_op jit(solution)/shard_map/ppermute | solution.py:33
  389.4 6.6 %collective-permute-start.104 = (f32[12,3,128]{2,0,1:T(8,128)S(1)}, f32[12,3,128]{2,0,1:T(8,128)S(1)}, u32[]{:S(2)}, u32[]{:S(2)}) collective-permute-start(f32[12,3,128]{2,0,1:T(8,128)S(1)} %get-tuple-element.61), channel_id=1, source_target_pairs={{0,4},{4,8},{8,12},{12,16},{16,20},{20,24},{24,28},{28,32},{32,36}... | collective-permute-start | bytes 55304 | tf_op jit(solution)/shard_map/ppermute | solution.py:33
  389.5 6.6 %collective-permute-start.105 = (f32[12,3,128]{2,0,1:T(8,128)S(1)}, f32[12,3,128]{2,0,1:T(8,128)S(1)}, u32[]{:S(2)}, u32[]{:S(2)}) collective-permute-start(f32[12,3,128]{2,0,1:T(8,128)S(1)} %get-tuple-element.62), channel_id=1, source_target_pairs={{4,0},{8,4},{12,8},{16,12},{20,16},{24,20},{28,24},{32,28},{36,32}... | collective-permute-start | bytes 55304 | tf_op jit(solution)/shard_map/ppermute | solution.py:34
  404.3 6.6 %collective-permute-start.108 = (f32[12,3,128]{2,0,1:T(8,128)S(1)}, f32[12,3,128]{2,0,1:T(8,128)S(1)}, u32[]{:S(2)}, u32[]{:S(2)}) collective-permute-start(f32[12,3,128]{2,0,1:T(8,128)S(1)} %get-tuple-element.59), channel_id=1, source_target_pairs={{0,4},{4,8},{8,12},{12,16},{16,20},{20,24},{24,28},{28,32},{32,36}... | collective-permute-start | bytes 55304 | tf_op jit(solution)/shard_map/ppermute | solution.py:33
  404.4 6.6 %collective-permute-start.109 = (f32[12,3,128]{2,0,1:T(8,128)S(1)}, f32[12,3,128]{2,0,1:T(8,128)S(1)}, u32[]{:S(2)}, u32[]{:S(2)}) collective-permute-start(f32[12,3,128]{2,0,1:T(8,128)S(1)} %get-tuple-element.60), channel_id=1, source_target_pairs={{4,0},{8,4},{12,8},{16,12},{20,16},{24,20},{28,24},{32,28},{36,32}... | collective-permute-start | bytes 55304 | tf_op jit(solution)/shard_map/ppermute | solution.py:34
  419.2 6.6 %collective-permute-start.112 = (f32[12,3,128]{2,0,1:T(8,128)S(1)}, f32[12,3,128]{2,0,1:T(8,128)S(1)}, u32[]{:S(2)}, u32[]{:S(2)}) collective-permute-start(f32[12,3,128]{2,0,1:T(8,128)S(1)} %get-tuple-element.57), channel_id=1, source_target_pairs={{0,4},{4,8},{8,12},{12,16},{16,20},{20,24},{24,28},{28,32},{32,36}... | collective-permute-start | bytes 55304 | tf_op jit(solution)/shard_map/ppermute | solution.py:33
  419.3 6.6 %collective-permute-start.113 = (f32[12,3,128]{2,0,1:T(8,128)S(1)}, f32[12,3,128]{2,0,1:T(8,128)S(1)}, u32[]{:S(2)}, u32[]{:S(2)}) collective-permute-start(f32[12,3,128]{2,0,1:T(8,128)S(1)} %get-tuple-element.58), channel_id=1, source_target_pairs={{4,0},{8,4},{12,8},{16,12},{20,16},{24,20},{28,24},{32,28},{36,32}... | collective-permute-start | bytes 55304 | tf_op jit(solution)/shard_map/ppermute | solution.py:34
  434.0 6.5 %collective-permute-start.116 = (f32[12,1,128]{2,0,1:T(8,128)S(1)}, f32[12,1,128]{2,0,1:T(8,128)S(1)}, u32[]{:S(2)}, u32[]{:S(2)}) collective-permute-start(f32[12,1,128]{2,0,1:T(8,128)S(1)} %get-tuple-element.55), channel_id=1, source_target_pairs={{0,4},{4,8},{8,12},{12,16},{16,20},{20,24},{24,28},{28,32},{32,36}... | collective-permute-start | bytes 18440 | tf_op jit(solution)/shard_map/ppermute | solution.py:33
  448.2 7.2 %collective-permute-start.120 = (f32[24,3,256]{2,0,1:T(8,128)S(1)}, f32[24,3,256]{2,0,1:T(8,128)S(1)}, u32[]{:S(2)}, u32[]{:S(2)}) collective-permute-start(f32[24,3,256]{2,0,1:T(8,128)S(1)} %get-tuple-element.23), channel_id=1, source_target_pairs={{0,4},{4,8},{8,12},{12,16},{16,20},{20,24},{24,28},{28,32},{32,36}... | collective-permute-start | bytes 221192 | tf_op jit(solution)/shard_map/ppermute | solution.py:33
  448.2 7.1 %collective-permute-start.121 = (f32[24,3,256]{2,0,1:T(8,128)S(1)}, f32[24,3,256]{2,0,1:T(8,128)S(1)}, u32[]{:S(2)}, u32[]{:S(2)}) collective-permute-start(f32[24,3,256]{2,0,1:T(8,128)S(1)} %get-tuple-element.24), channel_id=1, source_target_pairs={{4,0},{8,4},{12,8},{16,12},{20,16},{24,20},{28,24},{32,28},{36,32}... | collective-permute-start | bytes 221192 | tf_op jit(solution)/shard_map/ppermute | solution.py:34
  469.9 7.2 %collective-permute-start.124 = (f32[24,3,256]{2,0,1:T(8,128)S(1)}, f32[24,3,256]{2,0,1:T(8,128)S(1)}, u32[]{:S(2)}, u32[]{:S(2)}) collective-permute-start(f32[24,3,256]{2,0,1:T(8,128)S(1)} %get-tuple-element.21), channel_id=1, source_target_pairs={{0,4},{4,8},{8,12},{12,16},{16,20},{20,24},{24,28},{28,32},{32,36}... | collective-permute-start | bytes 221192 | tf_op jit(solution)/shard_map/ppermute | solution.py:33
  470.0 7.1 %collective-permute-start.125 = (f32[24,3,256]{2,0,1:T(8,128)S(1)}, f32[24,3,256]{2,0,1:T(8,128)S(1)}, u32[]{:S(2)}, u32[]{:S(2)}) collective-permute-start(f32[24,3,256]{2,0,1:T(8,128)S(1)} %get-tuple-element.22), channel_id=1, source_target_pairs={{4,0},{8,4},{12,8},{16,12},{20,16},{24,20},{28,24},{32,28},{36,32}... | collective-permute-start | bytes 221192 | tf_op jit(solution)/shard_map/ppermute | solution.py:34
  491.8 7.2 %collective-permute-start.128 = (f32[24,3,256]{2,0,1:T(8,128)S(1)}, f32[24,3,256]{2,0,1:T(8,128)S(1)}, u32[]{:S(2)}, u32[]{:S(2)}) collective-permute-start(f32[24,3,256]{2,0,1:T(8,128)S(1)} %get-tuple-element.19), channel_id=1, source_target_pairs={{0,4},{4,8},{8,12},{12,16},{16,20},{20,24},{24,28},{28,32},{32,36}... | collective-permute-start | bytes 221192 | tf_op jit(solution)/shard_map/ppermute | solution.py:33
  491.8 7.1 %collective-permute-start.129 = (f32[24,3,256]{2,0,1:T(8,128)S(1)}, f32[24,3,256]{2,0,1:T(8,128)S(1)}, u32[]{:S(2)}, u32[]{:S(2)}) collective-permute-start(f32[24,3,256]{2,0,1:T(8,128)S(1)} %get-tuple-element.20), channel_id=1, source_target_pairs={{4,0},{8,4},{12,8},{16,12},{20,16},{24,20},{28,24},{32,28},{36,32}... | collective-permute-start | bytes 221192 | tf_op jit(solution)/shard_map/ppermute | solution.py:34
  (87 other events, 417.7 us)
where the time goes:
time: 520 us; the launch traced here: 515 us
  starting transfers between devices  229 us (44%)
  waiting for transfers between devices  164 us (32%)
  matrix products  101 us (19%)
  local copies, waits for them, and re-layouts  11.7 us (2%)
    ppermute x66, starting transfers between devices, padded(): after = lax.ppermute(leading, axis, down)  196 us
    ppermute x66, waiting for transfers between devices, padded(): before = lax.ppermute(last, axis, up)  103 us
    ppermute x66, waiting for transfers between devices, padded(): after = lax.ppermute(leading, axis, down)  61.1 us
    dot_general x60, matrix products, along_last(): return jnp.einsum('uvw,jw->uvj', values, matrix, precision=HIGHEST)  39.6 us
    dot_general x87, matrix products, along_middle(): return jnp.einsum('ij,ujw->uiw', matrix, values, precision=HIGHEST)  35.9 us
    ppermute x66, starting transfers between devices, padded(): before = lax.ppermute(last, axis, up)  33.5 us
    dot_general x60, matrix products, along_first(): jnp.dot(matrix, values.reshape(old_shape[0], old_shape[1] * old_shape[2])...  25.7 us
  transfers between devices with their start and end apart: 132, of which 94 were waited for; matrix products, arithmetic and copies ran while one was open for 10% of the time, Pallas kernels for 0%

commit v1 on v0

v1 whole, which is shorter than its diff:
```python
import functools

import jax
import jax.numpy as jnp
from jax import lax
from jax.experimental import pallas as pl
from jax.experimental.pallas import tpu as pltpu
from jax.sharding import Mesh
from jax.sharding import PartitionSpec as P

F32 = jnp.float32
BF16 = jnp.bfloat16
LANES = 128

MASS = (2416.0, 1191.0, 120.0, 1.0)
STIFF = (80.0, -15.0, -24.0, -1.0)
ALPHA = 0.5 / (120.0 * 5040.0 * 5040.0)
PATCH = ("pz", "core")


def dot(a, b):
    return jnp.dot(a, b, preferred_element_type=F32)


def split(value):
    high = value.astype(BF16)
    return high, (value - high.astype(F32)).astype(BF16)


def dot_split(value, matrix):
    high, low = split(value)
    return dot(high, matrix) + dot(low, matrix)


def banded(rows, columns, size_r, size_c, coeffs, row_step, column_step):
    i = lax.broadcasted_iota(jnp.int32, (rows, columns), 0)
    j = lax.broadcasted_iota(jnp.int32, (rows, columns), 1)
    at = row_step * i + column_step * j
    out = jnp.zeros((rows, columns), F32)
    for key, weight in coeffs.items():
        out = jnp.where(at == key, weight, out)
    return jnp.where((i < size_r) & (j < size_c), out, 0.0).astype(BF16)


def fill_w(w_ref, depth, size):
    mass = {0: 2416.0, 1: 1192.0, -1: 1192.0, 2: 120.0, -2: 120.0, 3: 1.0, -3: 1.0}
    low = {1: -1.0, -1: -1.0}
    stiff = {0: 80.0, 1: -15.0, -1: -15.0, 2: -24.0, -2: -24.0, 3: -1.0, -3: -1.0}
    for block, table in enumerate((mass, mass, stiff, stiff, low)):
        w_ref[block * depth : (block + 1) * depth, :] = banded(
            depth, depth, size, size, table, 1, -1
        )


def restrict_w(rows, columns, size):
    taps = {-2: 0.125, -1: 0.5, 0: 0.75, 1: 0.5, 2: 0.125}
    return banded(rows, columns, size, size // 2, taps, 1, -2)


def prolong_w(rows, columns, size):
    taps = {-2: 0.125, -1: 0.5, 0: 0.75, 1: 0.5, 2: 0.125}
    return banded(rows, columns, size // 2, size, taps, -2, 1)


def stencil(x_ref, l_ref, u0, nu, v0, nv):
    tiles = x_ref.shape[0]
    depth = tiles * LANES

    def weigh(centre, one, two, three, taps):
        return taps[0] * centre + taps[1] * one + taps[2] * two + taps[3] * three

    for tile in range(tiles):
        for column in range(nv // 16):
            row = v0 + 16 * column

            def plane(u):
                x = [x_ref[tile, u, pl.ds(row - 3 + k, 16), :] for k in range(7)]
                one, two, three = x[2] + x[4], x[1] + x[5], x[0] + x[6]
                p = 2416.0 * x[3] + 1191.0 * one + 120.0 * two + three
                q = 80.0 * x[3] - 15.0 * one - 24.0 * two - three
                return p, q

            def emit(at, ps, qs):
                p1, p2, p3 = ps[2] + ps[4], ps[1] + ps[5], ps[0] + ps[6]
                q1, q2, q3 = qs[2] + qs[4], qs[1] + qs[5], qs[0] + qs[6]
                r = 2416.0 * ps[3] + 1191.0 * p1 + 120.0 * p2 + p3
                s = (80.0 * ps[3] - 15.0 * p1 - 24.0 * p2 - p3) + (
                    2416.0 * qs[3] + 1191.0 * q1 + 120.0 * q2 + q3
                )
                for part, value in enumerate(split(s) + split(r)):
                    lane = part * depth + tile * LANES
                    l_ref[at, 16 * column : 16 * column + 16, lane : lane + LANES] = value

            def several(first, count, carry):
                ps, qs = list(carry[:6]), list(carry[6:])
                for k in range(count):
                    p, q = plane(u0 + first + k + 3)
                    emit(first + k, ps + [p], qs + [q])
                    ps, qs = ps[1:] + [p], qs[1:] + [q]
                return tuple(ps + qs)

            start = [plane(u0 - 3 + k) for k in range(6)]
            carry = tuple([p for p, _ in start] + [q for _, q in start])
            groups = nu // 6
            if groups > 1:
                carry = lax.fori_loop(0, groups, lambda g, c: several(6 * g, 6, c), carry)
            elif groups == 1:
                carry = several(0, 6, carry)
            if nu % 6:
                several(6 * groups, nu % 6, carry)


def finish(l_ref, w_ref, nu, nv, use):
    depth = w_ref.shape[1]
    chunk = max(1, min(nu, 384 // nv))

    def some(first, count):
        left = l_ref[pl.ds(first, count), 0:nv, :].reshape(count * nv, 4 * depth)
        use(
            first,
            count,
            dot(left, w_ref[0 : 4 * depth, :])
            + dot(left[:, 0:depth], w_ref[4 * depth : 5 * depth, :]),
        )

    whole = nu // chunk
    if whole > 1:
        lax.fori_loop(0, whole, lambda c, _: some(c * chunk, chunk), None)
    elif whole == 1:
        some(0, chunk)
    if nu % chunk:
        some(whole * chunk, nu % chunk)


def sweep(x_ref, sf_ref, sa, l_ref, w_ref, u0, nu, v0, nv):
    stencil(x_ref, l_ref, u0, nu, v0, nv)

    def use(first, count, product):
        for tile in range(x_ref.shape[0]):
            at = (tile, pl.ds(u0 + first, count), pl.ds(v0, nv), slice(None))
            part = product[:, tile * LANES : (tile + 1) * LANES].reshape(count, nv, LANES)
            weight = sa if isinstance(sa, float) else sa[at]
            x_ref[at] = x_ref[at] + (sf_ref[at] - weight * part)

    finish(l_ref, w_ref, nu, nv, use)


def residual(x_ref, sf_ref, sa, l_ref, w_ref, rw, t_ref, scale, u0, nu, v0, nv, t0):
    stencil(x_ref, l_ref, u0, nu, v0, nv)

    def use(first, count, product):
        parts = []
        for tile in range(x_ref.shape[0]):
            at = (tile, pl.ds(u0 + first, count), pl.ds(v0, nv), slice(None))
            part = product[:, tile * LANES : (tile + 1) * LANES].reshape(count, nv, LANES)
            weight = sa if isinstance(sa, float) else sa[at]
            value = scale * (sf_ref[at] - weight * part)
            parts.append(value.reshape(count * nv, LANES))
        whole = parts[0] if len(parts) == 1 else jnp.concatenate(parts, axis=1)
        narrow = dot_split(whole, rw)
        t_ref[pl.ds(t0 + first, count), 0:nv, :] = narrow.reshape(count, nv, LANES)

    finish(l_ref, w_ref, nu, nv, use)


def narrow_plane(t_ref, tu_ref, j, nv, rows):
    at = [t_ref[2 * j + k, 0:nv, :] for k in range(5)]
    tu_ref[0:nv, :] = 0.125 * (at[0] + at[4]) + 0.5 * (at[1] + at[3]) + 0.75 * at[2]
    at = [tu_ref[pl.ds(k, rows, stride=2), :] for k in range(5)]
    return 0.125 * (at[0] + at[4]) + 0.5 * (at[1] + at[3]) + 0.75 * at[2]


def widen(read, even, tu_ref, z_ref, slot, rows):
    if even:
        plane = 0.125 * (read(-1) + read(1)) + 0.75 * read(0)
    else:
        plane = 0.5 * (read(0) + read(1))
    tu_ref[0 : plane.shape[0], :] = plane
    low, mid, high = (tu_ref[k : k + rows, :] for k in range(3))
    z_ref[slot, pl.ds(0, rows, stride=2), :] = 0.125 * (low + high) + 0.75 * mid
    z_ref[slot, pl.ds(1, rows, stride=2), :] = 0.5 * (mid + high)


def spread_mask(column, rows):
    return jnp.broadcast_to(column, (rows, LANES))


UB0, VB0, V0 = 14, 16, 64


def fill_fine(own, low, high, mask, x_ref, sf_ref, sa_ref):
    parts = ((low, 0, 16), (own, 16, 24), (high, 40, 16))
    for u in range(51):
        for tile in range(2):
            for source, row, rows in parts:
                at = slice(row, row + rows)
                lanes = slice(tile * LANES, (tile + 1) * LANES)
                lane = 2 * u + tile
                active = spread_mask(mask[at, lane : lane + 1], rows)
                if x_ref is not None:
                    x_ref[tile, u, at, :] = active * source[u, :, lanes]
                if 3 <= u < 48:
                    sa_ref[tile, u, at, :] = ALPHA * active
                    sf_ref[tile, u, at, :] = (0.5 * active) * source[51 + u - 3, :, lanes]


def fine_pre(own, low, high, mask, x_out, f1_out, x, sf, sa, l_ref, w_ref, t_ref, tu_ref):
    fill_w(w_ref, 256, 256)
    fill_fine(own, low, high, mask, x, sf, sa)
    sweep(x, sf, sa, l_ref, w_ref, 3, 45, 5, 48)
    sweep(x, sf, sa, l_ref, w_ref, 6, 39, 8, 48)
    sweep(x, sf, sa, l_ref, w_ref, 9, 33, 11, 48)
    for tile in range(2):
        x_out[:, :, tile * LANES : (tile + 1) * LANES] = x[tile, 14:38, 16:40, :]
    rw = restrict_w(256, LANES, 256)
    residual(x, sf, sa, l_ref, w_ref, rw, t_ref, 2.0, 12, 27, 14, 32, 0)
    for j in range(12):
        f1_out[j] = narrow_plane(t_ref, tu_ref, j, 32, 12)


def fine_post(
    own, low, high, mask, x_own, x_low, x_high, e_own, e_low, e_high,
    out, x, sf, sa, l_ref, w_ref, e_ref, tu_ref, z_ref,
):
    fill_w(w_ref, 256, 256)
    fill_fine(own, low, high, mask, None, sf, sa)
    e_ref[:, 0:8, :] = e_low[...]
    e_ref[:, 8:20, :] = e_own[...]
    e_ref[:, 20:28, :] = e_high[...]
    pw = prolong_w(LANES, 256, 256)
    position = lax.axis_index("dir")

    def one(i, even):
        u = 2 * i - 10 + (0 if even else 1)
        coarse = i + 1

        def read(k):
            at = coarse + k
            place = 12 * position + at - 6
            inside = jnp.logical_and(place >= 0, place < 48)
            return jnp.where(inside, e_ref[at, 2:26, :], 0.0)

        widen(read, even, tu_ref, z_ref, 0, 22)
        fine = dot_split(z_ref[0, 0:48, :], pw)
        at = u + UB0
        for tile in range(2):
            lanes = slice(tile * LANES, (tile + 1) * LANES)
            x[tile, at, 6:50, :] = fine[0:44, lanes]

    for i in range(22):
        for even in (True, False):
            u = 2 * i - 10 + (0 if even else 1)
            if -9 <= u <= 32:
                one(i, even)
    for u in range(42):
        for tile in range(2):
            lanes = slice(tile * LANES, (tile + 1) * LANES)
            at = u + 5
            for source, row, rows in ((x_low, 0, 16), (x_own, 16, 24), (x_high, 40, 16)):
                part = slice(row, row + rows)
                active = spread_mask(mask[part, 2 * at + tile : 2 * at + tile + 1], rows)
                x[tile, at, part, :] = active * (x[tile, at, part, :] + source[u, :, lanes])
    sweep(x, sf, sa, l_ref, w_ref, 8, 36, 10, 48)
    sweep(x, sf, sa, l_ref, w_ref, 11, 30, 13, 32)
    sweep(x, sf, sa, l_ref, w_ref, 14, 24, 16, 32)
    for tile in range(2):
        out[:, :, tile * LANES : (tile + 1) * LANES] = x[tile, 14:38, 16:40, :]


def fill_next(own, low, high, mask, x_ref, sf_ref, sa_ref):
    for u in range(36):
        for source, row in ((low, 0), (own, 12), (high, 24)):
            at = slice(row, row + 12)
            active = spread_mask(mask[at, u : u + 1], 12)
            value = (0.25 * active) * source[u]
            sa_ref[0, u, at, :] = ALPHA * active
            sf_ref[0, u, at, :] = value
            if x_ref is not None:
                x_ref[0, u, at, :] = value


def next_pre(own, low, high, mask, x_out, f2_out, x, sf, sa, l_ref, w_ref, t_ref, tu_ref):
    fill_w(w_ref, 128, 128)
    fill_next(own, low, high, mask, x, sf, sa)
    sweep(x, sf, sa, l_ref, w_ref, 4, 27, 4, 32)
    sweep(x, sf, sa, l_ref, w_ref, 7, 21, 7, 32)
    x_out[...] = x[0, 12:24, 12:24, :]
    rw = restrict_w(LANES, LANES, 128)
    residual(x, sf, sa, l_ref, w_ref, rw, t_ref, 4.0, 10, 15, 10, 16, 0)
    for j in range(3):
        even = narrow_plane(t_ref, tu_ref, 2 * j, 16, 6)
        odd = narrow_plane(t_ref, tu_ref, 2 * j + 1, 16, 6)
        f2_out[6 * j : 6 * j + 6, :] = even + pltpu.roll(odd, 64, 1)


def next_post(
    own, low, high, mask, x_own, x_low, x_high, e2,
    out, x, sf, sa, l_ref, w_ref, tu_ref, z_ref,
):
    fill_w(w_ref, 128, 128)
    fill_next(own, low, high, mask, None, sf, sa)
    for u in range(36):
        for source, row in ((x_low, 0), (x_own, 12), (x_high, 24)):
            x[0, u, row : row + 12, :] = source[u]
    pw = prolong_w(LANES, LANES, 128)
    for u in range(-9, 21):
        coarse = u // 2 + 5

        def read(k):
            return e2[coarse + k, 0:24, :]

        widen(read, u % 2 == 0, tu_ref, z_ref, 0, 16)
        first = 0.5 * (tu_ref[0:1, :] + tu_ref[1:2, :])
        fine = dot_split(z_ref[0, 0:32, :], pw)
        ahead = dot_split(jnp.broadcast_to(first, (16, LANES)), pw)
        x[0, u + 12, 4:36, :] = x[0, u + 12, 4:36, :] + fine
        x[0, u + 12, 3:4, :] = x[0, u + 12, 3:4, :] + ahead[0:1]
    for u in range(3, 33):
        for row in range(0, 36, 12):
            at = slice(row, row + 12)
            active = spread_mask(mask[at, u : u + 1], 12)
            x[0, u, at, :] = active * x[0, u, at, :]
    sweep(x, sf, sa, l_ref, w_ref, 6, 24, 6, 32)
    sweep(x, sf, sa, l_ref, w_ref, 9, 18, 9, 32)
    sweep(x, sf, sa, l_ref, w_ref, 12, 12, 12, 16)
    out[...] = x[0, 12:24, 12:24, :]


def coarse(same, other, e_out, x, sf, l_ref, w_ref, t_ref, tu_ref, x3, sf3, w3_ref, z_ref):
    fill_w(w_ref, 128, 64)
    fill_w(w3_ref, 128, 32)
    pair, core = lax.axis_index("pz"), lax.axis_index("core")
    position = lax.axis_index("dir")
    lane = lax.broadcasted_iota(jnp.int32, (6, LANES), 1)
    low_half = lane < 64

    for edge in (0, 1, 2, 27, 28, 29):
        x[0, edge] = jnp.zeros(x.shape[2:], F32)
    for edge in (0, 1, 26, 27, 28):
        t_ref[edge] = jnp.zeros(t_ref.shape[1:], F32)

    def place(source, offset, row):
        index = lax.rem(pair + 16 + offset, 16)
        for d in range(4):
            for k in range(3):
                both = 0.125 * source[index * 4 + d, 6 * k : 6 * k + 6, :]
                for odd in (0, 1):
                    value = pltpu.roll(both, 64, 1) if odd else both
                    value = jnp.where(low_half, value, 0.0)
                    u = 6 * d + 2 * k + odd + 3
                    x[0, u, pl.ds(row, 6), :] = value
                    sf[0, u, pl.ds(row, 6), :] = value

    def even_patch(k, _):
        place(same, k - 5, 12 * k)

    def odd_patch(k, _):
        place(other, k - 5 + core, 12 * k + 6)

    lax.fori_loop(0, 11, even_patch, None)
    lax.fori_loop(0, 10, odd_patch, None)

    sweep(x, sf, ALPHA, l_ref, w_ref, 3, 24, 6, 128)
    sweep(x, sf, ALPHA, l_ref, w_ref, 3, 24, 9, 112)
    rw = restrict_w(LANES, LANES, 64)
    residual(x, sf, ALPHA, l_ref, w_ref, rw, t_ref, 8.0, 3, 24, 12, 112, 2)

    for edge in (0, 1, 2, 15, 16, 17):
        x3[0, edge] = jnp.zeros(x3.shape[2:], F32)

    def narrow(j, _):
        value = 0.0625 * narrow_plane(t_ref, tu_ref, j, 112, 50)
        x3[0, j + 3, 3:53, :] = value
        sf3[0, j + 3, 3:53, :] = value

    lax.fori_loop(0, 12, narrow, None)
    sweep(x3, sf3, ALPHA, l_ref, w3_ref, 3, 12, 6, 48)
    sweep(x3, sf3, ALPHA, l_ref, w3_ref, 3, 12, 9, 48)
    sweep(x3, sf3, ALPHA, l_ref, w3_ref, 3, 12, 12, 32)
    sweep(x3, sf3, ALPHA, l_ref, w3_ref, 3, 12, 15, 32)
    sweep(x3, sf3, ALPHA, l_ref, w3_ref, 3, 12, 18, 32)

    pw = prolong_w(LANES, LANES, 64)

    def wide(j, _):
        def read(k):
            return x3[0, j + 3 + k, 18:42, :]

        for odd in (0, 1):
            widen(read, not odd, tu_ref, z_ref, odd, 22)
            fine = dot_split(z_ref[odd, 0:48, :], pw)
            at = (0, 2 * j + odd + 3, slice(46, 94), slice(None))
            x[at] = x[at] + fine

    lax.fori_loop(0, 12, wide, None)
    sweep(x, sf, ALPHA, l_ref, w_ref, 3, 24, 49, 32)
    sweep(x, sf, ALPHA, l_ref, w_ref, 3, 24, 52, 32)
    sweep(x, sf, ALPHA, l_ref, w_ref, 3, 24, 55, 32)

    def give(k, _):
        u = 6 * position - 5 + k
        inside = jnp.logical_and(u >= 0, u < 24)
        at = jnp.clip(u, 0, 23) + 3
        e_out[k] = jnp.where(inside, x[0, at, 55:79, :], 0.0)

    lax.fori_loop(0, 17, give, None)


def call(body, outs, scratch, operands, flops):
    vmem = pl.BlockSpec(memory_space=pltpu.VMEM)
    size = 0
    for array in list(operands) + list(outs):
        dims = list(array.shape)
        dims[-1] = -(-dims[-1] // 128) * 128
        dims[-2] = -(-dims[-2] // 16) * 16
        count = 1
        for dim in dims:
            count *= dim
        size += 4 * count
    for shape, kind in scratch:
        count = 1
        for dim in shape:
            count *= dim
        size += count * (2 if kind == BF16 else 4)
    return pl.pallas_call(
        body,
        out_shape=list(outs),
        in_specs=[vmem] * len(operands),
        out_specs=[vmem] * len(outs),
        scratch_shapes=[pltpu.VMEM(shape, kind) for shape, kind in scratch],
        compiler_params=pltpu.CompilerParams(vmem_limit_bytes=size + (6 << 20)),
        cost_estimate=pl.CostEstimate(flops=flops, bytes_accessed=size, transcendentals=0),
    )(*operands)


def shape_of(*dims):
    return jax.ShapeDtypeStruct(dims, F32)


def ring(value, axes, step):
    count = 1
    for axis in axes:
        count *= lax.axis_size(axis)
    pairs = [(i, (i + step) % count) for i in range(count)]
    return lax.ppermute(value, axes if len(axes) > 1 else axes[0], pairs)


def along_dir(value, before, after):
    count = value.shape[0]
    low = ring(value[count - before :], ("dir",), 1)
    high = ring(value[:after], ("dir",), -1)
    return low, high


def around_next(value):
    low, high = along_dir(value, 12, 12)
    extended = jnp.concatenate([low, value, high], axis=0)
    return extended, ring(extended, PATCH, 1), ring(extended, PATCH, -1)


def inside_lanes(first, count, per, total):
    plane = first + jnp.arange(count) // per
    return ((plane >= 0) & (plane < total)).astype(F32)


def on_device(right_side, guess, mask_fine, mask_next):
    position = lax.axis_index("dir")
    fine = jnp.transpose(mask_fine, (1, 0, 2)).reshape(24, 48).astype(F32)
    following = mask_next[:, :, 0].T.astype(F32)
    plane = jnp.concatenate(
        [
            jnp.pad(fine, ((0, 0), (0, 80))),
            jnp.pad(following, ((0, 12), (0, 116))),
        ],
        axis=1,
    )[None]
    up = jnp.concatenate([guess[10:], right_side[13:], plane], axis=0)
    down = jnp.concatenate([guess[:13], right_side[:10], plane], axis=0)
    low = ring(up, ("dir",), 1)
    high = ring(down, ("dir",), -1)
    m_low, m_high, m_own = low[25], high[23], plane[0]
    fine = jnp.concatenate([m_low[:, 20:48], m_own[:, :48], m_high[:, :26]], axis=1)
    fine = fine * inside_lanes(24 * position - 14, 102, 2, 96)
    following = jnp.concatenate(
        [m_low[:12, 128:140], m_own[:12, 128:140], m_high[:12, 128:140]], axis=1
    )
    following = following * inside_lanes(12 * position - 12, 36, 1, 48)
    plane = jnp.concatenate(
        [
            jnp.pad(fine, ((0, 0), (0, 26))),
            jnp.pad(following, ((12, 0), (0, 28))) + jnp.zeros((24, 64), F32),
            jnp.pad(following, ((0, 12), (0, 28))) + jnp.zeros((24, 64), F32),
        ],
        axis=1,
    )[None]
    own = jnp.concatenate(
        [low[:14], guess, high[:13], low[14:25], right_side, high[13:23], plane], axis=0
    )
    low = ring(own[:, 8:24], PATCH, 1)
    high = ring(own[:, 0:16], PATCH, -1)
    mask0 = jnp.concatenate([low[96, :, :128], own[96, :, :128], high[96, :, :128]], axis=0)
    mask1 = jnp.concatenate(
        [low[96, 4:16, 128:192], own[96, 12:24, 128:192], high[96, 0:12, 192:256]], axis=0
    )
    mask1 = jnp.pad(mask1, ((0, 4), (0, 64)))

    window = ((2, 52, V0, LANES), F32)
    left0 = ((46, 48, 1024), BF16)
    w0 = ((1280, 256), BF16)
    x0, f1 = call(
        fine_pre,
        [shape_of(24, 24, 256), shape_of(12, 12, 128)],
        [window, window, window, left0, w0, ((28, 32, 128), F32), ((48, 128), F32)],
        (own, low, high, mask0),
        10**10,
    )

    f1_own, f1_low, f1_high = around_next(f1)
    window1 = ((1, 36, 48, LANES), F32)
    left1 = ((28, 32, 512), BF16)
    w1 = ((640, 128), BF16)
    x1, f2 = call(
        next_pre,
        [shape_of(12, 12, 128), shape_of(18, 128)],
        [window1, window1, window1, left1, w1, ((16, 16, 128), F32), ((48, 128), F32)],
        (f1_own, f1_low, f1_high, mask1),
        10**9,
    )

    x0_low, x0_high = along_dir(x0, 9, 9)
    x0_own = jnp.concatenate([x0_low, x0, x0_high], axis=0)
    x0_low = ring(x0_own[:, 8:24], PATCH, 1)
    x0_high = ring(x0_own[:, 0:16], PATCH, -1)
    x1_own, x1_low, x1_high = around_next(x1)

    same = lax.all_to_all(jnp.broadcast_to(f2[None], (64, 18, 128)), ("pz", "dir"), 0, 0)
    other = lax.ppermute(same, "core", [(0, 1), (1, 0)])
    (e2,) = call(
        coarse,
        [shape_of(17, 24, 128)],
        [
            ((1, 30, 144, LANES), F32),
            ((1, 30, 144, LANES), F32),
            ((24, 128, 512), BF16),
            w1,
            ((29, 112, 128), F32),
            ((112, 128), F32),
            ((1, 18, 64, LANES), F32),
            ((1, 18, 64, LANES), F32),
            w1,
            ((2, 48, 128), F32),
        ],
        (same, other),
        4 * 10**9,
    )
    (e1,) = call(
        next_post,
        [shape_of(12, 12, 128)],
        [window1, window1, window1, left1, w1, ((48, 128), F32), ((2, 48, 128), F32)],
        (f1_own, f1_low, f1_high, mask1, x1_own, x1_low, x1_high, e2),
        10**9,
    )
    e1_low, e1_high = along_dir(e1, 6, 6)
    e1_own = jnp.concatenate([e1_low, e1, e1_high], axis=0)
    e1_low = ring(e1_own[:, 4:12], PATCH, 1)
    e1_high = ring(e1_own[:, 0:8], PATCH, -1)
    (out,) = call(
        fine_post,
        [shape_of(24, 24, 256)],
        [
            window,
            window,
            window,
            left0,
            w0,
            ((24, 32, 128), F32),
            ((48, 128), F32),
            ((2, 48, 128), F32),
        ],
        (own, low, high, mask0, x0_own, x0_low, x0_high, e1_own, e1_low, e1_high),
        10**10,
    )
    return out


def solution(mesh):
    pairs = Mesh(mesh.devices.reshape(16, 2, 4), ("pz", "core", "dir"))
    spec = P("dir", PATCH, None)
    return jax.shard_map(
        on_device, mesh=pairs, in_specs=(spec,) * 4, out_specs=spec, check_vma=False
    )
```

time: 520 us -> 203 us (0.39)
  starting transfers between devices: 229 us -> 49.9 us
  waiting for transfers between devices: 164 us -> 61.9 us
  matrix products: 101 us -> 0 us
  Pallas kernels: 0 us -> 71.5 us
    ppermute x132 -> x21, starting transfers between devices: 229 us -> 44.9 us  [the longest x20 40.8 us: ring(): return lax.ppermute(value, axes if len(axes) > 1 else axes[0], pairs)]
    ppermute x132 -> x21, waiting for transfers between devices: 164 us -> 61.9 us  [the longest x20 61.9 us: ring(): return lax.ppermute(value, axes if len(axes) > 1 else axes[0], pairs)]
    dot_general x207 -> x0, matrix products: 101 us -> none  [the longest x60 39.6 us: along_last(): return jnp.einsum('uvw,jw->uvj', values, matrix, precision=HIGHEST)]
    pallas_call x0 -> x5, Pallas kernels: none -> 71.5 us  [call(): pl.pallas_call(body, out_shape=list(outs), in_specs=[vmem] * len(operands...]
    unnamed x37 -> x45, local copies, waits for them, and re-layouts: 3.29 us -> 10.5 us
  transfers between devices with their start and end apart: 132 -> 22, of which waited for: 94 -> 11; matrix products, arithmetic and copies ran while one was open for 10% -> 3% of each run, Pallas kernels for 0% -> 18%
where the time goes in v1:
time: 203 us; the launch traced here: 202 us
  Pallas kernels  71.5 us (35%)
  waiting for transfers between devices  61.9 us (30%)
  starting transfers between devices  49.9 us (25%)
  local copies, waits for them, and re-layouts  16.6 us (8%)
  other arithmetic  2.09 us (1%)
    pallas_call x5, Pallas kernels, call(): pl.pallas_call(body, out_shape=list(outs), in_specs=[vmem] * len(operands...  71.5 us
    ppermute x20, waiting for transfers between devices, ring(): return lax.ppermute(value, axes if len(axes) > 1 else axes[0], pairs)  61.9 us
    ppermute x20, starting transfers between devices, ring(): return lax.ppermute(value, axes if len(axes) > 1 else axes[0], pairs)  40.8 us
    unnamed x45, local copies, waits for them, and re-layouts  10.5 us
    all_to_all x1, starting transfers between devices, on_device(): lax.all_to_all(jnp.broadcast_to(f2[None], (64, 18, 128)), ('pz', 'dir'),...  5.07 us
    ppermute x1, starting transfers between devices, on_device(): other = lax.ppermute(same, 'core', [(0, 1), (1, 0)])  4.08 us
  transfers between devices with their start and end apart: 22, of which 11 were waited for; matrix products, arithmetic and copies ran while one was open for 3% of the time, Pallas kernels for 18%

profile of v1, /device:TPU:6, one launch (start us, length us, event | category | flops | bytes accessed | tf_op | source)
XLA Modules:
  0.0 202.4 jit_solution(8627717731950438046)
XLA Ops:
  0.0 0.8 convert_element_type.44
  0.9 0.8 copy.11
  1.7 1.0 slice.95
  2.7 1.0 slice.96
  3.7 0.9 pad_maximum_fusion.1
  4.5 0.8 collective-permute-start.1
  5.4 2.5 %collective-permute-start = (f32[26,24,256]{2,1,0:T(8,128)S(1)}, f32[26,24,256]{2,1,0:T(8,128)S(1)}, u32[]{:S(2)}, u32[]{:S(2)}) collective-permute-start(f32[26,24,256]{2,1,0:T(8,128)S(1)} %pad_maximum_fusion), channel_id=1, source_target_pairs={{0,1},{1,2},{2,3},{3,0},{4,5},{5,6},{6,7},{7,4},{8,9},{9,10},{10,1... | collective-permute-start | bytes 1916936 | tf_op jit(solution)/shard_map/ppermute | solution.py:445
  7.9 13.1 %collective-permute-done.1 = f32[24,24,256]{2,1,0:T(8,128)S(1)} collective-permute-done((f32[24,24,256]{2,1,0:T(8,128)}, f32[24,24,256]{2,1,0:T(8,128)S(1)}, u32[]{:S(2)}, u32[]{:S(2)}) %collective-permute-start.1) | collective-permute-done | bytes 589856 | tf_op jit(solution)/shard_map/ppermute | solution.py:445
  21.4 0.4 copy-done.15
  22.2 1.0 slice_dynamic-update-slice_fusion
  23.2 1.0 slice_dynamic-update-slice_fusion.1
  24.2 1.0 slice_dynamic-update-slice_fusion.2
  25.2 1.1 constant_dynamic-update-slice_fusion.1
  26.5 1.0 slice_dynamic-update-slice_fusion.3
  27.8 5.0 %collective-permute-start.3 = (f32[97,16,256]{2,1,0:T(8,128)S(1)}, f32[97,16,256]{2,1,0:T(8,128)S(1)}, u32[]{:S(2)}, u32[]{:S(2)}) collective-permute-start(f32[97,16,256]{2,1,0:T(8,128)S(1)} %get-tuple-element.13), channel_id=1, source_target_pairs={{0,124},{4,0},{8,4},{12,8},{16,12},{20,16},{24,20},{28,24},{32,28}... | collective-permute-start | bytes 4767752 | tf_op jit(solution)/shard_map/ppermute | solution.py:445
  32.9 18.0 %collective-permute-done.3.high = f32[97,16,256]{2,1,0:T(8,128)S(1)} collective-permute-done((f32[97,16,256]{2,1,0:T(8,128)S(1)}, f32[97,16,256]{2,1,0:T(8,128)S(1)}, u32[]{:S(2)}, u32[]{:S(2)}) %collective-permute-start.3) | collective-permute-done | bytes 1589280 | tf_op jit(solution)/shard_map/ppermute | solution.py:445
  51.0 5.2 %collective-permute-done.2.low = f32[97,16,256]{2,1,0:T(8,128)S(1)} collective-permute-done((f32[97,16,256]{2,1,0:T(8,128)S(1)}, f32[97,16,256]{2,1,0:T(8,128)S(1)}, u32[]{:S(2)}, u32[]{:S(2)}) %collective-permute-start.2) | collective-permute-done | bytes 1589280 | tf_op jit(solution)/shard_map/ppermute | solution.py:445
  56.2 21.7 %shard_map.46 = (f32[24,24,256]{2,1,0:T(8,128)S(1)}, f32[12,12,128]{2,1,0:T(8,128)S(1)}) custom-call(f32[97,24,256]{2,1,0:T(8,128)S(1)} %constant_dynamic-update-slice_fusion.own, f32[97,16,256]{2,1,0:T(8,128)S(1)} %collective-permute-done.2.low, f32[97,16,256]{2,1,0:T(8,128)S(1)} %collective-permute-done.3.high, f32[56,128]{1,0:T(8,128)S(1)} %pad_maximum_fusion.3.mask), custom_call_target="tpu_custom_call" | custom-call | flops 10000000000 | bytes 23158784 | tf_op jit(solution)/shard_map/pallas_call | solution.py:425
  77.9 3.5 %collective-permute-start.8 = (f32[12,12,128]{2,1,0:T(8,128)S(1)}, f32[12,12,128]{2,1,0:T(8,128)S(1)}, u32[]{:S(2)}, u32[]{:S(2)}) collective-permute-start(f32[12,12,128]{2,1,0:T(8,128)S(1)} %get-tuple-element.10), channel_id=1, source_target_pairs={{0,1},{1,2},{2,3},{3,0},{4,5},{5,6},{6,7},{7,4},{8,9},{9,10},{10,1... | collective-permute-start | bytes 221192 | tf_op jit(solution)/shard_map/ppermute | solution.py:445
  81.4 0.7 fusion.6
  82.1 3.2 %collective-permute-start.4 = (f32[9,24,256]{2,1,0:T(8,128)}, f32[9,24,256]{2,1,0:T(8,128)}, u32[]{:S(2)}, u32[]{:S(2)}) collective-permute-start(f32[9,24,256]{2,1,0:T(8,128)} %get-tuple-element.18), channel_id=1, source_target_pairs={{0,1},{1,2},{2,3},{3,0},{4,5},{5,6},{6,7},{7,4},{8,9},{9,10},{10,1... | collective-permute-start | bytes 663560 | tf_op jit(solution)/shard_map/ppermute | solution.py:445
  85.5 1.8 collective-permute-done.9
  87.3 5.1 %collective-permute-start.11 = (f32[36,12,128]{2,1,0:T(8,128)S(1)}, f32[36,12,128]{2,1,0:T(8,128)S(1)}, u32[]{:S(2)}, u32[]{:S(2)}) collective-permute-start(f32[36,12,128]{2,1,0:T(8,128)S(1)} %constant_dynamic-update-slice_fusion.6.own), channel_id=1, source_target_pairs={{0,124},{4,0},{8,4},{12,8},{16,12},{20,16},{24,20},{28,24},{32,28}... | collective-permute-start | bytes 663560 | tf_op jit(solution)/shard_map/ppermute | solution.py:445
  92.4 4.4 %collective-permute-done.10.low = f32[36,12,128]{2,1,0:T(8,128)S(1)} collective-permute-done((f32[36,12,128]{2,1,0:T(8,128)S(1)}, f32[36,12,128]{2,1,0:T(8,128)S(1)}, u32[]{:S(2)}, u32[]{:S(2)}) %collective-permute-start.10) | collective-permute-done | bytes 221216 | tf_op jit(solution)/shard_map/ppermute | solution.py:445
  96.8 3.7 %shard_map.47 = (f32[12,12,128]{2,1,0:T(8,128)S(1)}, f32[18,128]{1,0:T(8,128)S(1)}) custom-call(f32[36,12,128]{2,1,0:T(8,128)S(1)} %constant_dynamic-update-slice_fusion.6.own, f32[36,12,128]{2,1,0:T(8,128)S(1)} %collective-permute-done.10.low, f32[36,12,128]{2,1,0:T(8,128)S(1)} %collective-permute-done.11.high, f32[40,128]{1,0:T(8,128)S(1)} %select_maximum_fusion.3.mask), custom_call_target="tpu_custom_call" | custom-call | flops 1000000000 | bytes 4915200 | tf_op jit(solution)/shard_map/pallas_call | solution.py:425
  100.5 0.7 copy-done.9
  101.2 1.0 broadcast_in_dim.16
  102.2 5.1 %all-to-all-start = ((f32[64,18,128]{2,1,0:T(8,128)}), f32[64,18,128]{2,1,0:T(8,128)S(1)}, u32[]{:S(2)}, u32[]{:S(2)}) async-start(f32[64,18,128]{2,1,0:T(8,128)} %broadcast_in_dim.16), calls=%async_computation | async-start | bytes 1572864 | tf_op jit(solution)/shard_map/all_to_all | solution.py:536
  107.2 0.9 collective-permute-start.5
  108.2 1.0 constant_dynamic-update-slice_fusion.5
  109.1 1.1 constant_dynamic-update-slice_fusion.4
  110.2 8.5 %collective-permute-done.5 = f32[9,24,256]{2,1,0:T(8,128)S(1)} collective-permute-done((f32[9,24,256]{2,1,0:T(8,128)S(1)}, f32[9,24,256]{2,1,0:T(8,128)S(1)}, u32[]{:S(2)}, u32[]{:S(2)}) %collective-permute-start.5) | collective-permute-done | bytes 221216 | tf_op jit(solution)/shard_map/ppermute | solution.py:445
  118.8 1.0 copy-done
  119.7 1.3 collective-permute-start.12
  121.2 4.1 %collective-permute-start.16 = (f32[64,18,128]{2,0,1:T(8,128)S(1)}, f32[64,18,128]{2,0,1:T(8,128)S(1)}, u32[]{:S(2)}, u32[]{:S(2)}) collective-permute-start(f32[64,18,128]{2,0,1:T(8,128)S(1)} %copy.13), channel_id=1, source_target_pairs={{0,4},{4,0},{1,5},{5,1},{2,6},{6,2},{3,7},{7,3},{8,12},{12,8},{9,1... | collective-permute-start | bytes 1769480 | tf_op jit(solution)/shard_map/ppermute | solution.py:537
  125.3 1.4 fusion.5
  126.8 5.0 %collective-permute-start.7 = (f32[42,16,256]{2,1,0:T(8,128)S(1)}, f32[42,16,256]{2,1,0:T(8,128)S(1)}, u32[]{:S(2)}, u32[]{:S(2)}) collective-permute-start(f32[42,16,256]{2,1,0:T(8,128)S(1)} %get-tuple-element.15), channel_id=1, source_target_pairs={{0,124},{4,0},{8,4},{12,8},{16,12},{20,16},{24,20},{28,24},{32,28}... | collective-permute-start | bytes 2064392 | tf_op jit(solution)/shard_map/ppermute | solution.py:445
  131.8 0.9 collective-permute-start.13
  132.8 4.9 %collective-permute-done.13 = f32[12,12,128]{2,1,0:T(8,128)S(1)} collective-permute-done((f32[12,12,128]{2,1,0:T(8,128)S(1)}, f32[12,12,128]{2,1,0:T(8,128)S(1)}, u32[]{:S(2)}, u32[]{:S(2)}) %collective-permute-start.13) | collective-permute-done | bytes 73760 | tf_op jit(solution)/shard_map/ppermute | solution.py:445
  137.8 5.1 %collective-permute-start.15 = (f32[36,12,128]{2,1,0:T(8,128)S(1)}, f32[36,12,128]{2,1,0:T(8,128)S(1)}, u32[]{:S(2)}, u32[]{:S(2)}) collective-permute-start(f32[36,12,128]{2,1,0:T(8,128)S(1)} %constant_dynamic-update-slice_fusion.9.x_own), channel_id=1, source_target_pairs={{0,124},{4,0},{8,4},{12,8},{16,12},{20,16},{24,20},{28,24},{32,28}... | collective-permute-start | bytes 663560 | tf_op jit(solution)/shard_map/ppermute | solution.py:445
  143.2 29.3 %shard_map.48.e2 = f32[17,24,128]{2,1,0:T(8,128)S(1)} custom-call(f32[64,18,128]{2,1,0:T(8,128)S(1)} %all-to-all-done.same, f32[64,18,128]{2,1,0:T(8,128)S(1)} %copy.14.other), custom_call_target="tpu_custom_call" | custom-call | flops 4000000000 | bytes 13221888 | tf_op jit(solution)/shard_map/pallas_call | solution.py:425
  172.6 3.4 %shard_map.49 = f32[12,12,128]{2,1,0:T(8,128)S(1)} custom-call(f32[36,12,128]{2,1,0:T(8,128)S(1)} %copy-done.4, f32[36,12,128]{2,1,0:T(8,128)S(1)} %copy-done.10, f32[36,12,128]{2,1,0:T(8,128)S(1)} %copy-done.12, f32[40,128]{1,0:T(8,128)S(1)} %select_maximum_fusion.3.mask, f32[36,12,128]{2,1,0:T(8,128)S(1)} %constant_dynamic-update-slice_fusion.9.x_own, ...), custom_call_target="tpu_custom_call" | custom-call | flops 1000000000 | bytes 5980160 | tf_op jit(solution)/shard_map/pallas_call | solution.py:425
  176.1 2.0 collective-permute-start.18
  178.1 2.1 %collective-permute-done.17 = f32[6,12,128]{2,1,0:T(8,128)S(1)} collective-permute-done((f32[6,12,128]{2,1,0:T(8,128)S(1)}, f32[6,12,128]{2,1,0:T(8,128)S(1)}, u32[]{:S(2)}, u32[]{:S(2)}) %collective-permute-start.17) | collective-permute-done | bytes 36896 | tf_op jit(solution)/shard_map/ppermute | solution.py:445
  180.2 1.3 collective-permute-done.18
  181.6 5.1 %collective-permute-start.20 = (f32[24,8,128]{2,1,0:T(8,128)S(1)}, f32[24,8,128]{2,1,0:T(8,128)S(1)}, u32[]{:S(2)}, u32[]{:S(2)}) collective-permute-start(f32[24,8,128]{2,1,0:T(8,128)S(1)} %get-tuple-element.19), channel_id=1, source_target_pairs={{0,124},{4,0},{8,4},{12,8},{16,12},{20,16},{24,20},{28,24},{32,28}... | collective-permute-start | bytes 294920 | tf_op jit(solution)/shard_map/ppermute | solution.py:445
  186.7 2.3 %collective-permute-done.19.e_low = f32[24,8,128]{2,1,0:T(8,128)S(1)} collective-permute-done((f32[24,8,128]{2,1,0:T(8,128)S(1)}, f32[24,8,128]{2,1,0:T(8,128)S(1)}, u32[]{:S(2)}, u32[]{:S(2)}) %collective-permute-start.19) | collective-permute-done | bytes 98336 | tf_op jit(solution)/shard_map/ppermute | solution.py:445
  189.0 13.5 %shard_map.50 = f32[24,24,256]{2,1,0:T(8,128)} custom-call(f32[97,24,256]{2,1,0:T(8,128)S(1)} %constant_dynamic-update-slice_fusion.own, f32[97,16,256]{2,1,0:T(8,128)S(1)} %copy-done.8, f32[97,16,256]{2,1,0:T(8,128)S(1)} %copy-done.6, f32[56,128]{1,0:T(8,128)S(1)} %pad_maximum_fusion.3.mask, f32[42,24,256]{2,1,0:T(8,128)S(1)} %copy-done.1, ...), custom_call_target="tpu_custom_call" | custom-call | flops 10000000000 | bytes 26386432 | tf_op jit(solution)/shard_map/pallas_call | solution.py:425
  (90 shorter events, 2.7 us)
Async XLA Ops:
  0.0 5.4 %slice-start = ((f32[24,24,256]{2,1,0:T(8,128)}), f32[14,24,256]{2,1,0:T(8,128)S(1)}, s32[]{:S(2)}) async-start(f32[24,24,256]{2,1,0:T(8,128)} %param.5), calls=%async_computation.1 | async-start | bytes 688128 | tf_op jit(solution)/shard_map/slice | solution.py:477
  0.0 5.4 %slice-start.1 = ((f32[24,24,256]{2,1,0:T(8,128)}), f32[11,24,256]{2,1,0:T(8,128)S(1)}, s32[]{:S(2)}) async-start(f32[24,24,256]{2,1,0:T(8,128)} %param.4), calls=%async_computation.2 | async-start | bytes 540672 | tf_op jit(solution)/shard_map/slice | solution.py:477
  3.6 19.5 %copy-start.13 = (f32[24,24,256]{2,1,0:T(8,128)S(1)}, f32[24,24,256]{2,1,0:T(8,128)}, u32[]{:S(2)}) copy-start(f32[24,24,256]{2,1,0:T(8,128)} %param.5) | copy-start | bytes 1769476
  4.5 16.5 %collective-permute-start.1 = (f32[24,24,256]{2,1,0:T(8,128)}, f32[24,24,256]{2,1,0:T(8,128)S(1)}, u32[]{:S(2)}, u32[]{:S(2)}) collective-permute-start(f32[24,24,256]{2,1,0:T(8,128)} %pad_maximum_fusion.1), channel_id=1, source_target_pairs={{0,3},{1,0},{2,1},{3,2},{4,7},{5,4},{6,5},{7,6},{8,11},{9,8},{10,9... | collective-permute-start | bytes 1769480 | tf_op jit(solution)/shard_map/ppermute | solution.py:445
  5.4 15.9 %collective-permute-start = (f32[26,24,256]{2,1,0:T(8,128)S(1)}, f32[26,24,256]{2,1,0:T(8,128)S(1)}, u32[]{:S(2)}, u32[]{:S(2)}) collective-permute-start(f32[26,24,256]{2,1,0:T(8,128)S(1)} %pad_maximum_fusion), channel_id=1, source_target_pairs={{0,1},{1,2},{2,3},{3,0},{4,5},{5,6},{6,7},{7,4},{8,9},{9,10},{10,1... | collective-permute-start | bytes 1916936 | tf_op jit(solution)/shard_map/ppermute | solution.py:445
  21.0 0.8 copy-start.15
  21.3 0.8 copy-start.14
  27.8 23.1 %collective-permute-start.3 = (f32[97,16,256]{2,1,0:T(8,128)S(1)}, f32[97,16,256]{2,1,0:T(8,128)S(1)}, u32[]{:S(2)}, u32[]{:S(2)}) collective-permute-start(f32[97,16,256]{2,1,0:T(8,128)S(1)} %get-tuple-element.13), channel_id=1, source_target_pairs={{0,124},{4,0},{8,4},{12,8},{16,12},{20,16},{24,20},{28,24},{32,28}... | collective-permute-start | bytes 4767752 | tf_op jit(solution)/shard_map/ppermute | solution.py:445
  32.9 23.3 %collective-permute-start.2 = (f32[97,16,256]{2,1,0:T(8,128)S(1)}, f32[97,16,256]{2,1,0:T(8,128)S(1)}, u32[]{:S(2)}, u32[]{:S(2)}) collective-permute-start(f32[97,16,256]{2,1,0:T(8,128)S(1)} %get-tuple-element.14), channel_id=1, source_target_pairs={{0,4},{4,8},{8,12},{12,16},{16,20},{20,24},{24,28},{28,32},{32,36}... | collective-permute-start | bytes 4767752 | tf_op jit(solution)/shard_map/ppermute | solution.py:445
  51.0 34.4 %copy-start.5 = (f32[97,16,256]{2,1,0:T(8,128)}, f32[97,16,256]{2,1,0:T(8,128)S(1)}, u32[]{:S(2)}) copy-start(f32[97,16,256]{2,1,0:T(8,128)S(1)} %collective-permute-done.3.high) | copy-start | bytes 4767748
  56.2 36.2 %copy-start.7 = (f32[97,16,256]{2,1,0:T(8,128)}, f32[97,16,256]{2,1,0:T(8,128)S(1)}, u32[]{:S(2)}) copy-start(f32[97,16,256]{2,1,0:T(8,128)S(1)} %collective-permute-done.2.low) | copy-start | bytes 4767748
  77.9 22.5 %copy-start.2 = (f32[24,24,256]{2,1,0:T(8,128)}, f32[24,24,256]{2,1,0:T(8,128)S(1)}, u32[]{:S(2)}) copy-start(f32[24,24,256]{2,1,0:T(8,128)S(1)} %get-tuple-element.9) | copy-start | bytes 1769476
  77.9 7.5 %collective-permute-start.8 = (f32[12,12,128]{2,1,0:T(8,128)S(1)}, f32[12,12,128]{2,1,0:T(8,128)S(1)}, u32[]{:S(2)}, u32[]{:S(2)}) collective-permute-start(f32[12,12,128]{2,1,0:T(8,128)S(1)} %get-tuple-element.10), channel_id=1, source_target_pairs={{0,1},{1,2},{2,3},{3,0},{4,5},{5,6},{6,7},{7,4},{8,9},{9,10},{10,1... | collective-permute-start | bytes 221192 | tf_op jit(solution)/shard_map/ppermute | solution.py:445
  81.4 5.8 %collective-permute-start.9 = (f32[12,12,128]{2,1,0:T(8,128)S(1)}, f32[12,12,128]{2,1,0:T(8,128)S(1)}, u32[]{:S(2)}, u32[]{:S(2)}) collective-permute-start(f32[12,12,128]{2,1,0:T(8,128)S(1)} %get-tuple-element.10), channel_id=1, source_target_pairs={{0,3},{1,0},{2,1},{3,2},{4,7},{5,4},{6,5},{7,6},{8,11},{9,8},{10,9... | collective-permute-start | bytes 221192 | tf_op jit(solution)/shard_map/ppermute | solution.py:445
  82.1 26.0 %collective-permute-start.4 = (f32[9,24,256]{2,1,0:T(8,128)}, f32[9,24,256]{2,1,0:T(8,128)}, u32[]{:S(2)}, u32[]{:S(2)}) collective-permute-start(f32[9,24,256]{2,1,0:T(8,128)} %get-tuple-element.18), channel_id=1, source_target_pairs={{0,1},{1,2},{2,3},{3,0},{4,5},{5,6},{6,7},{7,4},{8,9},{9,10},{10,1... | collective-permute-start | bytes 663560 | tf_op jit(solution)/shard_map/ppermute | solution.py:445
  87.2 14.9 %copy-start.3 = (f32[36,12,128]{2,1,0:T(8,128)}, f32[36,12,128]{2,1,0:T(8,128)S(1)}, u32[]{:S(2)}) copy-start(f32[36,12,128]{2,1,0:T(8,128)S(1)} %constant_dynamic-update-slice_fusion.6.own) | copy-start | bytes 663556
  87.3 9.5 %collective-permute-start.10 = (f32[36,12,128]{2,1,0:T(8,128)S(1)}, f32[36,12,128]{2,1,0:T(8,128)S(1)}, u32[]{:S(2)}, u32[]{:S(2)}) collective-permute-start(f32[36,12,128]{2,1,0:T(8,128)S(1)} %constant_dynamic-update-slice_fusion.6.own), channel_id=1, source_target_pairs={{0,4},{4,8},{8,12},{12,16},{16,20},{20,24},{24,28},{28,32},{32,36}... | collective-permute-start | bytes 663560 | tf_op jit(solution)/shard_map/ppermute | solution.py:445
  87.3 9.5 %collective-permute-start.11 = (f32[36,12,128]{2,1,0:T(8,128)S(1)}, f32[36,12,128]{2,1,0:T(8,128)S(1)}, u32[]{:S(2)}, u32[]{:S(2)}) collective-permute-start(f32[36,12,128]{2,1,0:T(8,128)S(1)} %constant_dynamic-update-slice_fusion.6.own), channel_id=1, source_target_pairs={{0,124},{4,0},{8,4},{12,8},{16,12},{20,16},{24,20},{28,24},{32,28}... | collective-permute-start | bytes 663560 | tf_op jit(solution)/shard_map/ppermute | solution.py:445
  96.8 3.7 %copy-start.11 = (f32[36,12,128]{2,1,0:T(8,128)}, f32[36,12,128]{2,1,0:T(8,128)S(1)}, u32[]{:S(2)}) copy-start(f32[36,12,128]{2,1,0:T(8,128)S(1)} %collective-permute-done.11.high) | copy-start | bytes 663556
  100.5 0.7 copy-start.9
  102.2 18.9 %all-to-all-start = ((f32[64,18,128]{2,1,0:T(8,128)}), f32[64,18,128]{2,1,0:T(8,128)S(1)}, u32[]{:S(2)}, u32[]{:S(2)}) async-start(f32[64,18,128]{2,1,0:T(8,128)} %broadcast_in_dim.16), calls=%async_computation | async-start | bytes 1572864 | tf_op jit(solution)/shard_map/all_to_all | solution.py:536
  107.2 11.5 %collective-permute-start.5 = (f32[9,24,256]{2,1,0:T(8,128)S(1)}, f32[9,24,256]{2,1,0:T(8,128)S(1)}, u32[]{:S(2)}, u32[]{:S(2)}) collective-permute-start(f32[9,24,256]{2,1,0:T(8,128)S(1)} %get-tuple-element.17), channel_id=1, source_target_pairs={{0,3},{1,0},{2,1},{3,2},{4,7},{5,4},{6,5},{7,6},{8,11},{9,8},{10,9... | collective-permute-start | bytes 663560 | tf_op jit(solution)/shard_map/ppermute | solution.py:445
  118.8 1.0 copy-start
  119.7 13.0 %collective-permute-start.12 = (f32[12,12,128]{2,1,0:T(8,128)S(1)}, f32[12,12,128]{2,1,0:T(8,128)S(1)}, u32[]{:S(2)}, u32[]{:S(2)}) collective-permute-start(f32[12,12,128]{2,1,0:T(8,128)S(1)} %get-tuple-element.11), channel_id=1, source_target_pairs={{0,1},{1,2},{2,3},{3,0},{4,5},{5,6},{6,7},{7,4},{8,9},{9,10},{10,1... | collective-permute-start | bytes 221192 | tf_op jit(solution)/shard_map/ppermute | solution.py:445
  121.2 21.6 %collective-permute-start.16 = (f32[64,18,128]{2,0,1:T(8,128)S(1)}, f32[64,18,128]{2,0,1:T(8,128)S(1)}, u32[]{:S(2)}, u32[]{:S(2)}) collective-permute-start(f32[64,18,128]{2,0,1:T(8,128)S(1)} %copy.13), channel_id=1, source_target_pairs={{0,4},{4,0},{1,5},{5,1},{2,6},{6,2},{3,7},{7,3},{8,12},{12,8},{9,1... | collective-permute-start | bytes 1769480 | tf_op jit(solution)/shard_map/ppermute | solution.py:537
  126.7 59.9 %collective-permute-start.6 = (f32[42,16,256]{2,1,0:T(8,128)S(1)}, f32[42,16,256]{2,1,0:T(8,128)S(1)}, u32[]{:S(2)}, u32[]{:S(2)}) collective-permute-start(f32[42,16,256]{2,1,0:T(8,128)S(1)} %get-tuple-element.16), channel_id=1, source_target_pairs={{0,4},{4,8},{8,12},{12,16},{16,20},{20,24},{24,28},{28,32},{32,36}... | collective-permute-start | bytes 2064392 | tf_op jit(solution)/shard_map/ppermute | solution.py:445
  126.8 59.9 %collective-permute-start.7 = (f32[42,16,256]{2,1,0:T(8,128)S(1)}, f32[42,16,256]{2,1,0:T(8,128)S(1)}, u32[]{:S(2)}, u32[]{:S(2)}) collective-permute-start(f32[42,16,256]{2,1,0:T(8,128)S(1)} %get-tuple-element.15), channel_id=1, source_target_pairs={{0,124},{4,0},{8,4},{12,8},{16,12},{20,16},{24,20},{28,24},{32,28}... | collective-permute-start | bytes 2064392 | tf_op jit(solution)/shard_map/ppermute | solution.py:445
  131.8 5.8 %collective-permute-start.13 = (f32[12,12,128]{2,1,0:T(8,128)S(1)}, f32[12,12,128]{2,1,0:T(8,128)S(1)}, u32[]{:S(2)}, u32[]{:S(2)}) collective-permute-start(f32[12,12,128]{2,1,0:T(8,128)S(1)} %get-tuple-element.11), channel_id=1, source_target_pairs={{0,3},{1,0},{2,1},{3,2},{4,7},{5,4},{6,5},{7,6},{8,11},{9,8},{10,9... | collective-permute-start | bytes 221192 | tf_op jit(solution)/shard_map/ppermute | solution.py:445
  137.7 34.9 %collective-permute-start.14 = (f32[36,12,128]{2,1,0:T(8,128)S(1)}, f32[36,12,128]{2,1,0:T(8,128)S(1)}, u32[]{:S(2)}, u32[]{:S(2)}) collective-permute-start(f32[36,12,128]{2,1,0:T(8,128)S(1)} %constant_dynamic-update-slice_fusion.9.x_own), channel_id=1, source_target_pairs={{0,4},{4,8},{8,12},{12,16},{16,20},{20,24},{24,28},{28,32},{32,36}... | collective-permute-start | bytes 663560 | tf_op jit(solution)/shard_map/ppermute | solution.py:445
  137.8 34.8 %collective-permute-start.15 = (f32[36,12,128]{2,1,0:T(8,128)S(1)}, f32[36,12,128]{2,1,0:T(8,128)S(1)}, u32[]{:S(2)}, u32[]{:S(2)}) collective-permute-start(f32[36,12,128]{2,1,0:T(8,128)S(1)} %constant_dynamic-update-slice_fusion.9.x_own), channel_id=1, source_target_pairs={{0,124},{4,0},{8,4},{12,8},{16,12},{20,16},{24,20},{28,24},{32,28}... | collective-permute-start | bytes 663560 | tf_op jit(solution)/shard_map/ppermute | solution.py:445
  143.2 29.4 %copy-start.4 = (f32[36,12,128]{2,1,0:T(8,128)S(1)}, f32[36,12,128]{2,1,0:T(8,128)}, u32[]{:S(2)}) copy-start(f32[36,12,128]{2,1,0:T(8,128)} %copy-done.3) | copy-start | bytes 663556
  143.2 29.4 %copy-start.10 = (f32[36,12,128]{2,1,0:T(8,128)S(1)}, f32[36,12,128]{2,1,0:T(8,128)}, u32[]{:S(2)}) copy-start(f32[36,12,128]{2,1,0:T(8,128)} %copy-done.9) | copy-start | bytes 663556
  143.2 29.4 %copy-start.12 = (f32[36,12,128]{2,1,0:T(8,128)S(1)}, f32[36,12,128]{2,1,0:T(8,128)}, u32[]{:S(2)}) copy-start(f32[36,12,128]{2,1,0:T(8,128)} %copy-done.11) | copy-start | bytes 663556
  172.5 16.4 %copy-start.1 = (f32[42,24,256]{2,1,0:T(8,128)S(1)}, f32[42,24,256]{2,1,0:T(8,128)}, u32[]{:S(2)}) copy-start(f32[42,24,256]{2,1,0:T(8,128)} %copy-done) | copy-start | bytes 3096580
  172.5 16.4 %copy-start.6 = (f32[97,16,256]{2,1,0:T(8,128)S(1)}, f32[97,16,256]{2,1,0:T(8,128)}, u32[]{:S(2)}) copy-start(f32[97,16,256]{2,1,0:T(8,128)} %copy-done.5) | copy-start | bytes 4767748
  172.5 16.4 %copy-start.8 = (f32[97,16,256]{2,1,0:T(8,128)S(1)}, f32[97,16,256]{2,1,0:T(8,128)}, u32[]{:S(2)}) copy-start(f32[97,16,256]{2,1,0:T(8,128)} %copy-done.7) | copy-start | bytes 4767748
  176.0 4.2 %collective-permute-start.17 = (f32[6,12,128]{2,1,0:T(8,128)S(1)}, f32[6,12,128]{2,1,0:T(8,128)S(1)}, u32[]{:S(2)}, u32[]{:S(2)}) collective-permute-start(f32[6,12,128]{2,1,0:T(8,128)S(1)} %get-tuple-element.21), channel_id=1, source_target_pairs={{0,1},{1,2},{2,3},{3,0},{4,5},{5,6},{6,7},{7,4},{8,9},{9,10},{10,1... | collective-permute-start | bytes 110600 | tf_op jit(solution)/shard_map/ppermute | solution.py:445
  176.1 5.4 %collective-permute-start.18 = (f32[6,12,128]{2,1,0:T(8,128)S(1)}, f32[6,12,128]{2,1,0:T(8,128)S(1)}, u32[]{:S(2)}, u32[]{:S(2)}) collective-permute-start(f32[6,12,128]{2,1,0:T(8,128)S(1)} %get-tuple-element.22), channel_id=1, source_target_pairs={{0,3},{1,0},{2,1},{3,2},{4,7},{5,4},{6,5},{7,6},{8,11},{9,8},{10,9... | collective-permute-start | bytes 110600 | tf_op jit(solution)/shard_map/ppermute | solution.py:445
  181.5 7.4 %collective-permute-start.19 = (f32[24,8,128]{2,1,0:T(8,128)S(1)}, f32[24,8,128]{2,1,0:T(8,128)S(1)}, u32[]{:S(2)}, u32[]{:S(2)}) collective-permute-start(f32[24,8,128]{2,1,0:T(8,128)S(1)} %get-tuple-element.20), channel_id=1, source_target_pairs={{0,4},{4,8},{8,12},{12,16},{16,20},{20,24},{24,28},{28,32},{32,36}... | collective-permute-start | bytes 294920 | tf_op jit(solution)/shard_map/ppermute | solution.py:445
  181.6 7.4 %collective-permute-start.20 = (f32[24,8,128]{2,1,0:T(8,128)S(1)}, f32[24,8,128]{2,1,0:T(8,128)S(1)}, u32[]{:S(2)}, u32[]{:S(2)}) collective-permute-start(f32[24,8,128]{2,1,0:T(8,128)S(1)} %get-tuple-element.19), channel_id=1, source_target_pairs={{0,124},{4,0},{8,4},{12,8},{16,12},{20,16},{24,20},{28,24},{32,28}... | collective-permute-start | bytes 294920 | tf_op jit(solution)/shard_map/ppermute | solution.py:445

commit v2 on v1

--- a/solution.py
+++ b/solution.py
@@ -32,34 +32,38 @@
     return dot(high, matrix) + dot(low, matrix)
 
 
-def banded(rows, columns, size_r, size_c, coeffs, row_step, column_step):
+def banded(rows, columns, size_r, size_c, coeffs, row_step, column_step, pairs=False):
     i = lax.broadcasted_iota(jnp.int32, (rows, columns), 0)
     j = lax.broadcasted_iota(jnp.int32, (rows, columns), 1)
+    same = i >= 0
+    if pairs:
+        same = (i < 64) == (j < 64)
+        i, j = jnp.where(i < 64, i, i - 64), jnp.where(j < 64, j, j - 64)
     at = row_step * i + column_step * j
     out = jnp.zeros((rows, columns), F32)
     for key, weight in coeffs.items():
         out = jnp.where(at == key, weight, out)
-    return jnp.where((i < size_r) & (j < size_c), out, 0.0).astype(BF16)
-
-
-def fill_w(w_ref, depth, size):
+    return jnp.where((i < size_r) & (j < size_c) & same, out, 0.0).astype(BF16)
+
+
+def fill_w(w_ref, depth, size, pairs=False):
     mass = {0: 2416.0, 1: 1192.0, -1: 1192.0, 2: 120.0, -2: 120.0, 3: 1.0, -3: 1.0}
     low = {1: -1.0, -1: -1.0}
     stiff = {0: 80.0, 1: -15.0, -1: -15.0, 2: -24.0, -2: -24.0, 3: -1.0, -3: -1.0}
     for block, table in enumerate((mass, mass, stiff, stiff, low)):
         w_ref[block * depth : (block + 1) * depth, :] = banded(
-            depth, depth, size, size, table, 1, -1
+            depth, depth, size, size, table, 1, -1, pairs
         )
 
 
-def restrict_w(rows, columns, size):
+def restrict_w(rows, columns, size, pairs=False):
     taps = {-2: 0.125, -1: 0.5, 0: 0.75, 1: 0.5, 2: 0.125}
-    return banded(rows, columns, size, size // 2, taps, 1, -2)
-
-
-def prolong_w(rows, columns, size):
+    return banded(rows, columns, size, size // 2, taps, 1, -2, pairs)
+
+
+def prolong_w(rows, columns, size, pairs=False):
     taps = {-2: 0.125, -1: 0.5, 0: 0.75, 1: 0.5, 2: 0.125}
-    return banded(rows, columns, size // 2, size, taps, -2, 1)
+    return banded(rows, columns, size // 2, size, taps, -2, 1, pairs)
 
 
 def stencil(x_ref, l_ref, u0, nu, v0, nv):
@@ -110,6 +114,49 @@
                 several(6 * groups, nu % 6, carry)
 
 
+def stencil_pairs(x_ref, l_ref, k0, nk, v0, nv):
+    low = lax.broadcasted_iota(jnp.int32, (16, LANES), 1) < 64
+
+    for column in range(nv // 16):
+        row = v0 + 16 * column
+
+        def plane(k):
+            x = [x_ref[0, k, pl.ds(row - 3 + i, 16), :] for i in range(7)]
+            one, two, three = x[2] + x[4], x[1] + x[5], x[0] + x[6]
+            p = 2416.0 * x[3] + 1191.0 * one + 120.0 * two + three
+            q = 80.0 * x[3] - 15.0 * one - 24.0 * two - three
+            return p, pltpu.roll(p, 64, 1), q, pltpu.roll(q, 64, 1)
+
+        def sums(own, other):
+            one = other[2] + jnp.where(low, other[1], other[3])
+            three = jnp.where(low, other[0], other[4]) + jnp.where(low, other[3], other[1])
+            return own[2], one, own[1] + own[3], three
+
+        def emit(at, planes):
+            p, p1, p2, p3 = sums([t[0] for t in planes], [t[1] for t in planes])
+            q, q1, q2, q3 = sums([t[2] for t in planes], [t[3] for t in planes])
+            r = 2416.0 * p + 1191.0 * p1 + 120.0 * p2 + p3
+            s = (80.0 * p - 15.0 * p1 - 24.0 * p2 - p3) + (
+                2416.0 * q + 1191.0 * q1 + 120.0 * q2 + q3
+            )
+            for part, value in enumerate(split(s) + split(r)):
+                l_ref[at, 16 * column : 16 * column + 16, part * LANES : (part + 1) * LANES] = value
+
+        def several(first, count, carry):
+            planes = [carry[4 * i : 4 * i + 4] for i in range(4)]
+            for i in range(count):
+                planes = planes + [plane(k0 + first + i + 2)]
+                emit(first + i, planes)
+                planes = planes[1:]
+            return tuple(value for t in planes for value in t)
+
+        carry = tuple(value for i in range(4) for value in plane(k0 - 2 + i))
+        if nk > 6:
+            lax.fori_loop(0, nk // 4, lambda g, c: several(4 * g, 4, c), carry)
+        else:
+            several(0, nk, carry)
+
+
 def finish(l_ref, w_ref, nu, nv, use):
     depth = w_ref.shape[1]
     chunk = max(1, min(nu, 384 // nv))
@@ -132,8 +179,8 @@
         some(whole * chunk, nu % chunk)
 
 
-def sweep(x_ref, sf_ref, sa, l_ref, w_ref, u0, nu, v0, nv):
-    stencil(x_ref, l_ref, u0, nu, v0, nv)
+def sweep(x_ref, sf_ref, sa, l_ref, w_ref, u0, nu, v0, nv, apply=stencil):
+    apply(x_ref, l_ref, u0, nu, v0, nv)
 
     def use(first, count, product):
         for tile in range(x_ref.shape[0]):
@@ -145,8 +192,8 @@
     finish(l_ref, w_ref, nu, nv, use)
 
 
-def residual(x_ref, sf_ref, sa, l_ref, w_ref, rw, t_ref, scale, u0, nu, v0, nv, t0):
-    stencil(x_ref, l_ref, u0, nu, v0, nv)
+def residual(x_ref, sf_ref, sa, l_ref, w_ref, rw, t_ref, scale, u0, nu, v0, nv, t0, apply=stencil):
+    apply(x_ref, l_ref, u0, nu, v0, nv)
 
     def use(first, count, product):
         parts = []
@@ -326,30 +373,24 @@
     out[...] = x[0, 12:24, 12:24, :]
 
 
-def coarse(same, other, e_out, x, sf, l_ref, w_ref, t_ref, tu_ref, x3, sf3, w3_ref, z_ref):
-    fill_w(w_ref, 128, 64)
-    fill_w(w3_ref, 128, 32)
+def coarse(same, other, e_out, x, sf, l_ref, w_ref, t_ref, tu_ref, x3, sf3, w3_ref, b_ref, z_ref):
+    fill_w(w_ref, 128, 64, True)
+    fill_w(w3_ref, 128, 32, True)
     pair, core = lax.axis_index("pz"), lax.axis_index("core")
     position = lax.axis_index("dir")
-    lane = lax.broadcasted_iota(jnp.int32, (6, LANES), 1)
-    low_half = lane < 64
-
-    for edge in (0, 1, 2, 27, 28, 29):
+
+    for edge in (0, 1, 14, 15):
         x[0, edge] = jnp.zeros(x.shape[2:], F32)
-    for edge in (0, 1, 26, 27, 28):
+    for edge in (0, 13):
         t_ref[edge] = jnp.zeros(t_ref.shape[1:], F32)
 
     def place(source, offset, row):
         index = lax.rem(pair + 16 + offset, 16)
         for d in range(4):
             for k in range(3):
-                both = 0.125 * source[index * 4 + d, 6 * k : 6 * k + 6, :]
-                for odd in (0, 1):
-                    value = pltpu.roll(both, 64, 1) if odd else both
-                    value = jnp.where(low_half, value, 0.0)
-                    u = 6 * d + 2 * k + odd + 3
-                    x[0, u, pl.ds(row, 6), :] = value
-                    sf[0, u, pl.ds(row, 6), :] = value
+                value = 0.125 * source[index * 4 + d, 6 * k : 6 * k + 6, :]
+                x[0, 3 * d + k + 2, pl.ds(row, 6), :] = value
+                sf[0, 3 * d + k + 2, pl.ds(row, 6), :] = value
 
     def even_patch(k, _):
         place(same, k - 5, 12 * k)
@@ -360,50 +401,77 @@
     lax.fori_loop(0, 11, even_patch, None)
     lax.fori_loop(0, 10, odd_patch, None)
 
-    sweep(x, sf, ALPHA, l_ref, w_ref, 3, 24, 6, 128)
-    sweep(x, sf, ALPHA, l_ref, w_ref, 3, 24, 9, 112)
-    rw = restrict_w(LANES, LANES, 64)
-    residual(x, sf, ALPHA, l_ref, w_ref, rw, t_ref, 8.0, 3, 24, 12, 112, 2)
-
-    for edge in (0, 1, 2, 15, 16, 17):
+    def smooth(u0, nu, values, loads, factors, v0, nv):
+        sweep(values, loads, ALPHA, l_ref, factors, u0, nu, v0, nv, stencil_pairs)
+
+    smooth(2, 12, x, sf, w_ref, 6, 128)
+    smooth(2, 12, x, sf, w_ref, 9, 112)
+    rw = restrict_w(LANES, LANES, 64, True)
+    residual(
+        x, sf, ALPHA, l_ref, w_ref, rw, t_ref, 8.0, 2, 12, 12, 112, 1, stencil_pairs
+    )
+
+    for edge in (0, 1, 8, 9):
         x3[0, edge] = jnp.zeros(x3.shape[2:], F32)
 
-    def narrow(j, _):
-        value = 0.0625 * narrow_plane(t_ref, tu_ref, j, 112, 50)
-        x3[0, j + 3, 3:53, :] = value
-        sf3[0, j + 3, 3:53, :] = value
-
-    lax.fori_loop(0, 12, narrow, None)
-    sweep(x3, sf3, ALPHA, l_ref, w3_ref, 3, 12, 6, 48)
-    sweep(x3, sf3, ALPHA, l_ref, w3_ref, 3, 12, 9, 48)
-    sweep(x3, sf3, ALPHA, l_ref, w3_ref, 3, 12, 12, 32)
-    sweep(x3, sf3, ALPHA, l_ref, w3_ref, 3, 12, 15, 32)
-    sweep(x3, sf3, ALPHA, l_ref, w3_ref, 3, 12, 18, 32)
-
-    pw = prolong_w(LANES, LANES, 64)
-
-    def wide(j, _):
-        def read(k):
-            return x3[0, j + 3 + k, 18:42, :]
-
+    def low_half(rows):
+        return lax.broadcasted_iota(jnp.int32, (rows, LANES), 1) < 64
+
+    def narrow(m, _):
+        parts = []
         for odd in (0, 1):
-            widen(read, not odd, tu_ref, z_ref, odd, 22)
-            fine = dot_split(z_ref[odd, 0:48, :], pw)
-            at = (0, 2 * j + odd + 3, slice(46, 94), slice(None))
-            x[at] = x[at] + fine
+            j = 2 * m + odd
+            before, own, after = (t_ref[j + i, 0:112, :] for i in range(3))
+            value = jnp.where(
+                low_half(112), 0.125 * (before + after) + 0.75 * own, 0.5 * (before + own)
+            )
+            parts.append(value + pltpu.roll(value, 64, 1))
+        tu_ref[0:112, :] = jnp.where(low_half(112), parts[0], parts[1])
+        at = [tu_ref[pl.ds(i, 50, stride=2), :] for i in range(5)]
+        value = 0.0625 * (0.125 * (at[0] + at[4]) + 0.5 * (at[1] + at[3]) + 0.75 * at[2])
+        x3[0, m + 2, 3:53, :] = value
+        sf3[0, m + 2, 3:53, :] = value
+
+    lax.fori_loop(0, 6, narrow, None)
+    smooth(2, 6, x3, sf3, w3_ref, 6, 48)
+    smooth(2, 6, x3, sf3, w3_ref, 9, 48)
+    smooth(2, 6, x3, sf3, w3_ref, 12, 32)
+    smooth(2, 6, x3, sf3, w3_ref, 15, 32)
+    smooth(2, 6, x3, sf3, w3_ref, 18, 32)
+
+    pw = prolong_w(LANES, LANES, 64, True)
+    for edge in (0, 13):
+        b_ref[edge] = jnp.zeros(b_ref.shape[1:], F32)
+    for m in range(6):
+        value = x3[0, m + 2, 18:42, :]
+        turned = pltpu.roll(value, 64, 1)
+        b_ref[2 * m + 1] = jnp.where(low_half(24), value, turned)
+        b_ref[2 * m + 2] = jnp.where(low_half(24), turned, value)
+
+    def wide(k, _):
+        before, own, after = (b_ref[k + i] for i in range(3))
+        tu_ref[0:24, :] = jnp.where(
+            low_half(24), 0.125 * (before + after) + 0.75 * own, 0.5 * (own + after)
+        )
+        first, mid, last = (tu_ref[i : i + 22, :] for i in range(3))
+        z_ref[0, pl.ds(0, 22, stride=2), :] = 0.125 * (first + last) + 0.75 * mid
+        z_ref[0, pl.ds(1, 22, stride=2), :] = 0.5 * (mid + last)
+        fine = dot_split(z_ref[0, 0:48, :], pw)
+        at = (0, k + 2, slice(46, 94), slice(None))
+        x[at] = x[at] + fine
 
     lax.fori_loop(0, 12, wide, None)
-    sweep(x, sf, ALPHA, l_ref, w_ref, 3, 24, 49, 32)
-    sweep(x, sf, ALPHA, l_ref, w_ref, 3, 24, 52, 32)
-    sweep(x, sf, ALPHA, l_ref, w_ref, 3, 24, 55, 32)
-
-    def give(k, _):
-        u = 6 * position - 5 + k
-        inside = jnp.logical_and(u >= 0, u < 24)
-        at = jnp.clip(u, 0, 23) + 3
-        e_out[k] = jnp.where(inside, x[0, at, 55:79, :], 0.0)
-
-    lax.fori_loop(0, 17, give, None)
+    smooth(2, 12, x, sf, w_ref, 49, 32)
+    smooth(2, 12, x, sf, w_ref, 52, 32)
+    smooth(2, 12, x, sf, w_ref, 55, 32)
+
+    for k in range(17):
+        index = 3 * position + (k - 5) // 2
+        inside = jnp.logical_and(index >= 0, index < 12)
+        value = x[0, jnp.clip(index, 0, 11) + 2, 55:79, :]
+        if k % 2 == 0:
+            value = pltpu.roll(value, 64, 1)
+        e_out[k] = jnp.where(inside & low_half(24), value, 0.0)
 
 
 def call(body, outs, scratch, operands, flops):
@@ -452,10 +520,19 @@
     return low, high
 
 
-def around_next(value):
+def along_next(value):
     low, high = along_dir(value, 12, 12)
-    extended = jnp.concatenate([low, value, high], axis=0)
-    return extended, ring(extended, PATCH, 1), ring(extended, PATCH, -1)
+    return jnp.concatenate([low, value, high], axis=0)
+
+
+def along_patch(value, low_rows, high_rows):
+    low = ring(value[:, low_rows[0] : low_rows[1]], PATCH, 1)
+    high = ring(value[:, high_rows[0] : high_rows[1]], PATCH, -1)
+    return low, high
+
+
+def after(value, other):
+    return lax.optimization_barrier((value, other))
 
 
 def inside_lanes(first, count, per, total):
@@ -515,7 +592,9 @@
         10**10,
     )
 
-    f1_own, f1_low, f1_high = around_next(f1)
+    f1_own = along_next(f1)
+    x0, f1_own = after(x0, f1_own)
+    f1_low, f1_high = along_patch(f1_own, (0, 12), (0, 12))
     window1 = ((1, 36, 48, LANES), F32)
     left1 = ((28, 32, 512), BF16)
     w1 = ((640, 128), BF16)
@@ -529,25 +608,28 @@
 
     x0_low, x0_high = along_dir(x0, 9, 9)
     x0_own = jnp.concatenate([x0_low, x0, x0_high], axis=0)
-    x0_low = ring(x0_own[:, 8:24], PATCH, 1)
-    x0_high = ring(x0_own[:, 0:16], PATCH, -1)
-    x1_own, x1_low, x1_high = around_next(x1)
+    x0_own, f2 = after(x0_own, f2)
+    x0_low, x0_high = along_patch(x0_own, (8, 24), (0, 16))
+    x1_own = along_next(x1)
 
     same = lax.all_to_all(jnp.broadcast_to(f2[None], (64, 18, 128)), ("pz", "dir"), 0, 0)
+    x1_own, same = after(x1_own, same)
     other = lax.ppermute(same, "core", [(0, 1), (1, 0)])
+    x1_low, x1_high = along_patch(x1_own, (0, 12), (0, 12))
     (e2,) = call(
         coarse,
         [shape_of(17, 24, 128)],
         [
-            ((1, 30, 144, LANES), F32),
-            ((1, 30, 144, LANES), F32),
-            ((24, 128, 512), BF16),
+            ((1, 16, 144, LANES), F32),
+            ((1, 16, 144, LANES), F32),
+            ((12, 128, 512), BF16),
             w1,
-            ((29, 112, 128), F32),
+            ((14, 112, 128), F32),
             ((112, 128), F32),
-            ((1, 18, 64, LANES), F32),
-            ((1, 18, 64, LANES), F32),
+            ((1, 10, 64, LANES), F32),
+            ((1, 10, 64, LANES), F32),
             w1,
+            ((14, 24, 128), F32),
             ((2, 48, 128), F32),
         ],
         (same, other),

time: 203 us -> 195 us (0.961)
  Pallas kernels: 71.5 us -> 65.9 us
  local copies, waits for them, and re-layouts: 16.6 us -> 12 us
  waiting for transfers between devices: 61.9 us -> 64.6 us
    pallas_call x5, Pallas kernels: 71.5 us -> 65.9 us  [call(): pl.pallas_call(body, out_shape=list(outs), in_specs=[vmem] * len(operands...]
    unnamed x45 -> x39, local copies, waits for them, and re-layouts: 10.5 us -> 6.69 us
    all_to_all x1, waiting for transfers between devices: 0.01 us -> 2.58 us  [on_device(): lax.all_to_all(jnp.broadcast_to(f2[None], (64, 18, 128)), ('pz', 'dir'),...]
  transfers between devices with their start and end apart: 22 -> 22, of which waited for: 11 -> 13; matrix products, arithmetic and copies ran while one was open for 3% -> 1% of each run, Pallas kernels for 18% -> 14%
where the time goes in v2:
time: 195 us; the launch traced here: 194 us
  Pallas kernels  65.9 us (34%)
  waiting for transfers between devices  64.6 us (33%)
  starting transfers between devices  48.5 us (25%)
  local copies, waits for them, and re-layouts  12 us (6%)
  other arithmetic  2.9 us (1%)
    pallas_call x5, Pallas kernels, call(): pl.pallas_call(body, out_shape=list(outs), in_specs=[vmem] * len(operands...  65.9 us
    ppermute x20, waiting for transfers between devices, ring(): return lax.ppermute(value, axes if len(axes) > 1 else axes[0], pairs)  62 us
    ppermute x20, starting transfers between devices, ring(): return lax.ppermute(value, axes if len(axes) > 1 else axes[0], pairs)  38.8 us
    unnamed x39, local copies, waits for them, and re-layouts  6.69 us
    all_to_all x1, starting transfers between devices, on_device(): lax.all_to_all(jnp.broadcast_to(f2[None], (64, 18, 128)), ('pz', 'dir'),...  6.14 us
  transfers between devices with their start and end apart: 22, of which 13 were waited for; matrix products, arithmetic and copies ran while one was open for 1% of the time, Pallas kernels for 14%

profile of v2, /device:TPU:6, one launch (start us, length us, event | category | flops | bytes accessed | tf_op | source)
XLA Modules:
  0.0 194.3 jit_solution(12707878442103292849)
XLA Ops:
  0.0 0.8 convert_element_type.44
  0.9 0.8 copy.11
  1.7 1.0 slice.95
  2.7 1.0 slice.96
  3.7 0.9 pad_maximum_fusion.2
  4.5 0.8 collective-permute-start.1
  5.4 2.5 %collective-permute-start = (f32[26,24,256]{2,1,0:T(8,128)S(1)}, f32[26,24,256]{2,1,0:T(8,128)S(1)}, u32[]{:S(2)}, u32[]{:S(2)}) collective-permute-start(f32[26,24,256]{2,1,0:T(8,128)S(1)} %pad_maximum_fusion.1), channel_id=1, source_target_pairs={{0,1},{1,2},{2,3},{3,0},{4,5},{5,6},{6,7},{7,4},{8,9},{9,10},{10,1... | collective-permute-start | bytes 1916936 | tf_op jit(solution)/shard_map/ppermute | solution.py:513
  7.9 13.1 %collective-permute-done.1 = f32[24,24,256]{2,1,0:T(8,128)S(1)} collective-permute-done((f32[24,24,256]{2,1,0:T(8,128)}, f32[24,24,256]{2,1,0:T(8,128)S(1)}, u32[]{:S(2)}, u32[]{:S(2)}) %collective-permute-start.1) | collective-permute-done | bytes 589856 | tf_op jit(solution)/shard_map/ppermute | solution.py:513
  21.0 0.3 collective-permute-done
  21.4 0.4 copy-done.15
  21.8 0.3 copy-done.14
  22.2 1.0 slice_dynamic-update-slice_fusion
  23.2 1.0 slice_dynamic-update-slice_fusion.1
  24.2 1.0 slice_dynamic-update-slice_fusion.2
  25.2 1.1 constant_dynamic-update-slice_fusion.1
  26.5 1.0 slice_dynamic-update-slice_fusion.3
  27.5 0.4 fusion.4
  27.9 5.0 %collective-permute-start.3 = (f32[97,16,256]{2,1,0:T(8,128)S(1)}, f32[97,16,256]{2,1,0:T(8,128)S(1)}, u32[]{:S(2)}, u32[]{:S(2)}) collective-permute-start(f32[97,16,256]{2,1,0:T(8,128)S(1)} %get-tuple-element.25), channel_id=1, source_target_pairs={{0,124},{4,0},{8,4},{12,8},{16,12},{20,16},{24,20},{28,24},{32,28}... | collective-permute-start | bytes 4767752 | tf_op jit(solution)/shard_map/ppermute | solution.py:513
  33.0 18.0 %collective-permute-done.3.high = f32[97,16,256]{2,1,0:T(8,128)S(1)} collective-permute-done((f32[97,16,256]{2,1,0:T(8,128)S(1)}, f32[97,16,256]{2,1,0:T(8,128)S(1)}, u32[]{:S(2)}, u32[]{:S(2)}) %collective-permute-start.3) | collective-permute-done | bytes 1589280 | tf_op jit(solution)/shard_map/ppermute | solution.py:513
  51.0 5.2 %collective-permute-done.2.low = f32[97,16,256]{2,1,0:T(8,128)S(1)} collective-permute-done((f32[97,16,256]{2,1,0:T(8,128)S(1)}, f32[97,16,256]{2,1,0:T(8,128)S(1)}, u32[]{:S(2)}, u32[]{:S(2)}) %collective-permute-start.2) | collective-permute-done | bytes 1589280 | tf_op jit(solution)/shard_map/ppermute | solution.py:513
  56.2 21.7 %shard_map.46 = (f32[24,24,256]{2,1,0:T(8,128)S(1)}, f32[12,12,128]{2,1,0:T(8,128)S(1)}) custom-call(f32[97,24,256]{2,1,0:T(8,128)S(1)} %constant_dynamic-update-slice_fusion.own, f32[97,16,256]{2,1,0:T(8,128)S(1)} %collective-permute-done.2.low, f32[97,16,256]{2,1,0:T(8,128)S(1)} %collective-permute-done.3.high, f32[56,128]{1,0:T(8,128)S(1)} %pad_maximum_fusion.6.mask), custom_call_target="tpu_custom_call" | custom-call | flops 10000000000 | bytes 23158784 | tf_op jit(solution)/shard_map/pallas_call | solution.py:493
  77.9 3.5 %collective-permute-start.4 = (f32[12,12,128]{2,1,0:T(8,128)S(1)}, f32[12,12,128]{2,1,0:T(8,128)S(1)}, u32[]{:S(2)}, u32[]{:S(2)}) collective-permute-start(f32[12,12,128]{2,1,0:T(8,128)S(1)} %get-tuple-element.16), channel_id=1, source_target_pairs={{0,1},{1,2},{2,3},{3,0},{4,5},{5,6},{6,7},{7,4},{8,9},{9,10},{10,1... | collective-permute-start | bytes 221192 | tf_op jit(solution)/shard_map/ppermute | solution.py:513
  81.5 2.1 %collective-permute-done.4 = f32[12,12,128]{2,1,0:T(8,128)S(1)} collective-permute-done((f32[12,12,128]{2,1,0:T(8,128)S(1)}, f32[12,12,128]{2,1,0:T(8,128)S(1)}, u32[]{:S(2)}, u32[]{:S(2)}) %collective-permute-start.4) | collective-permute-done | bytes 73760 | tf_op jit(solution)/shard_map/ppermute | solution.py:513
  83.6 3.6 %collective-permute-done.5 = f32[12,12,128]{2,1,0:T(8,128)S(1)} collective-permute-done((f32[12,12,128]{2,1,0:T(8,128)S(1)}, f32[12,12,128]{2,1,0:T(8,128)S(1)}, u32[]{:S(2)}, u32[]{:S(2)}) %collective-permute-start.5) | collective-permute-done | bytes 73760 | tf_op jit(solution)/shard_map/ppermute | solution.py:513
  87.4 2.0 %collective-permute-start.7 = (f32[9,24,256]{2,1,0:T(8,128)S(1)}, f32[9,24,256]{2,1,0:T(8,128)S(1)}, u32[]{:S(2)}, u32[]{:S(2)}) collective-permute-start(f32[9,24,256]{2,1,0:T(8,128)S(1)} %get-tuple-element.30), channel_id=1, source_target_pairs={{0,3},{1,0},{2,1},{3,2},{4,7},{5,4},{6,5},{7,6},{8,11},{9,8},{10,9... | collective-permute-start | bytes 663560 | tf_op jit(solution)/shard_map/ppermute | solution.py:513
  89.4 5.1 %collective-permute-start.9 = (f32[36,12,128]{2,1,0:T(8,128)S(1)}, f32[36,12,128]{2,1,0:T(8,128)S(1)}, u32[]{:S(2)}, u32[]{:S(2)}) collective-permute-start(f32[36,12,128]{2,1,0:T(8,128)S(1)} %pad_maximum_fusion.3.own), channel_id=1, source_target_pairs={{0,124},{4,0},{8,4},{12,8},{16,12},{20,16},{24,20},{28,24},{32,28}... | collective-permute-start | bytes 663560 | tf_op jit(solution)/shard_map/ppermute | solution.py:513
  94.7 4.2 %collective-permute-done.8.low = f32[36,12,128]{2,1,0:T(8,128)S(1)} collective-permute-done((f32[36,12,128]{2,1,0:T(8,128)S(1)}, f32[36,12,128]{2,1,0:T(8,128)S(1)}, u32[]{:S(2)}, u32[]{:S(2)}) %collective-permute-start.8) | collective-permute-done | bytes 221216 | tf_op jit(solution)/shard_map/ppermute | solution.py:513
  98.9 3.7 %shard_map.47 = (f32[12,12,128]{2,1,0:T(8,128)S(1)}, f32[18,128]{1,0:T(8,128)S(1)}) custom-call(f32[36,12,128]{2,1,0:T(8,128)S(1)} %pad_maximum_fusion.3.own, f32[36,12,128]{2,1,0:T(8,128)S(1)} %collective-permute-done.8.low, f32[36,12,128]{2,1,0:T(8,128)S(1)} %collective-permute-done.9.high, f32[40,128]{1,0:T(8,128)S(1)} %select_maximum_fusion.3.mask), custom_call_target="tpu_custom_call" | custom-call | flops 1000000000 | bytes 4915200 | tf_op jit(solution)/shard_map/pallas_call | solution.py:493
  102.6 0.9 broadcast_in_dim.16
  103.5 6.1 %all-to-all-start = ((f32[64,18,128]{2,1,0:T(8,128)}), f32[64,18,128]{2,1,0:T(8,128)}, u32[]{:S(2)}, u32[]{:S(2)}) async-start(f32[64,18,128]{2,1,0:T(8,128)} %broadcast_in_dim.16), calls=%async_computation | async-start | bytes 1572864 | tf_op jit(solution)/shard_map/all_to_all | solution.py:615
  109.7 0.7 collective-permute-start.12
  110.4 1.4 collective-permute-start.13
  111.8 7.7 %collective-permute-done.12 = f32[12,12,128]{2,1,0:T(8,128)S(1)} collective-permute-done((f32[12,12,128]{2,1,0:T(8,128)S(1)}, f32[12,12,128]{2,1,0:T(8,128)S(1)}, u32[]{:S(2)}, u32[]{:S(2)}) %collective-permute-start.12) | collective-permute-done | bytes 73760 | tf_op jit(solution)/shard_map/ppermute | solution.py:513
  119.5 0.7 pad_maximum_fusion.4.x_own
  120.2 2.6 %all-to-all-done.same = f32[64,18,128]{2,1,0:T(8,128)} async-done(((f32[64,18,128]{2,1,0:T(8,128)}), f32[64,18,128]{2,1,0:T(8,128)}, u32[]{:S(2)}, u32[]{:S(2)}) %all-to-all-start) | async-done | bytes 589856 | tf_op jit(solution)/shard_map/all_to_all | solution.py:615
  122.8 1.3 copy.13
  124.1 3.6 %collective-permute-start.16 = (f32[64,18,128]{2,0,1:T(8,128)S(1)}, f32[64,18,128]{2,0,1:T(8,128)S(1)}, u32[]{:S(2)}, u32[]{:S(2)}) collective-permute-start(f32[64,18,128]{2,0,1:T(8,128)S(1)} %copy.13), channel_id=1, source_target_pairs={{0,4},{4,0},{1,5},{5,1},{2,6},{6,2},{3,7},{7,3},{8,12},{12,8},{9,1... | collective-permute-start | bytes 1769480 | tf_op jit(solution)/shard_map/ppermute | solution.py:617
  127.8 5.1 %collective-permute-start.11 = (f32[42,16,256]{2,1,0:T(8,128)S(1)}, f32[42,16,256]{2,1,0:T(8,128)S(1)}, u32[]{:S(2)}, u32[]{:S(2)}) collective-permute-start(f32[42,16,256]{2,1,0:T(8,128)S(1)} %get-tuple-element.27), channel_id=1, source_target_pairs={{0,124},{4,0},{8,4},{12,8},{16,12},{20,16},{24,20},{28,24},{32,28}... | collective-permute-start | bytes 2064392 | tf_op jit(solution)/shard_map/ppermute | solution.py:513
  132.9 5.1 %collective-permute-start.15 = (f32[36,12,128]{2,1,0:T(8,128)S(1)}, f32[36,12,128]{2,1,0:T(8,128)S(1)}, u32[]{:S(2)}, u32[]{:S(2)}) collective-permute-start(f32[36,12,128]{2,1,0:T(8,128)S(1)} %copy-done.2), channel_id=1, source_target_pairs={{0,124},{4,0},{8,4},{12,8},{16,12},{20,16},{24,20},{28,24},{32,28}... | collective-permute-start | bytes 663560 | tf_op jit(solution)/shard_map/ppermute | solution.py:513
  138.0 0.4 copy.14.other
  138.4 23.7 %shard_map.48.e2 = f32[17,24,128]{2,1,0:T(8,128)S(1)} custom-call(f32[64,18,128]{2,1,0:T(8,128)} %all-to-all-done.same, f32[64,18,128]{2,1,0:T(8,128)S(1)} %copy.14.other), custom_call_target="tpu_custom_call" | custom-call | flops 4000000000 | bytes 8372224 | tf_op jit(solution)/shard_map/pallas_call | solution.py:493
  162.2 3.4 %shard_map.49 = f32[12,12,128]{2,1,0:T(8,128)S(1)} custom-call(f32[36,12,128]{2,1,0:T(8,128)S(1)} %copy-done.1, f32[36,12,128]{2,1,0:T(8,128)S(1)} %copy-done.10, f32[36,12,128]{2,1,0:T(8,128)S(1)} %copy-done.12, f32[40,128]{1,0:T(8,128)S(1)} %copy-done.4, f32[36,12,128]{2,1,0:T(8,128)S(1)} %copy-done.2, f32[36,12,128]{2,1,0:T(8,128)S(1)} %collective-permute-done.14.x_low, ...), custom_call_target="tpu_custom_call" | custom-call | flops 1000000000 | bytes 5980160 | tf_op jit(solution)/shard_map/pallas_call | solution.py:493
  165.6 2.4 %collective-permute-start.17 = (f32[6,12,128]{2,1,0:T(8,128)S(1)}, f32[6,12,128]{2,1,0:T(8,128)S(1)}, u32[]{:S(2)}, u32[]{:S(2)}) collective-permute-start(f32[6,12,128]{2,1,0:T(8,128)S(1)} %get-tuple-element.33), channel_id=1, source_target_pairs={{0,1},{1,2},{2,3},{3,0},{4,5},{5,6},{6,7},{7,4},{8,9},{9,10},{10,1... | collective-permute-start | bytes 110600 | tf_op jit(solution)/shard_map/ppermute | solution.py:513
  168.0 1.7 collective-permute-done.17
  169.8 3.5 %collective-permute-done.18 = f32[6,12,128]{2,1,0:T(8,128)S(1)} collective-permute-done((f32[6,12,128]{2,1,0:T(8,128)S(1)}, f32[6,12,128]{2,1,0:T(8,128)S(1)}, u32[]{:S(2)}, u32[]{:S(2)}) %collective-permute-start.18) | collective-permute-done | bytes 36896 | tf_op jit(solution)/shard_map/ppermute | solution.py:513
  173.5 5.1 %collective-permute-start.20 = (f32[24,8,128]{2,1,0:T(8,128)S(1)}, f32[24,8,128]{2,1,0:T(8,128)S(1)}, u32[]{:S(2)}, u32[]{:S(2)}) collective-permute-start(f32[24,8,128]{2,1,0:T(8,128)S(1)} %get-tuple-element.31), channel_id=1, source_target_pairs={{0,124},{4,0},{8,4},{12,8},{16,12},{20,16},{24,20},{28,24},{32,28}... | collective-permute-start | bytes 294920 | tf_op jit(solution)/shard_map/ppermute | solution.py:513
  178.5 2.3 %collective-permute-done.19.e_low = f32[24,8,128]{2,1,0:T(8,128)S(1)} collective-permute-done((f32[24,8,128]{2,1,0:T(8,128)S(1)}, f32[24,8,128]{2,1,0:T(8,128)S(1)}, u32[]{:S(2)}, u32[]{:S(2)}) %collective-permute-start.19) | collective-permute-done | bytes 98336 | tf_op jit(solution)/shard_map/ppermute | solution.py:513
  180.8 13.5 %shard_map.50 = f32[24,24,256]{2,1,0:T(8,128)} custom-call(f32[97,24,256]{2,1,0:T(8,128)S(1)} %constant_dynamic-update-slice_fusion.own, f32[97,16,256]{2,1,0:T(8,128)S(1)} %copy-done.8, f32[97,16,256]{2,1,0:T(8,128)S(1)} %copy-done.6, f32[56,128]{1,0:T(8,128)S(1)} %pad_maximum_fusion.6.mask, f32[42,24,256]{2,1,0:T(8,128)S(1)} %pad_maximum_fusion.x_own, ...), custom_call_target="tpu_custom_call" | custom-call | flops 10000000000 | bytes 26386432 | tf_op jit(solution)/shard_map/pallas_call | solution.py:493
  (84 shorter events, 1.4 us)
Async XLA Ops:
  0.0 5.4 %slice-start = ((f32[24,24,256]{2,1,0:T(8,128)}), f32[14,24,256]{2,1,0:T(8,128)S(1)}, s32[]{:S(2)}) async-start(f32[24,24,256]{2,1,0:T(8,128)} %param.5), calls=%async_computation.1 | async-start | bytes 688128 | tf_op jit(solution)/shard_map/slice | solution.py:554
  0.0 5.4 %slice-start.1 = ((f32[24,24,256]{2,1,0:T(8,128)}), f32[11,24,256]{2,1,0:T(8,128)S(1)}, s32[]{:S(2)}) async-start(f32[24,24,256]{2,1,0:T(8,128)} %param.4), calls=%async_computation.2 | async-start | bytes 540672 | tf_op jit(solution)/shard_map/slice | solution.py:554
  3.6 19.5 %copy-start.13 = (f32[24,24,256]{2,1,0:T(8,128)S(1)}, f32[24,24,256]{2,1,0:T(8,128)}, u32[]{:S(2)}) copy-start(f32[24,24,256]{2,1,0:T(8,128)} %param.5) | copy-start | bytes 1769476
  4.5 16.5 %collective-permute-start.1 = (f32[24,24,256]{2,1,0:T(8,128)}, f32[24,24,256]{2,1,0:T(8,128)S(1)}, u32[]{:S(2)}, u32[]{:S(2)}) collective-permute-start(f32[24,24,256]{2,1,0:T(8,128)} %pad_maximum_fusion.2), channel_id=1, source_target_pairs={{0,3},{1,0},{2,1},{3,2},{4,7},{5,4},{6,5},{7,6},{8,11},{9,8},{10,9... | collective-permute-start | bytes 1769480 | tf_op jit(solution)/shard_map/ppermute | solution.py:513
  5.4 15.9 %collective-permute-start = (f32[26,24,256]{2,1,0:T(8,128)S(1)}, f32[26,24,256]{2,1,0:T(8,128)S(1)}, u32[]{:S(2)}, u32[]{:S(2)}) collective-permute-start(f32[26,24,256]{2,1,0:T(8,128)S(1)} %pad_maximum_fusion.1), channel_id=1, source_target_pairs={{0,1},{1,2},{2,3},{3,0},{4,5},{5,6},{6,7},{7,4},{8,9},{9,10},{10,1... | collective-permute-start | bytes 1916936 | tf_op jit(solution)/shard_map/ppermute | solution.py:513
  21.0 0.8 copy-start.15
  21.3 0.8 copy-start.14
  27.9 23.1 %collective-permute-start.3 = (f32[97,16,256]{2,1,0:T(8,128)S(1)}, f32[97,16,256]{2,1,0:T(8,128)S(1)}, u32[]{:S(2)}, u32[]{:S(2)}) collective-permute-start(f32[97,16,256]{2,1,0:T(8,128)S(1)} %get-tuple-element.25), channel_id=1, source_target_pairs={{0,124},{4,0},{8,4},{12,8},{16,12},{20,16},{24,20},{28,24},{32,28}... | collective-permute-start | bytes 4767752 | tf_op jit(solution)/shard_map/ppermute | solution.py:513
  32.9 23.3 %collective-permute-start.2 = (f32[97,16,256]{2,1,0:T(8,128)S(1)}, f32[97,16,256]{2,1,0:T(8,128)S(1)}, u32[]{:S(2)}, u32[]{:S(2)}) collective-permute-start(f32[97,16,256]{2,1,0:T(8,128)S(1)} %get-tuple-element.26), channel_id=1, source_target_pairs={{0,4},{4,8},{8,12},{12,16},{16,20},{20,24},{24,28},{28,32},{32,36}... | collective-permute-start | bytes 4767752 | tf_op jit(solution)/shard_map/ppermute | solution.py:513
  51.0 30.4 %copy-start.5 = (f32[97,16,256]{2,1,0:T(8,128)}, f32[97,16,256]{2,1,0:T(8,128)S(1)}, u32[]{:S(2)}) copy-start(f32[97,16,256]{2,1,0:T(8,128)S(1)} %collective-permute-done.3.high) | copy-start | bytes 4767748
  56.2 33.2 %copy-start.7 = (f32[97,16,256]{2,1,0:T(8,128)}, f32[97,16,256]{2,1,0:T(8,128)S(1)}, u32[]{:S(2)}) copy-start(f32[97,16,256]{2,1,0:T(8,128)S(1)} %collective-permute-done.2.low) | copy-start | bytes 4767748
  77.9 5.7 %collective-permute-start.4 = (f32[12,12,128]{2,1,0:T(8,128)S(1)}, f32[12,12,128]{2,1,0:T(8,128)S(1)}, u32[]{:S(2)}, u32[]{:S(2)}) collective-permute-start(f32[12,12,128]{2,1,0:T(8,128)S(1)} %get-tuple-element.16), channel_id=1, source_target_pairs={{0,1},{1,2},{2,3},{3,0},{4,5},{5,6},{6,7},{7,4},{8,9},{9,10},{10,1... | collective-permute-start | bytes 221192 | tf_op jit(solution)/shard_map/ppermute | solution.py:513
  81.4 5.8 %collective-permute-start.5 = (f32[12,12,128]{2,1,0:T(8,128)S(1)}, f32[12,12,128]{2,1,0:T(8,128)S(1)}, u32[]{:S(2)}, u32[]{:S(2)}) collective-permute-start(f32[12,12,128]{2,1,0:T(8,128)S(1)} %get-tuple-element.16), channel_id=1, source_target_pairs={{0,3},{1,0},{2,1},{3,2},{4,7},{5,4},{6,5},{7,6},{8,11},{9,8},{10,9... | collective-permute-start | bytes 221192 | tf_op jit(solution)/shard_map/ppermute | solution.py:513
  87.2 15.3 %copy-start = (f32[36,12,128]{2,1,0:T(8,128)}, f32[36,12,128]{2,1,0:T(8,128)S(1)}, u32[]{:S(2)}) copy-start(f32[36,12,128]{2,1,0:T(8,128)S(1)} %pad_maximum_fusion.3.own) | copy-start | bytes 663556
  87.3 7.2 %collective-permute-start.6 = (f32[9,24,256]{2,1,0:T(8,128)S(1)}, f32[9,24,256]{2,1,0:T(8,128)S(1)}, u32[]{:S(2)}, u32[]{:S(2)}) collective-permute-start(f32[9,24,256]{2,1,0:T(8,128)S(1)} %get-tuple-element.29), channel_id=1, source_target_pairs={{0,1},{1,2},{2,3},{3,0},{4,5},{5,6},{6,7},{7,4},{8,9},{9,10},{10,1... | collective-permute-start | bytes 663560 | tf_op jit(solution)/shard_map/ppermute | solution.py:513
  87.4 7.2 %collective-permute-start.7 = (f32[9,24,256]{2,1,0:T(8,128)S(1)}, f32[9,24,256]{2,1,0:T(8,128)S(1)}, u32[]{:S(2)}, u32[]{:S(2)}) collective-permute-start(f32[9,24,256]{2,1,0:T(8,128)S(1)} %get-tuple-element.30), channel_id=1, source_target_pairs={{0,3},{1,0},{2,1},{3,2},{4,7},{5,4},{6,5},{7,6},{8,11},{9,8},{10,9... | collective-permute-start | bytes 663560 | tf_op jit(solution)/shard_map/ppermute | solution.py:513
  89.4 9.5 %collective-permute-start.8 = (f32[36,12,128]{2,1,0:T(8,128)S(1)}, f32[36,12,128]{2,1,0:T(8,128)S(1)}, u32[]{:S(2)}, u32[]{:S(2)}) collective-permute-start(f32[36,12,128]{2,1,0:T(8,128)S(1)} %pad_maximum_fusion.3.own), channel_id=1, source_target_pairs={{0,4},{4,8},{8,12},{12,16},{16,20},{20,24},{24,28},{28,32},{32,36}... | collective-permute-start | bytes 663560 | tf_op jit(solution)/shard_map/ppermute | solution.py:513
  89.4 9.5 %collective-permute-start.9 = (f32[36,12,128]{2,1,0:T(8,128)S(1)}, f32[36,12,128]{2,1,0:T(8,128)S(1)}, u32[]{:S(2)}, u32[]{:S(2)}) collective-permute-start(f32[36,12,128]{2,1,0:T(8,128)S(1)} %pad_maximum_fusion.3.own), channel_id=1, source_target_pairs={{0,124},{4,0},{8,4},{12,8},{16,12},{20,16},{24,20},{28,24},{32,28}... | collective-permute-start | bytes 663560 | tf_op jit(solution)/shard_map/ppermute | solution.py:513
  94.5 8.1 %copy-start.3 = (f32[40,128]{1,0:T(8,128)}, f32[40,128]{1,0:T(8,128)S(1)}, u32[]{:S(2)}) copy-start(f32[40,128]{1,0:T(8,128)S(1)} %select_maximum_fusion.3.mask) | copy-start | bytes 61444
  98.9 3.7 %copy-start.9 = (f32[36,12,128]{2,1,0:T(8,128)}, f32[36,12,128]{2,1,0:T(8,128)S(1)}, u32[]{:S(2)}) copy-start(f32[36,12,128]{2,1,0:T(8,128)S(1)} %collective-permute-done.8.low) | copy-start | bytes 663556
  98.9 3.7 %copy-start.11 = (f32[36,12,128]{2,1,0:T(8,128)}, f32[36,12,128]{2,1,0:T(8,128)S(1)}, u32[]{:S(2)}) copy-start(f32[36,12,128]{2,1,0:T(8,128)S(1)} %collective-permute-done.9.high) | copy-start | bytes 663556
  103.5 19.2 %all-to-all-start = ((f32[64,18,128]{2,1,0:T(8,128)}), f32[64,18,128]{2,1,0:T(8,128)}, u32[]{:S(2)}, u32[]{:S(2)}) async-start(f32[64,18,128]{2,1,0:T(8,128)} %broadcast_in_dim.16), calls=%async_computation | async-start | bytes 1572864 | tf_op jit(solution)/shard_map/all_to_all | solution.py:615
  109.7 9.8 %collective-permute-start.12 = (f32[12,12,128]{2,1,0:T(8,128)S(1)}, f32[12,12,128]{2,1,0:T(8,128)S(1)}, u32[]{:S(2)}, u32[]{:S(2)}) collective-permute-start(f32[12,12,128]{2,1,0:T(8,128)S(1)} %get-tuple-element.21), channel_id=1, source_target_pairs={{0,1},{1,2},{2,3},{3,0},{4,5},{5,6},{6,7},{7,4},{8,9},{9,10},{10,1... | collective-permute-start | bytes 221192 | tf_op jit(solution)/shard_map/ppermute | solution.py:513
  110.4 9.1 %collective-permute-start.13 = (f32[12,12,128]{2,1,0:T(8,128)S(1)}, f32[12,12,128]{2,1,0:T(8,128)S(1)}, u32[]{:S(2)}, u32[]{:S(2)}) collective-permute-start(f32[12,12,128]{2,1,0:T(8,128)S(1)} %get-tuple-element.21), channel_id=1, source_target_pairs={{0,3},{1,0},{2,1},{3,2},{4,7},{5,4},{6,5},{7,6},{8,11},{9,8},{10,9... | collective-permute-start | bytes 221192 | tf_op jit(solution)/shard_map/ppermute | solution.py:513
  122.8 10.1 %copy-start.2 = (f32[36,12,128]{2,1,0:T(8,128)S(1)}, f32[36,12,128]{2,1,0:T(8,128)}, u32[]{:S(2)}) copy-start(f32[36,12,128]{2,1,0:T(8,128)} %pad_maximum_fusion.4.x_own) | copy-start | bytes 663556
  124.1 13.9 %collective-permute-start.16 = (f32[64,18,128]{2,0,1:T(8,128)S(1)}, f32[64,18,128]{2,0,1:T(8,128)S(1)}, u32[]{:S(2)}, u32[]{:S(2)}) collective-permute-start(f32[64,18,128]{2,0,1:T(8,128)S(1)} %copy.13), channel_id=1, source_target_pairs={{0,4},{4,0},{1,5},{5,1},{2,6},{6,2},{3,7},{7,3},{8,12},{12,8},{9,1... | collective-permute-start | bytes 1769480 | tf_op jit(solution)/shard_map/ppermute | solution.py:617
  127.8 50.8 %collective-permute-start.10 = (f32[42,16,256]{2,1,0:T(8,128)S(1)}, f32[42,16,256]{2,1,0:T(8,128)S(1)}, u32[]{:S(2)}, u32[]{:S(2)}) collective-permute-start(f32[42,16,256]{2,1,0:T(8,128)S(1)} %get-tuple-element.28), channel_id=1, source_target_pairs={{0,4},{4,8},{8,12},{12,16},{16,20},{20,24},{24,28},{28,32},{32,36}... | collective-permute-start | bytes 2064392 | tf_op jit(solution)/shard_map/ppermute | solution.py:513
  127.8 50.7 %collective-permute-start.11 = (f32[42,16,256]{2,1,0:T(8,128)S(1)}, f32[42,16,256]{2,1,0:T(8,128)S(1)}, u32[]{:S(2)}, u32[]{:S(2)}) collective-permute-start(f32[42,16,256]{2,1,0:T(8,128)S(1)} %get-tuple-element.27), channel_id=1, source_target_pairs={{0,124},{4,0},{8,4},{12,8},{16,12},{20,16},{24,20},{28,24},{32,28}... | collective-permute-start | bytes 2064392 | tf_op jit(solution)/shard_map/ppermute | solution.py:513
  132.9 29.2 %collective-permute-start.14 = (f32[36,12,128]{2,1,0:T(8,128)S(1)}, f32[36,12,128]{2,1,0:T(8,128)S(1)}, u32[]{:S(2)}, u32[]{:S(2)}) collective-permute-start(f32[36,12,128]{2,1,0:T(8,128)S(1)} %copy-done.2), channel_id=1, source_target_pairs={{0,4},{4,8},{8,12},{12,16},{16,20},{20,24},{24,28},{28,32},{32,36}... | collective-permute-start | bytes 663560 | tf_op jit(solution)/shard_map/ppermute | solution.py:513
  132.9 29.2 %collective-permute-start.15 = (f32[36,12,128]{2,1,0:T(8,128)S(1)}, f32[36,12,128]{2,1,0:T(8,128)S(1)}, u32[]{:S(2)}, u32[]{:S(2)}) collective-permute-start(f32[36,12,128]{2,1,0:T(8,128)S(1)} %copy-done.2), channel_id=1, source_target_pairs={{0,124},{4,0},{8,4},{12,8},{16,12},{20,16},{24,20},{28,24},{32,28}... | collective-permute-start | bytes 663560 | tf_op jit(solution)/shard_map/ppermute | solution.py:513
  138.3 23.8 %copy-start.1 = (f32[36,12,128]{2,1,0:T(8,128)S(1)}, f32[36,12,128]{2,1,0:T(8,128)}, u32[]{:S(2)}) copy-start(f32[36,12,128]{2,1,0:T(8,128)} %copy-done) | copy-start | bytes 663556
  138.3 23.8 %copy-start.4 = (f32[40,128]{1,0:T(8,128)S(1)}, f32[40,128]{1,0:T(8,128)}, u32[]{:S(2)}) copy-start(f32[40,128]{1,0:T(8,128)} %copy-done.3) | copy-start | bytes 61444
  138.4 23.8 %copy-start.10 = (f32[36,12,128]{2,1,0:T(8,128)S(1)}, f32[36,12,128]{2,1,0:T(8,128)}, u32[]{:S(2)}) copy-start(f32[36,12,128]{2,1,0:T(8,128)} %copy-done.9) | copy-start | bytes 663556
  138.4 23.8 %copy-start.12 = (f32[36,12,128]{2,1,0:T(8,128)S(1)}, f32[36,12,128]{2,1,0:T(8,128)}, u32[]{:S(2)}) copy-start(f32[36,12,128]{2,1,0:T(8,128)} %copy-done.11) | copy-start | bytes 663556
  162.1 18.7 %copy-start.6 = (f32[97,16,256]{2,1,0:T(8,128)S(1)}, f32[97,16,256]{2,1,0:T(8,128)}, u32[]{:S(2)}) copy-start(f32[97,16,256]{2,1,0:T(8,128)} %copy-done.5) | copy-start | bytes 4767748
  162.1 18.7 %copy-start.8 = (f32[97,16,256]{2,1,0:T(8,128)S(1)}, f32[97,16,256]{2,1,0:T(8,128)}, u32[]{:S(2)}) copy-start(f32[97,16,256]{2,1,0:T(8,128)} %copy-done.7) | copy-start | bytes 4767748
  165.6 4.2 %collective-permute-start.17 = (f32[6,12,128]{2,1,0:T(8,128)S(1)}, f32[6,12,128]{2,1,0:T(8,128)S(1)}, u32[]{:S(2)}, u32[]{:S(2)}) collective-permute-start(f32[6,12,128]{2,1,0:T(8,128)S(1)} %get-tuple-element.33), channel_id=1, source_target_pairs={{0,1},{1,2},{2,3},{3,0},{4,5},{5,6},{6,7},{7,4},{8,9},{9,10},{10,1... | collective-permute-start | bytes 110600 | tf_op jit(solution)/shard_map/ppermute | solution.py:513
  168.0 5.3 %collective-permute-start.18 = (f32[6,12,128]{2,1,0:T(8,128)S(1)}, f32[6,12,128]{2,1,0:T(8,128)S(1)}, u32[]{:S(2)}, u32[]{:S(2)}) collective-permute-start(f32[6,12,128]{2,1,0:T(8,128)S(1)} %get-tuple-element.34), channel_id=1, source_target_pairs={{0,3},{1,0},{2,1},{3,2},{4,7},{5,4},{6,5},{7,6},{8,11},{9,8},{10,9... | collective-permute-start | bytes 110600 | tf_op jit(solution)/shard_map/ppermute | solution.py:513
  173.4 7.4 %collective-permute-start.19 = (f32[24,8,128]{2,1,0:T(8,128)S(1)}, f32[24,8,128]{2,1,0:T(8,128)S(1)}, u32[]{:S(2)}, u32[]{:S(2)}) collective-permute-start(f32[24,8,128]{2,1,0:T(8,128)S(1)} %get-tuple-element.32), channel_id=1, source_target_pairs={{0,4},{4,8},{8,12},{12,16},{16,20},{20,24},{24,28},{28,32},{32,36}... | collective-permute-start | bytes 294920 | tf_op jit(solution)/shard_map/ppermute | solution.py:513
  173.5 7.4 %collective-permute-start.20 = (f32[24,8,128]{2,1,0:T(8,128)S(1)}, f32[24,8,128]{2,1,0:T(8,128)S(1)}, u32[]{:S(2)}, u32[]{:S(2)}) collective-permute-start(f32[24,8,128]{2,1,0:T(8,128)S(1)} %get-tuple-element.31), channel_id=1, source_target_pairs={{0,124},{4,0},{8,4},{12,8},{16,12},{20,16},{24,20},{28,24},{32,28}... | collective-permute-start | bytes 294920 | tf_op jit(solution)/shard_map/ppermute | solution.py:513

commit v3 on v2

--- a/solution.py
+++ b/solution.py
@@ -234,26 +234,108 @@
 
 UB0, VB0, V0 = 14, 16, 64
 
-
-def fill_fine(own, low, high, mask, x_ref, sf_ref, sa_ref):
-    parts = ((low, 0, 16), (own, 16, 24), (high, 40, 16))
+UP_X, UP_F, DOWN_X, DOWN_F = 14, 11, 13, 10
+UP_AT = (0, 102 * UP_X, 102 * UP_X + 90 * UP_F)
+DOWN_AT = (0, 102 * DOWN_X, 102 * DOWN_X + 90 * DOWN_F)
+UP_ROWS = 2448
+DOWN_ROWS = 2256
+
+
+def pack_dir(guess, load, up, down, sems):
+    copies = [
+        pltpu.make_async_copy(guess.at[10:24], up.at[0:14], sems.at[0]),
+        pltpu.make_async_copy(load.at[13:24], up.at[14:25], sems.at[1]),
+        pltpu.make_async_copy(guess.at[0:13], down.at[0:13], sems.at[2]),
+        pltpu.make_async_copy(load.at[0:10], down.at[13:23], sems.at[3]),
+    ]
+    for copy in copies:
+        copy.start()
+    for copy in copies:
+        copy.wait()
+
+
+def x_plane(low, guess, high, u):
+    if u < 14:
+        return low.at[u]
+    return guess.at[u - 14] if u < 38 else high.at[u - 38]
+
+
+def f_plane(low, load, high, u):
+    if u < 11:
+        return low.at[14 + u]
+    return load.at[u - 11] if u < 35 else high.at[13 + u - 35]
+
+
+def pack_patch(guess, load, low, high, plane, up, down):
+    def put(source, at, tile, index, rows, target, top):
+        lanes = slice(tile * LANES, (tile + 1) * LANES)
+        first = 24 - rows if top else 0
+        row = at + (2 * index + tile) * rows
+        target[row : row + rows, :] = source[first : first + rows, lanes]
+
     for u in range(51):
         for tile in range(2):
-            for source, row, rows in parts:
-                at = slice(row, row + rows)
-                lanes = slice(tile * LANES, (tile + 1) * LANES)
-                lane = 2 * u + tile
-                active = spread_mask(mask[at, lane : lane + 1], rows)
-                if x_ref is not None:
-                    x_ref[tile, u, at, :] = active * source[u, :, lanes]
-                if 3 <= u < 48:
-                    sa_ref[tile, u, at, :] = ALPHA * active
-                    sf_ref[tile, u, at, :] = (0.5 * active) * source[51 + u - 3, :, lanes]
-
-
-def fine_pre(own, low, high, mask, x_out, f1_out, x, sf, sa, l_ref, w_ref, t_ref, tu_ref):
+            source = x_plane(low, guess, high, u)
+            put(source, UP_AT[0], tile, u, UP_X, up, True)
+            put(source, DOWN_AT[0], tile, u, DOWN_X, down, False)
+    for u in range(45):
+        for tile in range(2):
+            source = f_plane(low, load, high, u)
+            put(source, UP_AT[1], tile, u, UP_F, up, True)
+            put(source, DOWN_AT[1], tile, u, DOWN_F, down, False)
+    at = UP_AT[2]
+    up[at : at + 14, :] = plane[10:24, 0:LANES]
+    up[at + 14 : at + 26, :] = plane[0:12, LANES:]
+    at = DOWN_AT[2]
+    down[at : at + 13, :] = plane[0:13, 0:LANES]
+    down[at + 13 : at + 25, :] = plane[0:12, LANES:]
+
+
+def fill_fine(pieces, m_ref, x_ref, sf_ref, sa_ref):
+    guess, load, low, high, up, down, plane = pieces
+    m_ref[2:16, :] = up[UP_AT[2] : UP_AT[2] + 14, :]
+    m_ref[16:40, :] = plane[:, 0:LANES]
+    m_ref[40:53, :] = down[DOWN_AT[2] : DOWN_AT[2] + 13, :]
+    for u in range(51):
+        for tile in range(2):
+            lanes = slice(tile * LANES, (tile + 1) * LANES)
+            lane = slice(2 * u + tile, 2 * u + tile + 1)
+            if x_ref is not None:
+                source = x_plane(low, guess, high, u)
+                index = 2 * u + tile
+                row = UP_AT[0] + index * UP_X
+                x_ref[tile, u, 2:16, :] = up[row : row + 14, :] * spread_mask(m_ref[2:16, lane], 14)
+                x_ref[tile, u, 16:40, :] = source[:, lanes] * spread_mask(m_ref[16:40, lane], 24)
+                row = DOWN_AT[0] + index * DOWN_X
+                x_ref[tile, u, 40:53, :] = down[row : row + 13, :] * spread_mask(
+                    m_ref[40:53, lane], 13
+                )
+            if 3 <= u < 48:
+                source = f_plane(low, load, high, u - 3)
+                index = 2 * (u - 3) + tile
+                row = UP_AT[1] + index * UP_F
+                active = spread_mask(m_ref[5:16, lane], 11)
+                sa_ref[tile, u, 5:16, :] = ALPHA * active
+                sf_ref[tile, u, 5:16, :] = (0.5 * active) * up[row : row + 11, :]
+                active = spread_mask(m_ref[16:40, lane], 24)
+                sa_ref[tile, u, 16:40, :] = ALPHA * active
+                sf_ref[tile, u, 16:40, :] = (0.5 * active) * source[:, lanes]
+                row = DOWN_AT[1] + index * DOWN_F
+                active = spread_mask(m_ref[40:50, lane], 10)
+                sa_ref[tile, u, 40:50, :] = ALPHA * active
+                sf_ref[tile, u, 40:50, :] = (0.5 * active) * down[row : row + 10, :]
+
+
+def fine_pre(
+    guess, load, low, high, up, down, plane,
+    x_out, f1_out, mask_out, x, sf, sa, l_ref, w_ref, t_ref, tu_ref, m_ref,
+):
     fill_w(w_ref, 256, 256)
-    fill_fine(own, low, high, mask, x, sf, sa)
+    fill_fine((guess, load, low, high, up, down, plane), m_ref, x, sf, sa)
+    mask_out[0:12, :] = up[UP_AT[2] + 14 : UP_AT[2] + 26, :]
+    mask_out[12:24, :] = plane[0:12, LANES:]
+    mask_out[24:36, :] = down[DOWN_AT[2] + 13 : DOWN_AT[2] + 25, :]
+    mask_out[36:40, :] = jnp.zeros((4, LANES), F32)
     sweep(x, sf, sa, l_ref, w_ref, 3, 45, 5, 48)
     sweep(x, sf, sa, l_ref, w_ref, 6, 39, 8, 48)
     sweep(x, sf, sa, l_ref, w_ref, 9, 33, 11, 48)
@@ -266,47 +348,45 @@
 
 
 def fine_post(
-    own, low, high, mask, x_own, x_low, x_high, e_own, e_low, e_high,
-    out, x, sf, sa, l_ref, w_ref, e_ref, tu_ref, z_ref,
+    guess, load, low, high, up, down, plane, x_own, x_low, x_high,
+    f1_own, f1_low, f1_high, mask1, y_own, y_low, y_high,
+    out, x, sf, sa, l_ref, w_ref, tu_ref, z_ref, m_ref, y, sf1, sa1, l1_ref, w1_ref,
 ):
     fill_w(w_ref, 256, 256)
-    fill_fine(own, low, high, mask, None, sf, sa)
-    e_ref[:, 0:8, :] = e_low[...]
-    e_ref[:, 8:20, :] = e_own[...]
-    e_ref[:, 20:28, :] = e_high[...]
+    fill_fine((guess, load, low, high, up, down, plane), m_ref, None, sf, sa)
+
+    fill_w(w1_ref, 128, 128)
+    fill_next(f1_own, f1_low, f1_high, mask1, None, sf1, sa1)
+    for u in range(30):
+        for source, row, rows in ((y_low, 4, 8), (y_own, 12, 12), (y_high, 24, 9)):
+            part = slice(row, row + rows)
+            active = spread_mask(mask1[part, u + 3 : u + 4], rows)
+            y[0, u + 3, part, :] = active * source[u]
+    sweep(y, sf1, sa1, l1_ref, w1_ref, 7, 23, 7, 32)
+
     pw = prolong_w(LANES, 256, 256)
-    position = lax.axis_index("dir")
-
-    def one(i, even):
-        u = 2 * i - 10 + (0 if even else 1)
-        coarse = i + 1
+    for u in range(-9, 33):
 
         def read(k):
-            at = coarse + k
-            place = 12 * position + at - 6
-            inside = jnp.logical_and(place >= 0, place < 48)
-            return jnp.where(inside, e_ref[at, 2:26, :], 0.0)
-
-        widen(read, even, tu_ref, z_ref, 0, 22)
+            return y[0, u // 2 + 12 + k, 6:30, :]
+
+        widen(read, u % 2 == 0, tu_ref, z_ref, 0, 22)
         fine = dot_split(z_ref[0, 0:48, :], pw)
-        at = u + UB0
         for tile in range(2):
             lanes = slice(tile * LANES, (tile + 1) * LANES)
-            x[tile, at, 6:50, :] = fine[0:44, lanes]
-
-    for i in range(22):
-        for even in (True, False):
-            u = 2 * i - 10 + (0 if even else 1)
-            if -9 <= u <= 32:
-                one(i, even)
+            x[tile, u + UB0, 6:50, :] = fine[0:44, lanes]
     for u in range(42):
         for tile in range(2):
             lanes = slice(tile * LANES, (tile + 1) * LANES)
             at = u + 5
-            for source, row, rows in ((x_low, 0, 16), (x_own, 16, 24), (x_high, 40, 16)):
+            for source, row, rows, first in (
+                (x_low, 7, 9, 7), (x_own, 16, 24, 0), (x_high, 40, 9, 0)
+            ):
                 part = slice(row, row + rows)
-                active = spread_mask(mask[part, 2 * at + tile : 2 * at + tile + 1], rows)
-                x[tile, at, part, :] = active * (x[tile, at, part, :] + source[u, :, lanes])
+                active = spread_mask(m_ref[part, 2 * at + tile : 2 * at + tile + 1], rows)
+                x[tile, at, part, :] = active * (
+                    x[tile, at, part, :] + source[u, first : first + rows, lanes]
+                )
     sweep(x, sf, sa, l_ref, w_ref, 8, 36, 10, 48)
     sweep(x, sf, sa, l_ref, w_ref, 11, 30, 13, 32)
     sweep(x, sf, sa, l_ref, w_ref, 14, 24, 16, 32)
@@ -329,45 +409,40 @@
 def next_pre(own, low, high, mask, x_out, f2_out, x, sf, sa, l_ref, w_ref, t_ref, tu_ref):
     fill_w(w_ref, 128, 128)
     fill_next(own, low, high, mask, x, sf, sa)
-    sweep(x, sf, sa, l_ref, w_ref, 4, 27, 4, 32)
-    sweep(x, sf, sa, l_ref, w_ref, 7, 21, 7, 32)
-    x_out[...] = x[0, 12:24, 12:24, :]
+    sweep(x, sf, sa, l_ref, w_ref, 3, 30, 3, 32)
+    sweep(x, sf, sa, l_ref, w_ref, 6, 24, 6, 32)
+    x_out[...] = x[0, 6:30, 6:30, :]
     rw = restrict_w(LANES, LANES, 128)
     residual(x, sf, sa, l_ref, w_ref, rw, t_ref, 4.0, 10, 15, 10, 16, 0)
     for j in range(3):
         even = narrow_plane(t_ref, tu_ref, 2 * j, 16, 6)
         odd = narrow_plane(t_ref, tu_ref, 2 * j + 1, 16, 6)
-        f2_out[6 * j : 6 * j + 6, :] = even + pltpu.roll(odd, 64, 1)
+        tu_ref[24 + 6 * j : 30 + 6 * j, :] = even + pltpu.roll(odd, 64, 1)
+    value = tu_ref[24:42, :]
+    for peer in range(64):
+        f2_out[peer] = value
 
 
 def next_post(
-    own, low, high, mask, x_own, x_low, x_high, e2,
+    own, low, high, mask, x_own, e2,
     out, x, sf, sa, l_ref, w_ref, tu_ref, z_ref,
 ):
     fill_w(w_ref, 128, 128)
     fill_next(own, low, high, mask, None, sf, sa)
-    for u in range(36):
-        for source, row in ((x_low, 0), (x_own, 12), (x_high, 24)):
-            x[0, u, row : row + 12, :] = source[u]
     pw = prolong_w(LANES, LANES, 128)
-    for u in range(-9, 21):
+    for u in range(-6, 18):
         coarse = u // 2 + 5
 
         def read(k):
             return e2[coarse + k, 0:24, :]
 
         widen(read, u % 2 == 0, tu_ref, z_ref, 0, 16)
-        first = 0.5 * (tu_ref[0:1, :] + tu_ref[1:2, :])
-        fine = dot_split(z_ref[0, 0:32, :], pw)
-        ahead = dot_split(jnp.broadcast_to(first, (16, LANES)), pw)
-        x[0, u + 12, 4:36, :] = x[0, u + 12, 4:36, :] + fine
-        x[0, u + 12, 3:4, :] = x[0, u + 12, 3:4, :] + ahead[0:1]
-    for u in range(3, 33):
-        for row in range(0, 36, 12):
+        x[0, u + 12, 4:36, :] = dot_split(z_ref[0, 0:32, :], pw)
+    for u in range(6, 30):
+        for row in (6, 18):
             at = slice(row, row + 12)
             active = spread_mask(mask[at, u : u + 1], 12)
-            x[0, u, at, :] = active * x[0, u, at, :]
-    sweep(x, sf, sa, l_ref, w_ref, 6, 24, 6, 32)
+            x[0, u, at, :] = active * (x[0, u, at, :] + x_own[u - 6, row - 6 : row + 6, :])
     sweep(x, sf, sa, l_ref, w_ref, 9, 18, 9, 32)
     sweep(x, sf, sa, l_ref, w_ref, 12, 12, 12, 16)
     out[...] = x[0, 12:24, 12:24, :]
@@ -542,6 +617,19 @@
 
 def on_device(right_side, guess, mask_fine, mask_next):
     position = lax.axis_index("dir")
+    anywhere = pl.BlockSpec(memory_space=pl.ANY)
+    vmem = pl.BlockSpec(memory_space=pltpu.VMEM)
+    up, down = pl.pallas_call(
+        pack_dir,
+        out_shape=[shape_of(25, 24, 256), shape_of(23, 24, 256)],
+        in_specs=[anywhere] * 2,
+        out_specs=[vmem] * 2,
+        scratch_shapes=[pltpu.SemaphoreType.DMA((4,))],
+    )(guess, right_side)
+    x_low = ring(up, ("dir",), 1)
+    x_high = ring(down, ("dir",), -1)
+
+    mask_fine, mask_next, up = lax.optimization_barrier((mask_fine, mask_next, up))
     fine = jnp.transpose(mask_fine, (1, 0, 2)).reshape(24, 48).astype(F32)
     following = mask_next[:, :, 0].T.astype(F32)
     plane = jnp.concatenate(
@@ -550,45 +638,42 @@
             jnp.pad(following, ((0, 12), (0, 116))),
         ],
         axis=1,
-    )[None]
-    up = jnp.concatenate([guess[10:], right_side[13:], plane], axis=0)
-    down = jnp.concatenate([guess[:13], right_side[:10], plane], axis=0)
-    low = ring(up, ("dir",), 1)
-    high = ring(down, ("dir",), -1)
-    m_low, m_high, m_own = low[25], high[23], plane[0]
-    fine = jnp.concatenate([m_low[:, 20:48], m_own[:, :48], m_high[:, :26]], axis=1)
+    )
+    m_low = ring(plane, ("dir",), 1)
+    m_high = ring(plane, ("dir",), -1)
+    fine = jnp.concatenate([m_low[:, 20:48], fine, m_high[:, :26]], axis=1)
     fine = fine * inside_lanes(24 * position - 14, 102, 2, 96)
     following = jnp.concatenate(
-        [m_low[:12, 128:140], m_own[:12, 128:140], m_high[:12, 128:140]], axis=1
+        [m_low[:12, 128:140], following, m_high[:12, 128:140]], axis=1
     )
     following = following * inside_lanes(12 * position - 12, 36, 1, 48)
     plane = jnp.concatenate(
         [
             jnp.pad(fine, ((0, 0), (0, 26))),
-            jnp.pad(following, ((12, 0), (0, 28))) + jnp.zeros((24, 64), F32),
-            jnp.pad(following, ((0, 12), (0, 28))) + jnp.zeros((24, 64), F32),
+            jnp.pad(following, ((0, 12), (0, 92))),
         ],
         axis=1,
-    )[None]
-    own = jnp.concatenate(
-        [low[:14], guess, high[:13], low[14:25], right_side, high[13:23], plane], axis=0
-    )
-    low = ring(own[:, 8:24], PATCH, 1)
-    high = ring(own[:, 0:16], PATCH, -1)
-    mask0 = jnp.concatenate([low[96, :, :128], own[96, :, :128], high[96, :, :128]], axis=0)
-    mask1 = jnp.concatenate(
-        [low[96, 4:16, 128:192], own[96, 12:24, 128:192], high[96, 0:12, 192:256]], axis=0
-    )
-    mask1 = jnp.pad(mask1, ((0, 4), (0, 64)))
+    )
+    to_up, to_down = call(
+        pack_patch,
+        [shape_of(UP_ROWS, 128), shape_of(DOWN_ROWS, 128)],
+        [],
+        (guess, right_side, x_low, x_high, plane),
+        10**6,
+    )
+    p_high = ring(to_down, PATCH, -1)
+    p_low = ring(to_up, PATCH, 1)
+    pieces = (guess, right_side, x_low, x_high, p_low, p_high, plane)
 
     window = ((2, 52, V0, LANES), F32)
     left0 = ((46, 48, 1024), BF16)
     w0 = ((1280, 256), BF16)
-    x0, f1 = call(
+    columns = ((56, LANES), F32)
+    x0, f1, mask1 = call(
         fine_pre,
-        [shape_of(24, 24, 256), shape_of(12, 12, 128)],
-        [window, window, window, left0, w0, ((28, 32, 128), F32), ((48, 128), F32)],
-        (own, low, high, mask0),
+        [shape_of(24, 24, 256), shape_of(12, 12, 128), shape_of(40, 128)],
+        [window, window, window, left0, w0, ((28, 32, 128), F32), ((48, 128), F32), columns],
+        pieces,
         10**10,
     )
 
@@ -596,11 +681,11 @@
     x0, f1_own = after(x0, f1_own)
     f1_low, f1_high = along_patch(f1_own, (0, 12), (0, 12))
     window1 = ((1, 36, 48, LANES), F32)
-    left1 = ((28, 32, 512), BF16)
+    left1 = ((30, 32, 512), BF16)
     w1 = ((640, 128), BF16)
     x1, f2 = call(
         next_pre,
-        [shape_of(12, 12, 128), shape_of(18, 128)],
+        [shape_of(24, 24, 128), shape_of(64, 18, 128)],
         [window1, window1, window1, left1, w1, ((16, 16, 128), F32), ((48, 128), F32)],
         (f1_own, f1_low, f1_high, mask1),
         10**9,
@@ -610,12 +695,9 @@
     x0_own = jnp.concatenate([x0_low, x0, x0_high], axis=0)
     x0_own, f2 = after(x0_own, f2)
     x0_low, x0_high = along_patch(x0_own, (8, 24), (0, 16))
-    x1_own = along_next(x1)
-
-    same = lax.all_to_all(jnp.broadcast_to(f2[None], (64, 18, 128)), ("pz", "dir"), 0, 0)
-    x1_own, same = after(x1_own, same)
+
+    same = lax.all_to_all(f2, ("pz", "dir"), 0, 0)
     other = lax.ppermute(same, "core", [(0, 1), (1, 0)])
-    x1_low, x1_high = along_patch(x1_own, (0, 12), (0, 12))
     (e2,) = call(
         coarse,
         [shape_of(17, 24, 128)],
@@ -635,17 +717,16 @@
         (same, other),
         4 * 10**9,
     )
-    (e1,) = call(
+    (y,) = call(
         next_post,
         [shape_of(12, 12, 128)],
         [window1, window1, window1, left1, w1, ((48, 128), F32), ((2, 48, 128), F32)],
-        (f1_own, f1_low, f1_high, mask1, x1_own, x1_low, x1_high, e2),
+        (f1_own, f1_low, f1_high, mask1, x1, e2),
         10**9,
     )
-    e1_low, e1_high = along_dir(e1, 6, 6)
-    e1_own = jnp.concatenate([e1_low, e1, e1_high], axis=0)
-    e1_low = ring(e1_own[:, 4:12], PATCH, 1)
-    e1_high = ring(e1_own[:, 0:8], PATCH, -1)
+    y_low, y_high = along_dir(y, 9, 9)
+    y_own = jnp.concatenate([y_low, y, y_high], axis=0)
+    y_low, y_high = along_patch(y_own, (4, 12), (0, 9))
     (out,) = call(
         fine_post,
         [shape_of(24, 24, 256)],
@@ -655,11 +736,17 @@
             window,
             left0,
             w0,
-            ((24, 32, 128), F32),
             ((48, 128), F32),
             ((2, 48, 128), F32),
+            columns,
+            window1,
+            window1,
+            window1,
+            left1,
+            w1,
         ],
-        (own, low, high, mask0, x0_own, x0_low, x0_high, e1_own, e1_low, e1_high),
+        pieces
+        + (x0_own, x0_low, x0_high, f1_own, f1_low, f1_high, mask1, y_own, y_low, y_high),
         10**10,
     )
     return out

time: 195 us -> 172 us (0.88)
  starting transfers between devices: 48.5 us -> 28.1 us
  blocking collectives: 0 us -> 19.4 us
  waiting for transfers between devices: 64.6 us -> 53.3 us
  local copies, waits for them, and re-layouts: 12 us -> 1.56 us
  Pallas kernels: 65.9 us -> 68.5 us
    all_to_all x0 -> x1, blocking collectives: none -> 19.4 us  [on_device(): same = lax.all_to_all(f2, ('pz', 'dir'), 0, 0)]
    ppermute x20 -> x18, starting transfers between devices: 38.8 us -> 28.1 us  [ring(): return lax.ppermute(value, axes if len(axes) > 1 else axes[0], pairs)]
    ppermute x20 -> x18, waiting for transfers between devices: 62 us -> 52.9 us  [ring(): return lax.ppermute(value, axes if len(axes) > 1 else axes[0], pairs)]
    unnamed x39 -> x4, local copies, waits for them, and re-layouts: 6.69 us -> 0.01 us
    all_to_all x1 -> x0, starting transfers between devices: 6.14 us -> none  [on_device(): lax.all_to_all(jnp.broadcast_to(f2[None], (64, 18, 128)), ('pz', 'dir'),...]
    ppermute x1, starting transfers between devices: 3.56 us -> 0.09 us  [on_device(): other = lax.ppermute(same, 'core', [(0, 1), (1, 0)])]
    all_to_all x1 -> x0, waiting for transfers between devices: 2.58 us -> none  [on_device(): lax.all_to_all(jnp.broadcast_to(f2[None], (64, 18, 128)), ('pz', 'dir'),...]
    pallas_call x0 -> x1, Pallas kernels: none -> 2.36 us  [on_device(): pl.pallas_call(pack_dir, out_shape=[shape_of(25, 24, 256), shape_of(23, 2...]
  transfers between devices with their start and end apart: 22 -> 19, of which waited for: 13 -> 11; matrix products, arithmetic and copies ran while one was open for 1% -> 0% of each run, Pallas kernels for 14% -> 14%
where the time goes in v3:
time: 172 us
  Pallas kernels  68.5 us (40%)
  waiting for transfers between devices  53.3 us (31%)
  starting transfers between devices  28.1 us (16%)
  blocking collectives  19.4 us (11%)
    pallas_call x6, Pallas kernels, call(): pl.pallas_call(body, out_shape=list(outs), in_specs=[vmem] * len(operands...  66.2 us
    ppermute x18, waiting for transfers between devices, ring(): return lax.ppermute(value, axes if len(axes) > 1 else axes[0], pairs)  52.9 us
    ppermute x18, starting transfers between devices, ring(): return lax.ppermute(value, axes if len(axes) > 1 else axes[0], pairs)  28.1 us
    all_to_all x1, blocking collectives, on_device(): same = lax.all_to_all(f2, ('pz', 'dir'), 0, 0)  19.4 us
  transfers between devices with their start and end apart: 19, of which 11 were waited for; matrix products, arithmetic and copies ran while one was open for 0% of the time, Pallas kernels for 14%

profile of v3, /device:TPU:6, one launch (start us, length us, event | category | flops | bytes accessed | tf_op | source)
XLA Modules:
  0.0 172.2 jit_solution(15640868895959524608)
XLA Ops:
  0.0 2.4 %shard_map.46 = (f32[25,24,256]{2,1,0:T(8,128)}, f32[23,24,256]{2,1,0:T(8,128)}) custom-call(f32[24,24,256]{2,1,0:T(8,128)} %guess.7, f32[24,24,256]{2,1,0:T(8,128)} %load.7), custom_call_target="tpu_custom_call" | custom-call | tf_op jit(solution)/shard_map/pallas_call | solution.py:622
  2.4 0.8 copy.11
  3.2 0.7 convert_element_type.40
  3.9 0.1 copy.10
  4.0 0.9 collective-permute-start.3
  4.9 2.4 %collective-permute-start.2 = (f32[24,256]{1,0:T(8,128)S(1)}, f32[24,256]{1,0:T(8,128)S(1)}, u32[]{:S(2)}, u32[]{:S(2)}) collective-permute-start(f32[24,256]{1,0:T(8,128)S(1)} %select_maximum_fusion.1), channel_id=1, source_target_pairs={{0,1},{1,2},{2,3},{3,0},{4,5},{5,6},{6,7},{7,4},{8,9},{9,10},{10,1... | collective-permute-start | bytes 73736 | tf_op jit(solution)/shard_map/ppermute | solution.py:588
  7.3 0.0 collective-permute-start
  7.3 2.0 %collective-permute-start.1 = (f32[23,24,256]{2,1,0:T(8,128)}, f32[23,24,256]{2,1,0:T(8,128)S(1)}, u32[]{:S(2)}, u32[]{:S(2)}) collective-permute-start(f32[23,24,256]{2,1,0:T(8,128)} %get-tuple-element.21), channel_id=1, source_target_pairs={{0,3},{1,0},{2,1},{3,2},{4,7},{5,4},{6,5},{7,6},{8,11},{9,8},{10,9... | collective-permute-start | bytes 1695752 | tf_op jit(solution)/shard_map/ppermute | solution.py:588
  9.4 0.0 collective-permute-done.2
  9.4 0.1 slice.48
  9.4 0.1 maximum_multiply_fusion.1
  9.5 0.1 maximum_multiply_fusion
  9.6 13.1 %collective-permute-done.1.high = f32[23,24,256]{2,1,0:T(8,128)S(1)} collective-permute-done((f32[23,24,256]{2,1,0:T(8,128)}, f32[23,24,256]{2,1,0:T(8,128)S(1)}, u32[]{:S(2)}, u32[]{:S(2)}) %collective-permute-start.1) | collective-permute-done | bytes 565280 | tf_op jit(solution)/shard_map/ppermute | solution.py:588
  22.7 0.2 shard_map.47
  22.9 0.1 collective-permute-start.4
  23.0 5.1 %collective-permute-start.5 = (f32[2256,128]{1,0:T(8,128)S(1)}, f32[2256,128]{1,0:T(8,128)S(1)}, u32[]{:S(2)}, u32[]{:S(2)}) collective-permute-start(f32[2256,128]{1,0:T(8,128)S(1)} %get-tuple-element.25), channel_id=1, source_target_pairs={{0,124},{4,0},{8,4},{12,8},{16,12},{20,16},{24,20},{28,24},{32,28}... | collective-permute-start | bytes 3465224 | tf_op jit(solution)/shard_map/ppermute | solution.py:588
  28.1 13.5 %collective-permute-done.5.down = f32[2256,128]{1,0:T(8,128)S(1)} collective-permute-done((f32[2256,128]{1,0:T(8,128)S(1)}, f32[2256,128]{1,0:T(8,128)S(1)}, u32[]{:S(2)}, u32[]{:S(2)}) %collective-permute-start.5) | collective-permute-done | bytes 1155104 | tf_op jit(solution)/shard_map/ppermute | solution.py:588
  41.5 1.2 collective-permute-done.4.up
  42.8 22.4 %shard_map.48 = (f32[24,24,256]{2,1,0:T(8,128)S(1)}, f32[12,12,128]{2,1,0:T(8,128)S(1)}, f32[40,128]{1,0:T(8,128)S(1)}) custom-call(f32[24,24,256]{2,1,0:T(8,128)S(1)} %copy-done, f32[24,24,256]{2,1,0:T(8,128)S(1)} %copy-done.1, f32[25,24,256]{2,1,0:T(8,128)S(1)} %collective-permute-done.low, f32[23,24,256]{2,1,0:T(8,128)S(1)} %collective-permute-done.1.high, ...), custom_call_target="tpu_custom_call" | custom-call | flops 10000000000 | bytes 22409216 | tf_op jit(solution)/shard_map/pallas_call | solution.py:568
  65.1 0.6 collective-permute-start.7
  65.7 2.7 %collective-permute-start.6 = (f32[12,12,128]{2,1,0:T(8,128)S(1)}, f32[12,12,128]{2,1,0:T(8,128)S(1)}, u32[]{:S(2)}, u32[]{:S(2)}) collective-permute-start(f32[12,12,128]{2,1,0:T(8,128)S(1)} %get-tuple-element.27), channel_id=1, source_target_pairs={{0,1},{1,2},{2,3},{3,0},{4,5},{5,6},{6,7},{7,4},{8,9},{9,10},{10,1... | collective-permute-start | bytes 221192 | tf_op jit(solution)/shard_map/ppermute | solution.py:588
  68.4 2.6 %collective-permute-done.7 = f32[12,12,128]{2,1,0:T(8,128)S(1)} collective-permute-done((f32[12,12,128]{2,1,0:T(8,128)S(1)}, f32[12,12,128]{2,1,0:T(8,128)S(1)}, u32[]{:S(2)}, u32[]{:S(2)}) %collective-permute-start.7) | collective-permute-done | bytes 73760 | tf_op jit(solution)/shard_map/ppermute | solution.py:588
  71.0 0.0 collective-permute-done.6
  71.1 3.3 %collective-permute-start.8 = (f32[9,24,256]{2,1,0:T(8,128)S(1)}, f32[9,24,256]{2,1,0:T(8,128)S(1)}, u32[]{:S(2)}, u32[]{:S(2)}) collective-permute-start(f32[9,24,256]{2,1,0:T(8,128)S(1)} %get-tuple-element.37), channel_id=1, source_target_pairs={{0,1},{1,2},{2,3},{3,0},{4,5},{5,6},{6,7},{7,4},{8,9},{9,10},{10,1... | collective-permute-start | bytes 663560 | tf_op jit(solution)/shard_map/ppermute | solution.py:588
  74.4 0.0 collective-permute-start.9
  74.4 3.6 %collective-permute-start.11 = (f32[36,12,128]{2,1,0:T(8,128)S(1)}, f32[36,12,128]{2,1,0:T(8,128)S(1)}, u32[]{:S(2)}, u32[]{:S(2)}) collective-permute-start(f32[36,12,128]{2,1,0:T(8,128)S(1)} %pad_maximum_fusion.1.own.f1_own), channel_id=1, source_target_pairs={{0,124},{4,0},{8,4},{12,8},{16,12},{20,16},{24,20},{28,24},{32,28}... | collective-permute-start | bytes 663560 | tf_op jit(solution)/shard_map/ppermute | solution.py:588
  78.1 3.5 %collective-permute-done.9 = f32[9,24,256]{2,1,0:T(8,128)S(1)} collective-permute-done((f32[9,24,256]{2,1,0:T(8,128)S(1)}, f32[9,24,256]{2,1,0:T(8,128)S(1)}, u32[]{:S(2)}, u32[]{:S(2)}) %collective-permute-start.9) | collective-permute-done | bytes 221216 | tf_op jit(solution)/shard_map/ppermute | solution.py:588
  81.5 0.1 pad_maximum_fusion.x_own
  81.6 0.7 collective-permute-done.11.high.f1_high
  82.3 5.2 %collective-permute-done.10.low.f1_low = f32[36,12,128]{2,1,0:T(8,128)S(1)} collective-permute-done((f32[36,12,128]{2,1,0:T(8,128)S(1)}, f32[36,12,128]{2,1,0:T(8,128)S(1)}, u32[]{:S(2)}, u32[]{:S(2)}) %collective-permute-start.10) | collective-permute-done | bytes 221216 | tf_op jit(solution)/shard_map/ppermute | solution.py:588
  87.5 4.1 %shard_map.49 = (f32[24,24,128]{2,1,0:T(8,128)S(1)}, f32[64,18,128]{2,1,0:T(8,128)S(1)}) custom-call(f32[36,12,128]{2,1,0:T(8,128)S(1)} %pad_maximum_fusion.1.own.f1_own, f32[36,12,128]{2,1,0:T(8,128)S(1)} %collective-permute-done.10.low.f1_low, f32[36,12,128]{2,1,0:T(8,128)S(1)} %collective-permute-done.11.high.f1_high, ...), custom_call_target="tpu_custom_call" | custom-call | flops 1000000000 | bytes 6307840 | tf_op jit(solution)/shard_map/pallas_call | solution.py:568
  91.6 19.4 %all_to_all.5.same = f32[64,18,128]{2,1,0:T(8,128)S(1)} all-to-all(f32[64,18,128]{2,1,0:T(8,128)S(1)} %get-tuple-element.34), channel_id=1, replica_groups=mesh['pz'=16,'core'=2,'dir'=4] {'pz','dir'}, dimensions={0} | all-to-all | bytes 1179648 | tf_op jit(solution)/shard_map/all_to_all | solution.py:699
  111.0 0.1 copy.13
  111.2 0.1 collective-permute-start.14
  111.2 0.1 fusion.1
  111.3 1.5 collective-permute-start.13
  112.8 0.0 collective-permute-start.12
  112.8 0.4 collective-permute-done.14
  113.2 0.4 copy.14.other
  113.6 22.4 %shard_map.50.e2 = f32[17,24,128]{2,1,0:T(8,128)S(1)} custom-call(f32[64,18,128]{2,1,0:T(8,128)S(1)} %all_to_all.5.same, f32[64,18,128]{2,1,0:T(8,128)S(1)} %copy.14.other), custom_call_target="tpu_custom_call" | custom-call | flops 4000000000 | bytes 8372224 | tf_op jit(solution)/shard_map/pallas_call | solution.py:568
  136.0 1.9 %shard_map.51 = f32[12,12,128]{2,1,0:T(8,128)S(1)} custom-call(f32[36,12,128]{2,1,0:T(8,128)S(1)} %pad_maximum_fusion.1.own.f1_own, f32[36,12,128]{2,1,0:T(8,128)S(1)} %collective-permute-done.10.low.f1_low, f32[36,12,128]{2,1,0:T(8,128)S(1)} %collective-permute-done.11.high.f1_high, f32[40,128]{1,0:T(8,128)S(1)} %get-tuple-element.30.mask.mask1, ...), custom_call_target="tpu_custom_call" | custom-call | flops 1000000000 | bytes 5554176 | tf_op jit(solution)/shard_map/pallas_call | solution.py:568
  138.0 2.4 %collective-permute-start.15 = (f32[9,12,128]{2,1,0:T(8,128)S(1)}, f32[9,12,128]{2,1,0:T(8,128)S(1)}, u32[]{:S(2)}, u32[]{:S(2)}) collective-permute-start(f32[9,12,128]{2,1,0:T(8,128)S(1)} %get-tuple-element.39), channel_id=1, source_target_pairs={{0,1},{1,2},{2,3},{3,0},{4,5},{5,6},{6,7},{7,4},{8,9},{9,10},{10,1... | collective-permute-start | bytes 165896 | tf_op jit(solution)/shard_map/ppermute | solution.py:588
  140.4 2.3 %collective-permute-done.15 = f32[9,12,128]{2,1,0:T(8,128)S(1)} collective-permute-done((f32[9,12,128]{2,1,0:T(8,128)S(1)}, f32[9,12,128]{2,1,0:T(8,128)S(1)}, u32[]{:S(2)}, u32[]{:S(2)}) %collective-permute-start.15) | collective-permute-done | bytes 55328 | tf_op jit(solution)/shard_map/ppermute | solution.py:588
  142.6 3.3 %collective-permute-done.16 = f32[9,12,128]{2,1,0:T(8,128)S(1)} collective-permute-done((f32[9,12,128]{2,1,0:T(8,128)S(1)}, f32[9,12,128]{2,1,0:T(8,128)S(1)}, u32[]{:S(2)}, u32[]{:S(2)}) %collective-permute-start.16) | collective-permute-done | bytes 55328 | tf_op jit(solution)/shard_map/ppermute | solution.py:588
  146.0 3.1 %collective-permute-start.18 = (f32[30,9,128]{2,1,0:T(8,128)S(1)}, f32[30,9,128]{2,1,0:T(8,128)S(1)}, u32[]{:S(2)}, u32[]{:S(2)}) collective-permute-start(f32[30,9,128]{2,1,0:T(8,128)S(1)} %bitcast.8), channel_id=1, source_target_pairs={{0,124},{4,0},{8,4},{12,8},{16,12},{20,16},{24,20},{28,24},{32,28}... | collective-permute-start | bytes 414728 | tf_op jit(solution)/shard_map/ppermute | solution.py:588
  149.1 0.3 collective-permute-start.17
  149.5 7.6 %collective-permute-done.17.y_low = f32[30,8,128]{2,1,0:T(8,128)S(1)} collective-permute-done((f32[30,8,128]{2,1,0:T(8,128)S(1)}, f32[30,8,128]{2,1,0:T(8,128)S(1)}, u32[]{:S(2)}, u32[]{:S(2)}) %collective-permute-start.17) | collective-permute-done | bytes 122912 | tf_op jit(solution)/shard_map/ppermute | solution.py:588
  157.1 15.1 %shard_map.52 = f32[24,24,256]{2,1,0:T(8,128)} custom-call(f32[24,24,256]{2,1,0:T(8,128)S(1)} %copy-done, f32[24,24,256]{2,1,0:T(8,128)S(1)} %copy-done.1, f32[25,24,256]{2,1,0:T(8,128)S(1)} %collective-permute-done.low, f32[23,24,256]{2,1,0:T(8,128)S(1)} %collective-permute-done.1.high, f32[2448,128]{1,0:T(8,128)S(1)} %collective-permute-done.4.up, ...), custom_call_target="tpu_custom_call" | custom-call | flops 10000000000 | bytes 30076928 | tf_op jit(solution)/shard_map/pallas_call | solution.py:568
  (25 shorter events, 0.2 us)
Async XLA Ops:
  0.0 22.7 %copy-start = (f32[24,24,256]{2,1,0:T(8,128)S(1)}, f32[24,24,256]{2,1,0:T(8,128)}, u32[]{:S(2)}) copy-start(f32[24,24,256]{2,1,0:T(8,128)} %guess.7) | copy-start | bytes 1769476
  0.0 22.7 %copy-start.1 = (f32[24,24,256]{2,1,0:T(8,128)S(1)}, f32[24,24,256]{2,1,0:T(8,128)}, u32[]{:S(2)}) copy-start(f32[24,24,256]{2,1,0:T(8,128)} %load.7) | copy-start | bytes 1769476
  4.0 5.3 %collective-permute-start.3 = (f32[24,256]{1,0:T(8,128)S(1)}, f32[24,256]{1,0:T(8,128)S(1)}, u32[]{:S(2)}, u32[]{:S(2)}) collective-permute-start(f32[24,256]{1,0:T(8,128)S(1)} %select_maximum_fusion.1), channel_id=1, source_target_pairs={{0,3},{1,0},{2,1},{3,2},{4,7},{5,4},{6,5},{7,6},{8,11},{9,8},{10,9... | collective-permute-start | bytes 73736 | tf_op jit(solution)/shard_map/ppermute | solution.py:588
  4.9 4.5 %collective-permute-start.2 = (f32[24,256]{1,0:T(8,128)S(1)}, f32[24,256]{1,0:T(8,128)S(1)}, u32[]{:S(2)}, u32[]{:S(2)}) collective-permute-start(f32[24,256]{1,0:T(8,128)S(1)} %select_maximum_fusion.1), channel_id=1, source_target_pairs={{0,1},{1,2},{2,3},{3,0},{4,5},{5,6},{6,7},{7,4},{8,9},{9,10},{10,1... | collective-permute-start | bytes 73736 | tf_op jit(solution)/shard_map/ppermute | solution.py:588
  7.3 15.4 %collective-permute-start = (f32[25,24,256]{2,1,0:T(8,128)}, f32[25,24,256]{2,1,0:T(8,128)S(1)}, u32[]{:S(2)}, u32[]{:S(2)}) collective-permute-start(f32[25,24,256]{2,1,0:T(8,128)} %get-tuple-element.20), channel_id=1, source_target_pairs={{0,1},{1,2},{2,3},{3,0},{4,5},{5,6},{6,7},{7,4},{8,9},{9,10},{10,1... | collective-permute-start | bytes 1843208 | tf_op jit(solution)/shard_map/ppermute | solution.py:588
  7.3 15.4 %collective-permute-start.1 = (f32[23,24,256]{2,1,0:T(8,128)}, f32[23,24,256]{2,1,0:T(8,128)S(1)}, u32[]{:S(2)}, u32[]{:S(2)}) collective-permute-start(f32[23,24,256]{2,1,0:T(8,128)} %get-tuple-element.21), channel_id=1, source_target_pairs={{0,3},{1,0},{2,1},{3,2},{4,7},{5,4},{6,5},{7,6},{8,11},{9,8},{10,9... | collective-permute-start | bytes 1695752 | tf_op jit(solution)/shard_map/ppermute | solution.py:588
  22.9 19.8 %collective-permute-start.4 = (f32[2448,128]{1,0:T(8,128)S(1)}, f32[2448,128]{1,0:T(8,128)S(1)}, u32[]{:S(2)}, u32[]{:S(2)}) collective-permute-start(f32[2448,128]{1,0:T(8,128)S(1)} %get-tuple-element.24), channel_id=1, source_target_pairs={{0,4},{4,8},{8,12},{12,16},{16,20},{20,24},{24,28},{28,32},{32,36}... | collective-permute-start | bytes 3760136 | tf_op jit(solution)/shard_map/ppermute | solution.py:588
  23.0 18.5 %collective-permute-start.5 = (f32[2256,128]{1,0:T(8,128)S(1)}, f32[2256,128]{1,0:T(8,128)S(1)}, u32[]{:S(2)}, u32[]{:S(2)}) collective-permute-start(f32[2256,128]{1,0:T(8,128)S(1)} %get-tuple-element.25), channel_id=1, source_target_pairs={{0,124},{4,0},{8,4},{12,8},{16,12},{20,16},{24,20},{28,24},{32,28}... | collective-permute-start | bytes 3465224 | tf_op jit(solution)/shard_map/ppermute | solution.py:588
  65.1 5.9 %collective-permute-start.7 = (f32[12,12,128]{2,1,0:T(8,128)S(1)}, f32[12,12,128]{2,1,0:T(8,128)S(1)}, u32[]{:S(2)}, u32[]{:S(2)}) collective-permute-start(f32[12,12,128]{2,1,0:T(8,128)S(1)} %get-tuple-element.27), channel_id=1, source_target_pairs={{0,3},{1,0},{2,1},{3,2},{4,7},{5,4},{6,5},{7,6},{8,11},{9,8},{10,9... | collective-permute-start | bytes 221192 | tf_op jit(solution)/shard_map/ppermute | solution.py:588
  65.7 5.3 %collective-permute-start.6 = (f32[12,12,128]{2,1,0:T(8,128)S(1)}, f32[12,12,128]{2,1,0:T(8,128)S(1)}, u32[]{:S(2)}, u32[]{:S(2)}) collective-permute-start(f32[12,12,128]{2,1,0:T(8,128)S(1)} %get-tuple-element.27), channel_id=1, source_target_pairs={{0,1},{1,2},{2,3},{3,0},{4,5},{5,6},{6,7},{7,4},{8,9},{9,10},{10,1... | collective-permute-start | bytes 221192 | tf_op jit(solution)/shard_map/ppermute | solution.py:588
  71.1 7.0 %collective-permute-start.8 = (f32[9,24,256]{2,1,0:T(8,128)S(1)}, f32[9,24,256]{2,1,0:T(8,128)S(1)}, u32[]{:S(2)}, u32[]{:S(2)}) collective-permute-start(f32[9,24,256]{2,1,0:T(8,128)S(1)} %get-tuple-element.37), channel_id=1, source_target_pairs={{0,1},{1,2},{2,3},{3,0},{4,5},{5,6},{6,7},{7,4},{8,9},{9,10},{10,1... | collective-permute-start | bytes 663560 | tf_op jit(solution)/shard_map/ppermute | solution.py:588
  74.4 7.1 %collective-permute-start.9 = (f32[9,24,256]{2,1,0:T(8,128)S(1)}, f32[9,24,256]{2,1,0:T(8,128)S(1)}, u32[]{:S(2)}, u32[]{:S(2)}) collective-permute-start(f32[9,24,256]{2,1,0:T(8,128)S(1)} %get-tuple-element.38), channel_id=1, source_target_pairs={{0,3},{1,0},{2,1},{3,2},{4,7},{5,4},{6,5},{7,6},{8,11},{9,8},{10,9... | collective-permute-start | bytes 663560 | tf_op jit(solution)/shard_map/ppermute | solution.py:588
  74.4 7.9 %collective-permute-start.11 = (f32[36,12,128]{2,1,0:T(8,128)S(1)}, f32[36,12,128]{2,1,0:T(8,128)S(1)}, u32[]{:S(2)}, u32[]{:S(2)}) collective-permute-start(f32[36,12,128]{2,1,0:T(8,128)S(1)} %pad_maximum_fusion.1.own.f1_own), channel_id=1, source_target_pairs={{0,124},{4,0},{8,4},{12,8},{16,12},{20,16},{24,20},{28,24},{32,28}... | collective-permute-start | bytes 663560 | tf_op jit(solution)/shard_map/ppermute | solution.py:588
  78.0 9.5 %collective-permute-start.10 = (f32[36,12,128]{2,1,0:T(8,128)S(1)}, f32[36,12,128]{2,1,0:T(8,128)S(1)}, u32[]{:S(2)}, u32[]{:S(2)}) collective-permute-start(f32[36,12,128]{2,1,0:T(8,128)S(1)} %pad_maximum_fusion.1.own.f1_own), channel_id=1, source_target_pairs={{0,4},{4,8},{8,12},{12,16},{16,20},{20,24},{24,28},{28,32},{32,36}... | collective-permute-start | bytes 663560 | tf_op jit(solution)/shard_map/ppermute | solution.py:588
  111.2 2.1 %collective-permute-start.14 = (f32[64,18,128]{2,0,1:T(8,128)S(1)}, f32[64,18,128]{2,0,1:T(8,128)S(1)}, u32[]{:S(2)}, u32[]{:S(2)}) collective-permute-start(f32[64,18,128]{2,0,1:T(8,128)S(1)} %copy.13), channel_id=1, source_target_pairs={{0,4},{4,0},{1,5},{5,1},{2,6},{6,2},{3,7},{7,3},{8,12},{12,8},{9,1... | collective-permute-start | bytes 1769480 | tf_op jit(solution)/shard_map/ppermute | solution.py:700
  111.3 38.1 %collective-permute-start.13 = (f32[42,16,256]{2,1,0:T(8,128)S(1)}, f32[42,16,256]{2,1,0:T(8,128)S(1)}, u32[]{:S(2)}, u32[]{:S(2)}) collective-permute-start(f32[42,16,256]{2,1,0:T(8,128)S(1)} %get-tuple-element.35), channel_id=1, source_target_pairs={{0,124},{4,0},{8,4},{12,8},{16,12},{20,16},{24,20},{28,24},{32,28}... | collective-permute-start | bytes 2064392 | tf_op jit(solution)/shard_map/ppermute | solution.py:588
  112.8 36.7 %collective-permute-start.12 = (f32[42,16,256]{2,1,0:T(8,128)S(1)}, f32[42,16,256]{2,1,0:T(8,128)S(1)}, u32[]{:S(2)}, u32[]{:S(2)}) collective-permute-start(f32[42,16,256]{2,1,0:T(8,128)S(1)} %get-tuple-element.36), channel_id=1, source_target_pairs={{0,4},{4,8},{8,12},{12,16},{16,20},{20,24},{24,28},{28,32},{32,36}... | collective-permute-start | bytes 2064392 | tf_op jit(solution)/shard_map/ppermute | solution.py:588
  138.0 4.7 %collective-permute-start.15 = (f32[9,12,128]{2,1,0:T(8,128)S(1)}, f32[9,12,128]{2,1,0:T(8,128)S(1)}, u32[]{:S(2)}, u32[]{:S(2)}) collective-permute-start(f32[9,12,128]{2,1,0:T(8,128)S(1)} %get-tuple-element.39), channel_id=1, source_target_pairs={{0,1},{1,2},{2,3},{3,0},{4,5},{5,6},{6,7},{7,4},{8,9},{9,10},{10,1... | collective-permute-start | bytes 165896 | tf_op jit(solution)/shard_map/ppermute | solution.py:588
  140.4 5.6 %collective-permute-start.16 = (f32[9,12,128]{2,1,0:T(8,128)S(1)}, f32[9,12,128]{2,1,0:T(8,128)S(1)}, u32[]{:S(2)}, u32[]{:S(2)}) collective-permute-start(f32[9,12,128]{2,1,0:T(8,128)S(1)} %get-tuple-element.40), channel_id=1, source_target_pairs={{0,3},{1,0},{2,1},{3,2},{4,7},{5,4},{6,5},{7,6},{8,11},{9,8},{10,9... | collective-permute-start | bytes 165896 | tf_op jit(solution)/shard_map/ppermute | solution.py:588
  146.0 11.1 %collective-permute-start.18 = (f32[30,9,128]{2,1,0:T(8,128)S(1)}, f32[30,9,128]{2,1,0:T(8,128)S(1)}, u32[]{:S(2)}, u32[]{:S(2)}) collective-permute-start(f32[30,9,128]{2,1,0:T(8,128)S(1)} %bitcast.8), channel_id=1, source_target_pairs={{0,124},{4,0},{8,4},{12,8},{16,12},{20,16},{24,20},{28,24},{32,28}... | collective-permute-start | bytes 414728 | tf_op jit(solution)/shard_map/ppermute | solution.py:588
  149.1 8.0 %collective-permute-start.17 = (f32[30,8,128]{2,1,0:T(8,128)S(1)}, f32[30,8,128]{2,1,0:T(8,128)S(1)}, u32[]{:S(2)}, u32[]{:S(2)}) collective-permute-start(f32[30,8,128]{2,1,0:T(8,128)S(1)} %slice.54), channel_id=1, source_target_pairs={{0,4},{4,8},{8,12},{12,16},{16,20},{20,24},{24,28},{28,32},{32,36}... | collective-permute-start | bytes 368648 | tf_op jit(solution)/shard_map/ppermute | solution.py:588

commit v4 on v3

--- a/solution.py
+++ b/solution.py
@@ -235,106 +235,109 @@
 UB0, VB0, V0 = 14, 16, 64
 
 UP_X, UP_F, DOWN_X, DOWN_F = 14, 11, 13, 10
-UP_AT = (0, 102 * UP_X, 102 * UP_X + 90 * UP_F)
-DOWN_AT = (0, 102 * DOWN_X, 102 * DOWN_X + 90 * DOWN_F)
-UP_ROWS = 2448
-DOWN_ROWS = 2256
-
-
-def pack_dir(guess, load, up, down, sems):
-    copies = [
-        pltpu.make_async_copy(guess.at[10:24], up.at[0:14], sems.at[0]),
-        pltpu.make_async_copy(load.at[13:24], up.at[14:25], sems.at[1]),
-        pltpu.make_async_copy(guess.at[0:13], down.at[0:13], sems.at[2]),
-        pltpu.make_async_copy(load.at[0:10], down.at[13:23], sems.at[3]),
-    ]
-    for copy in copies:
-        copy.start()
-    for copy in copies:
-        copy.wait()
-
-
-def x_plane(low, guess, high, u):
-    if u < 14:
-        return low.at[u]
-    return guess.at[u - 14] if u < 38 else high.at[u - 38]
-
-
-def f_plane(low, load, high, u):
-    if u < 11:
-        return low.at[14 + u]
-    return load.at[u - 11] if u < 35 else high.at[13 + u - 35]
-
-
-def pack_patch(guess, load, low, high, plane, up, down):
-    def put(source, at, tile, index, rows, target, top):
+OWN_UP, OWN_DOWN = 48 * (UP_X + UP_F), 48 * (DOWN_X + DOWN_F)
+UP_MASK = 54 * UP_X + 42 * UP_F
+DOWN_MASK = 54 * DOWN_X + 42 * DOWN_F
+OUTER_UP, OUTER_DOWN = 1248, 1152
+
+
+def put_plane(source, index, at, rows, target, top):
+    for tile in range(2):
         lanes = slice(tile * LANES, (tile + 1) * LANES)
         first = 24 - rows if top else 0
         row = at + (2 * index + tile) * rows
         target[row : row + rows, :] = source[first : first + rows, lanes]
 
+
+def pack_own(guess, load, plane, up, down, to_up, to_down):
+    up[0:14] = guess[10:24]
+    up[14:25] = load[13:24]
+    up[25] = plane[...]
+    down[0:13] = guess[0:13]
+    down[13:23] = load[0:10]
+    down[23] = plane[...]
+    for u in range(24):
+        put_plane(guess.at[u], u, 0, UP_X, to_up, True)
+        put_plane(guess.at[u], u, 0, DOWN_X, to_down, False)
+        put_plane(load.at[u], u, 48 * UP_X, UP_F, to_up, True)
+        put_plane(load.at[u], u, 48 * DOWN_X, DOWN_F, to_down, False)
+
+
+def pack_outer(low, high, plane, to_up, to_down):
+    for u in range(27):
+        source = low.at[u] if u < 14 else high.at[u - 14]
+        put_plane(source, u, 0, UP_X, to_up, True)
+        put_plane(source, u, 0, DOWN_X, to_down, False)
+    for u in range(21):
+        source = low.at[14 + u] if u < 11 else high.at[13 + u - 11]
+        put_plane(source, u, 54 * UP_X, UP_F, to_up, True)
+        put_plane(source, u, 54 * DOWN_X, DOWN_F, to_down, False)
+    at = UP_MASK
+    to_up[at : at + 14, :] = plane[10:24, 0:LANES]
+    to_up[at + 14 : at + 26, :] = plane[0:12, LANES:]
+    at = DOWN_MASK
+    to_down[at : at + 13, :] = plane[0:13, 0:LANES]
+    to_down[at + 13 : at + 25, :] = plane[0:12, LANES:]
+
+
+def x_pieces(pieces, u, tile):
+    guess, _, low, high, own_up, own_down, up, down, _ = pieces
+    lanes = slice(tile * LANES, (tile + 1) * LANES)
+    if 14 <= u < 38:
+        centre, below, above, index = guess.at[u - 14], own_up, own_down, u - 14
+    else:
+        centre = low.at[u] if u < 14 else high.at[u - 38]
+        below, above, index = up, down, u if u < 14 else u - 24
+    row, line = (2 * index + tile) * UP_X, (2 * index + tile) * DOWN_X
+    return below[row : row + UP_X, :], centre[:, lanes], above[line : line + DOWN_X, :]
+
+
+def f_pieces(pieces, u, tile):
+    _, load, low, high, own_up, own_down, up, down, _ = pieces
+    lanes = slice(tile * LANES, (tile + 1) * LANES)
+    if 11 <= u < 35:
+        centre, below, above, index = load.at[u - 11], own_up, own_down, u - 11
+        first, start = 48 * UP_X, 48 * DOWN_X
+    else:
+        centre = low.at[14 + u] if u < 11 else high.at[13 + u - 35]
+        below, above, index = up, down, u if u < 11 else u - 24
+        first, start = 54 * UP_X, 54 * DOWN_X
+    row = first + (2 * index + tile) * UP_F
+    line = start + (2 * index + tile) * DOWN_F
+    return below[row : row + UP_F, :], centre[:, lanes], above[line : line + DOWN_F, :]
+
+
+def fill_fine(pieces, m_ref, x_ref, sf_ref, sa_ref):
+    up, down, plane = pieces[6:]
+    m_ref[2:16, :] = up[UP_MASK : UP_MASK + 14, :]
+    m_ref[16:40, :] = plane[:, 0:LANES]
+    m_ref[40:53, :] = down[DOWN_MASK : DOWN_MASK + 13, :]
     for u in range(51):
         for tile in range(2):
-            source = x_plane(low, guess, high, u)
-            put(source, UP_AT[0], tile, u, UP_X, up, True)
-            put(source, DOWN_AT[0], tile, u, DOWN_X, down, False)
-    for u in range(45):
-        for tile in range(2):
-            source = f_plane(low, load, high, u)
-            put(source, UP_AT[1], tile, u, UP_F, up, True)
-            put(source, DOWN_AT[1], tile, u, DOWN_F, down, False)
-    at = UP_AT[2]
-    up[at : at + 14, :] = plane[10:24, 0:LANES]
-    up[at + 14 : at + 26, :] = plane[0:12, LANES:]
-    at = DOWN_AT[2]
-    down[at : at + 13, :] = plane[0:13, 0:LANES]
-    down[at + 13 : at + 25, :] = plane[0:12, LANES:]
-
-
-def fill_fine(pieces, m_ref, x_ref, sf_ref, sa_ref):
-    guess, load, low, high, up, down, plane = pieces
-    m_ref[2:16, :] = up[UP_AT[2] : UP_AT[2] + 14, :]
-    m_ref[16:40, :] = plane[:, 0:LANES]
-    m_ref[40:53, :] = down[DOWN_AT[2] : DOWN_AT[2] + 13, :]
-    for u in range(51):
-        for tile in range(2):
-            lanes = slice(tile * LANES, (tile + 1) * LANES)
             lane = slice(2 * u + tile, 2 * u + tile + 1)
             if x_ref is not None:
-                source = x_plane(low, guess, high, u)
-                index = 2 * u + tile
-                row = UP_AT[0] + index * UP_X
-                x_ref[tile, u, 2:16, :] = up[row : row + 14, :] * spread_mask(m_ref[2:16, lane], 14)
-                x_ref[tile, u, 16:40, :] = source[:, lanes] * spread_mask(m_ref[16:40, lane], 24)
-                row = DOWN_AT[0] + index * DOWN_X
-                x_ref[tile, u, 40:53, :] = down[row : row + 13, :] * spread_mask(
-                    m_ref[40:53, lane], 13
-                )
+                ranges = ((2, 16), (16, 40), (40, 53))
+                for (first, last), value in zip(ranges, x_pieces(pieces, u, tile)):
+                    active = spread_mask(m_ref[first:last, lane], last - first)
+                    x_ref[tile, u, first:last, :] = active * value
             if 3 <= u < 48:
-                source = f_plane(low, load, high, u - 3)
-                index = 2 * (u - 3) + tile
-                row = UP_AT[1] + index * UP_F
-                active = spread_mask(m_ref[5:16, lane], 11)
-                sa_ref[tile, u, 5:16, :] = ALPHA * active
-                sf_ref[tile, u, 5:16, :] = (0.5 * active) * up[row : row + 11, :]
-                active = spread_mask(m_ref[16:40, lane], 24)
-                sa_ref[tile, u, 16:40, :] = ALPHA * active
-                sf_ref[tile, u, 16:40, :] = (0.5 * active) * source[:, lanes]
-                row = DOWN_AT[1] + index * DOWN_F
-                active = spread_mask(m_ref[40:50, lane], 10)
-                sa_ref[tile, u, 40:50, :] = ALPHA * active
-                sf_ref[tile, u, 40:50, :] = (0.5 * active) * down[row : row + 10, :]
+                ranges = ((5, 16), (16, 40), (40, 50))
+                for (first, last), value in zip(ranges, f_pieces(pieces, u - 3, tile)):
+                    active = spread_mask(m_ref[first:last, lane], last - first)
+                    sa_ref[tile, u, first:last, :] = ALPHA * active
+                    sf_ref[tile, u, first:last, :] = (0.5 * active) * value
 
 
 def fine_pre(
-    guess, load, low, high, up, down, plane,
+    guess, load, low, high, own_up, own_down, up, down, plane,
     x_out, f1_out, mask_out, x, sf, sa, l_ref, w_ref, t_ref, tu_ref, m_ref,
 ):
     fill_w(w_ref, 256, 256)
-    fill_fine((guess, load, low, high, up, down, plane), m_ref, x, sf, sa)
-    mask_out[0:12, :] = up[UP_AT[2] + 14 : UP_AT[2] + 26, :]
+    pieces = (guess, load, low, high, own_up, own_down, up, down, plane)
+    fill_fine(pieces, m_ref, x, sf, sa)
+    mask_out[0:12, :] = up[UP_MASK + 14 : UP_MASK + 26, :]
     mask_out[12:24, :] = plane[0:12, LANES:]
-    mask_out[24:36, :] = down[DOWN_AT[2] + 13 : DOWN_AT[2] + 25, :]
+    mask_out[24:36, :] = down[DOWN_MASK + 13 : DOWN_MASK + 25, :]
     mask_out[36:40, :] = jnp.zeros((4, LANES), F32)
     sweep(x, sf, sa, l_ref, w_ref, 3, 45, 5, 48)
     sweep(x, sf, sa, l_ref, w_ref, 6, 39, 8, 48)
@@ -348,14 +351,15 @@
 
 
 def fine_post(
-    guess, load, low, high, up, down, plane, x_own, x_low, x_high,
-    f1_own, f1_low, f1_high, mask1, y_own, y_low, y_high,
+    guess, load, low, high, own_up, own_down, up, down, plane,
+    x_own, x_low, x_high, f1_own, f1_low, f1_high, mask1, y_own, y_low, y_high,
     out, x, sf, sa, l_ref, w_ref, tu_ref, z_ref, m_ref, y, sf1, sa1, l1_ref, w1_ref,
 ):
     fill_w(w_ref, 256, 256)
-    fill_fine((guess, load, low, high, up, down, plane), m_ref, None, sf, sa)
-
     fill_w(w1_ref, 128, 128)
+    pieces = (guess, load, low, high, own_up, own_down, up, down, plane)
+    fill_fine(pieces, m_ref, None, sf, sa)
+
     fill_next(f1_own, f1_low, f1_high, mask1, None, sf1, sa1)
     for u in range(30):
         for source, row, rows in ((y_low, 4, 8), (y_own, 12, 12), (y_high, 24, 9)):
@@ -448,7 +452,9 @@
     out[...] = x[0, 12:24, 12:24, :]
 
 
-def coarse(same, other, e_out, x, sf, l_ref, w_ref, t_ref, tu_ref, x3, sf3, w3_ref, b_ref, z_ref):
+def coarse(
+    same, other, e_out, x, sf, l_ref, w_ref, t_ref, tu_ref, x3, sf3, w3_ref, b_ref, z_ref
+):
     fill_w(w_ref, 128, 64, True)
     fill_w(w3_ref, 128, 32, True)
     pair, core = lax.axis_index("pz"), lax.axis_index("core")
@@ -479,11 +485,11 @@
     def smooth(u0, nu, values, loads, factors, v0, nv):
         sweep(values, loads, ALPHA, l_ref, factors, u0, nu, v0, nv, stencil_pairs)
 
-    smooth(2, 12, x, sf, w_ref, 6, 128)
-    smooth(2, 12, x, sf, w_ref, 9, 112)
+    smooth(2, 12, x, sf, w_ref, 8, 112)
+    smooth(2, 12, x, sf, w_ref, 11, 112)
     rw = restrict_w(LANES, LANES, 64, True)
     residual(
-        x, sf, ALPHA, l_ref, w_ref, rw, t_ref, 8.0, 2, 12, 12, 112, 1, stencil_pairs
+        x, sf, ALPHA, l_ref, w_ref, rw, t_ref, 8.0, 2, 12, 14, 112, 1, stencil_pairs
     )
 
     for edge in (0, 1, 8, 9):
@@ -502,17 +508,17 @@
             )
             parts.append(value + pltpu.roll(value, 64, 1))
         tu_ref[0:112, :] = jnp.where(low_half(112), parts[0], parts[1])
-        at = [tu_ref[pl.ds(i, 50, stride=2), :] for i in range(5)]
+        at = [tu_ref[pl.ds(i, 48, stride=2), :] for i in range(5)]
         value = 0.0625 * (0.125 * (at[0] + at[4]) + 0.5 * (at[1] + at[3]) + 0.75 * at[2])
-        x3[0, m + 2, 3:53, :] = value
-        sf3[0, m + 2, 3:53, :] = value
+        x3[0, m + 2, 4:52, :] = value
+        sf3[0, m + 2, 4:52, :] = value
 
     lax.fori_loop(0, 6, narrow, None)
-    smooth(2, 6, x3, sf3, w3_ref, 6, 48)
-    smooth(2, 6, x3, sf3, w3_ref, 9, 48)
-    smooth(2, 6, x3, sf3, w3_ref, 12, 32)
-    smooth(2, 6, x3, sf3, w3_ref, 15, 32)
-    smooth(2, 6, x3, sf3, w3_ref, 18, 32)
+    smooth(2, 6, x3, sf3, w3_ref, 7, 48)
+    smooth(2, 6, x3, sf3, w3_ref, 10, 48)
+    smooth(2, 6, x3, sf3, w3_ref, 13, 32)
+    smooth(2, 6, x3, sf3, w3_ref, 16, 32)
+    smooth(2, 6, x3, sf3, w3_ref, 19, 32)
 
     pw = prolong_w(LANES, LANES, 64, True)
     for edge in (0, 13):
@@ -536,9 +542,9 @@
         x[at] = x[at] + fine
 
     lax.fori_loop(0, 12, wide, None)
-    smooth(2, 12, x, sf, w_ref, 49, 32)
-    smooth(2, 12, x, sf, w_ref, 52, 32)
-    smooth(2, 12, x, sf, w_ref, 55, 32)
+    smooth(2, 12, x, sf, w_ref, 50, 32)
+    smooth(2, 12, x, sf, w_ref, 53, 32)
+    smooth(2, 12, x, sf, w_ref, 56, 16)
 
     for k in range(17):
         index = 3 * position + (k - 5) // 2
@@ -617,19 +623,6 @@
 
 def on_device(right_side, guess, mask_fine, mask_next):
     position = lax.axis_index("dir")
-    anywhere = pl.BlockSpec(memory_space=pl.ANY)
-    vmem = pl.BlockSpec(memory_space=pltpu.VMEM)
-    up, down = pl.pallas_call(
-        pack_dir,
-        out_shape=[shape_of(25, 24, 256), shape_of(23, 24, 256)],
-        in_specs=[anywhere] * 2,
-        out_specs=[vmem] * 2,
-        scratch_shapes=[pltpu.SemaphoreType.DMA((4,))],
-    )(guess, right_side)
-    x_low = ring(up, ("dir",), 1)
-    x_high = ring(down, ("dir",), -1)
-
-    mask_fine, mask_next, up = lax.optimization_barrier((mask_fine, mask_next, up))
     fine = jnp.transpose(mask_fine, (1, 0, 2)).reshape(24, 48).astype(F32)
     following = mask_next[:, :, 0].T.astype(F32)
     plane = jnp.concatenate(
@@ -639,8 +632,24 @@
         ],
         axis=1,
     )
-    m_low = ring(plane, ("dir",), 1)
-    m_high = ring(plane, ("dir",), -1)
+    up, down, to_up, to_down = call(
+        pack_own,
+        [
+            shape_of(26, 24, 256),
+            shape_of(24, 24, 256),
+            shape_of(OWN_UP, 128),
+            shape_of(OWN_DOWN, 128),
+        ],
+        [],
+        (guess, right_side, plane),
+        10**6,
+    )
+    x_low = ring(up, ("dir",), 1)
+    x_high = ring(down, ("dir",), -1)
+    own_down = ring(to_down, PATCH, -1)
+    own_up = ring(to_up, PATCH, 1)
+    x_low, x_high, own_up, own_down = lax.optimization_barrier((x_low, x_high, own_up, own_down))
+    m_low, m_high = x_low[25], x_high[23]
     fine = jnp.concatenate([m_low[:, 20:48], fine, m_high[:, :26]], axis=1)
     fine = fine * inside_lanes(24 * position - 14, 102, 2, 96)
     following = jnp.concatenate(
@@ -655,19 +664,20 @@
         axis=1,
     )
     to_up, to_down = call(
-        pack_patch,
-        [shape_of(UP_ROWS, 128), shape_of(DOWN_ROWS, 128)],
+        pack_outer,
+        [shape_of(OUTER_UP, 128), shape_of(OUTER_DOWN, 128)],
         [],
-        (guess, right_side, x_low, x_high, plane),
+        (x_low, x_high, plane),
         10**6,
     )
     p_high = ring(to_down, PATCH, -1)
     p_low = ring(to_up, PATCH, 1)
-    pieces = (guess, right_side, x_low, x_high, p_low, p_high, plane)
+    pieces = (guess, right_side, x_low, x_high, own_up, own_down, p_low, p_high, plane)
 
     window = ((2, 52, V0, LANES), F32)
+    w0 = ((1280, 256), BF16)
+    w1 = ((640, 128), BF16)
     left0 = ((46, 48, 1024), BF16)
-    w0 = ((1280, 256), BF16)
     columns = ((56, LANES), F32)
     x0, f1, mask1 = call(
         fine_pre,
@@ -678,11 +688,11 @@
     )
 
     f1_own = along_next(f1)
-    x0, f1_own = after(x0, f1_own)
     f1_low, f1_high = along_patch(f1_own, (0, 12), (0, 12))
+    x0, f1_low = after(x0, f1_low)
+    x0_low, x0_high = along_dir(x0, 9, 9)
     window1 = ((1, 36, 48, LANES), F32)
     left1 = ((30, 32, 512), BF16)
-    w1 = ((640, 128), BF16)
     x1, f2 = call(
         next_pre,
         [shape_of(24, 24, 128), shape_of(64, 18, 128)],
@@ -691,11 +701,9 @@
         10**9,
     )
 
-    x0_low, x0_high = along_dir(x0, 9, 9)
     x0_own = jnp.concatenate([x0_low, x0, x0_high], axis=0)
     x0_own, f2 = after(x0_own, f2)
     x0_low, x0_high = along_patch(x0_own, (8, 24), (0, 16))
-
     same = lax.all_to_all(f2, ("pz", "dir"), 0, 0)
     other = lax.ppermute(same, "core", [(0, 1), (1, 0)])
     (e2,) = call(

time: 172 us -> 165 us (0.959)
  waiting for transfers between devices: 53.3 us -> 41.4 us
  local copies, waits for them, and re-layouts: 1.56 us -> 3.73 us
    ppermute x18, waiting for transfers between devices: 52.9 us -> 41 us  [ring(): return lax.ppermute(value, axes if len(axes) > 1 else axes[0], pairs)]
    unnamed x4 -> x13, local copies, waits for them, and re-layouts: 0.01 us -> 2.95 us
    pallas_call x1 -> x0, Pallas kernels: 2.36 us -> none  [on_device(): pl.pallas_call(pack_dir, out_shape=[shape_of(25, 24, 256), shape_of(23, 2...]
    pallas_call x6 -> x7, Pallas kernels: 66.2 us -> 68.5 us  [call(): pl.pallas_call(body, out_shape=list(outs), in_specs=[vmem] * len(operands...]
  transfers between devices with their start and end apart: 19 -> 19, of which waited for: 11 -> 12; matrix products, arithmetic and copies ran while one was open for 0% -> 0% of each run, Pallas kernels for 14% -> 17%
where the time goes in v4:
time: 165 us; the launch traced here: 164 us
  Pallas kernels  68.5 us (42%)
  waiting for transfers between devices  41.4 us (25%)
  starting transfers between devices  29.3 us (18%)
  blocking collectives  20.9 us (13%)
  local copies, waits for them, and re-layouts  3.73 us (2%)
    pallas_call x7, Pallas kernels, call(): pl.pallas_call(body, out_shape=list(outs), in_specs=[vmem] * len(operands...  68.5 us
    ppermute x18, waiting for transfers between devices, ring(): return lax.ppermute(value, axes if len(axes) > 1 else axes[0], pairs)  41 us
    ppermute x18, starting transfers between devices, ring(): return lax.ppermute(value, axes if len(axes) > 1 else axes[0], pairs)  29.2 us
    all_to_all x1, blocking collectives, on_device(): same = lax.all_to_all(f2, ('pz', 'dir'), 0, 0)  20.9 us
  transfers between devices with their start and end apart: 19, of which 12 were waited for; matrix products, arithmetic and copies ran while one was open for 0% of the time, Pallas kernels for 17%

profile of v4, /device:TPU:6, one launch (start us, length us, event | category | flops | bytes accessed | tf_op | source)
XLA Modules:
  0.0 164.3 jit_solution(13886695660344482561)
XLA Ops:
  0.0 0.8 copy.11
  0.8 0.1 copy.10
  0.9 1.1 copy-done
  2.0 1.1 copy-done.2
  3.0 1.2 shard_map.46
  4.2 0.4 collective-permute-start
  4.6 1.6 collective-permute-start.1
  6.2 5.4 %collective-permute-start.3 = (f32[1104,128]{1,0:T(8,128)}, f32[1104,128]{1,0:T(8,128)}, u32[]{:S(2)}, u32[]{:S(2)}) collective-permute-start(f32[1104,128]{1,0:T(8,128)} %get-tuple-element.27), channel_id=1, source_target_pairs={{0,124},{4,0},{8,4},{12,8},{16,12},{20,16},{24,20},{28,24},{32,28}... | collective-permute-start | bytes 1695752 | tf_op jit(solution)/shard_map/ppermute | solution.py:594
  11.6 7.4 %collective-permute-done.3.own_down = f32[1104,128]{1,0:T(8,128)} collective-permute-done((f32[1104,128]{1,0:T(8,128)}, f32[1104,128]{1,0:T(8,128)}, u32[]{:S(2)}, u32[]{:S(2)}) %collective-permute-start.3) | collective-permute-done | bytes 565280 | tf_op jit(solution)/shard_map/ppermute | solution.py:594
  19.1 2.4 %collective-permute-done.1.high = f32[24,24,256]{2,1,0:T(8,128)S(1)} collective-permute-done((f32[24,24,256]{2,1,0:T(8,128)}, f32[24,24,256]{2,1,0:T(8,128)S(1)}, u32[]{:S(2)}, u32[]{:S(2)}) %collective-permute-start.1) | collective-permute-done | bytes 589856 | tf_op jit(solution)/shard_map/ppermute | solution.py:594
  21.5 0.1 slice.56
  21.6 0.1 maximum_multiply_fusion.1
  21.7 0.1 maximum_multiply_fusion
  21.8 0.0 copy-start.3
  21.8 0.1 shard_map.47
  21.9 0.7 collective-permute-start.4
  22.5 4.5 %collective-permute-start.5 = (f32[1152,128]{1,0:T(8,128)S(1)}, f32[1152,128]{1,0:T(8,128)S(1)}, u32[]{:S(2)}, u32[]{:S(2)}) collective-permute-start(f32[1152,128]{1,0:T(8,128)S(1)} %get-tuple-element.33), channel_id=1, source_target_pairs={{0,124},{4,0},{8,4},{12,8},{16,12},{20,16},{24,20},{28,24},{32,28}... | collective-permute-start | bytes 1769480 | tf_op jit(solution)/shard_map/ppermute | solution.py:594
  27.0 7.4 %collective-permute-done.5.down = f32[1152,128]{1,0:T(8,128)S(1)} collective-permute-done((f32[1152,128]{1,0:T(8,128)S(1)}, f32[1152,128]{1,0:T(8,128)S(1)}, u32[]{:S(2)}, u32[]{:S(2)}) %collective-permute-start.5) | collective-permute-done | bytes 589856 | tf_op jit(solution)/shard_map/ppermute | solution.py:594
  34.4 0.7 collective-permute-done.4.up
  35.1 23.4 %shard_map.48 = (f32[24,24,256]{2,1,0:T(8,128)S(1)}, f32[12,12,128]{2,1,0:T(8,128)S(1)}, f32[40,128]{1,0:T(8,128)S(1)}) custom-call(f32[24,24,256]{2,1,0:T(8,128)S(1)} %copy-done.1, f32[24,24,256]{2,1,0:T(8,128)S(1)} %copy-done.3, f32[26,24,256]{2,1,0:T(8,128)S(1)} %collective-permute-done.low, f32[24,24,256]{2,1,0:T(8,128)S(1)} %collective-permute-done.1.high, ...), custom_call_target="tpu_custom_call" | custom-call | flops 10000000000 | bytes 22474752 | tf_op jit(solution)/shard_map/pallas_call | solution.py:574
  58.5 0.6 collective-permute-start.6
  59.1 1.5 collective-permute-start.7
  60.6 2.6 %collective-permute-done.6 = f32[12,12,128]{2,1,0:T(8,128)S(1)} collective-permute-done((f32[12,12,128]{2,1,0:T(8,128)S(1)}, f32[12,12,128]{2,1,0:T(8,128)S(1)}, u32[]{:S(2)}, u32[]{:S(2)}) %collective-permute-start.6) | collective-permute-done | bytes 73760 | tf_op jit(solution)/shard_map/ppermute | solution.py:594
  63.2 1.7 %collective-permute-done.7 = f32[12,12,128]{2,1,0:T(8,128)S(1)} collective-permute-done((f32[12,12,128]{2,1,0:T(8,128)S(1)}, f32[12,12,128]{2,1,0:T(8,128)S(1)}, u32[]{:S(2)}, u32[]{:S(2)}) %collective-permute-start.7) | collective-permute-done | bytes 73760 | tf_op jit(solution)/shard_map/ppermute | solution.py:594
  65.0 0.1 collective-permute-start.8
  65.1 5.1 %collective-permute-start.11 = (f32[36,12,128]{2,1,0:T(8,128)S(1)}, f32[36,12,128]{2,1,0:T(8,128)S(1)}, u32[]{:S(2)}, u32[]{:S(2)}) collective-permute-start(f32[36,12,128]{2,1,0:T(8,128)S(1)} %constant_dynamic-update-slice_fusion.own.f1_own), channel_id=1, source_target_pairs={{0,124},{4,0},{8,4},{12,8},{16,12},{20,16},{24,20},{28,24},{32,28}... | collective-permute-start | bytes 663560 | tf_op jit(solution)/shard_map/ppermute | solution.py:594
  70.1 4.4 %collective-permute-done.8.low.f1_low = f32[36,12,128]{2,1,0:T(8,128)S(1)} collective-permute-done((f32[36,12,128]{2,1,0:T(8,128)S(1)}, f32[36,12,128]{2,1,0:T(8,128)S(1)}, u32[]{:S(2)}, u32[]{:S(2)}) %collective-permute-start.8) | collective-permute-done | bytes 221216 | tf_op jit(solution)/shard_map/ppermute | solution.py:594
  74.5 0.3 collective-permute-start.9
  74.8 1.8 %collective-permute-start.10 = (f32[9,24,256]{2,1,0:T(8,128)S(1)}, f32[9,24,256]{2,1,0:T(8,128)S(1)}, u32[]{:S(2)}, u32[]{:S(2)}) collective-permute-start(f32[9,24,256]{2,1,0:T(8,128)S(1)} %get-tuple-element.46), channel_id=1, source_target_pairs={{0,3},{1,0},{2,1},{3,2},{4,7},{5,4},{6,5},{7,6},{8,11},{9,8},{10,9... | collective-permute-start | bytes 663560 | tf_op jit(solution)/shard_map/ppermute | solution.py:594
  76.6 4.1 %shard_map.49 = (f32[24,24,128]{2,1,0:T(8,128)S(1)}, f32[64,18,128]{2,1,0:T(8,128)S(1)}) custom-call(f32[36,12,128]{2,1,0:T(8,128)S(1)} %constant_dynamic-update-slice_fusion.own.f1_own, f32[36,12,128]{2,1,0:T(8,128)S(1)} %collective-permute-done.8.low.f1_low, f32[36,12,128]{2,1,0:T(8,128)S(1)} %collective-permute-done.11.high.f1_high, ...), custom_call_target="tpu_custom_call" | custom-call | flops 1000000000 | bytes 6307840 | tf_op jit(solution)/shard_map/pallas_call | solution.py:574
  80.8 1.2 collective-permute-done.10
  82.0 0.1 pad_maximum_fusion.x_own
  82.0 20.9 %all_to_all.5.same = f32[64,18,128]{2,1,0:T(8,128)S(1)} all-to-all(f32[64,18,128]{2,1,0:T(8,128)S(1)} %get-tuple-element.42), channel_id=1, replica_groups=mesh['pz'=16,'core'=2,'dir'=4] {'pz','dir'}, dimensions={0} | all-to-all | bytes 1179648 | tf_op jit(solution)/shard_map/all_to_all | solution.py:707
  102.9 0.1 copy.13
  103.0 0.1 collective-permute-start.14
  103.1 0.1 fusion.1
  103.2 1.5 collective-permute-start.13
  104.7 0.4 collective-permute-done.14
  105.1 0.4 copy.14.other
  105.5 21.6 %shard_map.50.e2 = f32[17,24,128]{2,1,0:T(8,128)S(1)} custom-call(f32[64,18,128]{2,1,0:T(8,128)S(1)} %all_to_all.5.same, f32[64,18,128]{2,1,0:T(8,128)S(1)} %copy.14.other), custom_call_target="tpu_custom_call" | custom-call | flops 4000000000 | bytes 8372224 | tf_op jit(solution)/shard_map/pallas_call | solution.py:574
  127.1 1.9 %shard_map.51 = f32[12,12,128]{2,1,0:T(8,128)S(1)} custom-call(f32[36,12,128]{2,1,0:T(8,128)S(1)} %constant_dynamic-update-slice_fusion.own.f1_own, f32[36,12,128]{2,1,0:T(8,128)S(1)} %collective-permute-done.8.low.f1_low, f32[36,12,128]{2,1,0:T(8,128)S(1)} %collective-permute-done.11.high.f1_high, f32[40,128]{1,0:T(8,128)S(1)} %get-tuple-element.38.mask.mask1, ...), custom_call_target="tpu_custom_call" | custom-call | flops 1000000000 | bytes 5554176 | tf_op jit(solution)/shard_map/pallas_call | solution.py:574
  129.0 2.4 %collective-permute-start.15 = (f32[9,12,128]{2,1,0:T(8,128)S(1)}, f32[9,12,128]{2,1,0:T(8,128)S(1)}, u32[]{:S(2)}, u32[]{:S(2)}) collective-permute-start(f32[9,12,128]{2,1,0:T(8,128)S(1)} %get-tuple-element.47), channel_id=1, source_target_pairs={{0,1},{1,2},{2,3},{3,0},{4,5},{5,6},{6,7},{7,4},{8,9},{9,10},{10,1... | collective-permute-start | bytes 165896 | tf_op jit(solution)/shard_map/ppermute | solution.py:594
  131.4 2.3 %collective-permute-done.15 = f32[9,12,128]{2,1,0:T(8,128)S(1)} collective-permute-done((f32[9,12,128]{2,1,0:T(8,128)S(1)}, f32[9,12,128]{2,1,0:T(8,128)S(1)}, u32[]{:S(2)}, u32[]{:S(2)}) %collective-permute-start.15) | collective-permute-done | bytes 55328 | tf_op jit(solution)/shard_map/ppermute | solution.py:594
  133.7 3.3 %collective-permute-done.16 = f32[9,12,128]{2,1,0:T(8,128)S(1)} collective-permute-done((f32[9,12,128]{2,1,0:T(8,128)S(1)}, f32[9,12,128]{2,1,0:T(8,128)S(1)}, u32[]{:S(2)}, u32[]{:S(2)}) %collective-permute-start.16) | collective-permute-done | bytes 55328 | tf_op jit(solution)/shard_map/ppermute | solution.py:594
  137.0 3.1 %collective-permute-start.18 = (f32[30,9,128]{2,1,0:T(8,128)S(1)}, f32[30,9,128]{2,1,0:T(8,128)S(1)}, u32[]{:S(2)}, u32[]{:S(2)}) collective-permute-start(f32[30,9,128]{2,1,0:T(8,128)S(1)} %bitcast.12), channel_id=1, source_target_pairs={{0,124},{4,0},{8,4},{12,8},{16,12},{20,16},{24,20},{28,24},{32,28}... | collective-permute-start | bytes 414728 | tf_op jit(solution)/shard_map/ppermute | solution.py:594
  140.1 0.3 collective-permute-start.17
  140.5 7.6 %collective-permute-done.17.y_low = f32[30,8,128]{2,1,0:T(8,128)S(1)} collective-permute-done((f32[30,8,128]{2,1,0:T(8,128)S(1)}, f32[30,8,128]{2,1,0:T(8,128)S(1)}, u32[]{:S(2)}, u32[]{:S(2)}) %collective-permute-start.17) | collective-permute-done | bytes 122912 | tf_op jit(solution)/shard_map/ppermute | solution.py:594
  148.1 16.2 %shard_map.52 = f32[24,24,256]{2,1,0:T(8,128)} custom-call(f32[24,24,256]{2,1,0:T(8,128)S(1)} %copy-done.1, f32[24,24,256]{2,1,0:T(8,128)S(1)} %copy-done.3, f32[26,24,256]{2,1,0:T(8,128)S(1)} %collective-permute-done.low, f32[24,24,256]{2,1,0:T(8,128)S(1)} %collective-permute-done.1.high, f32[1200,128]{1,0:T(8,128)S(1)} %collective-permute-done.2.own_up, ...), custom_call_target="tpu_custom_call" | custom-call | flops 10000000000 | bytes 30142464 | tf_op jit(solution)/shard_map/pallas_call | solution.py:574
  (34 shorter events, 0.2 us)
Async XLA Ops:
  0.0 0.8 copy-start.4
  0.9 1.1 copy-start
  2.0 1.1 copy-start.2
  4.2 17.2 %collective-permute-start = (f32[26,24,256]{2,1,0:T(8,128)S(1)}, f32[26,24,256]{2,1,0:T(8,128)S(1)}, u32[]{:S(2)}, u32[]{:S(2)}) collective-permute-start(f32[26,24,256]{2,1,0:T(8,128)S(1)} %get-tuple-element.24), channel_id=1, source_target_pairs={{0,1},{1,2},{2,3},{3,0},{4,5},{5,6},{6,7},{7,4},{8,9},{9,10},{10,1... | collective-permute-start | bytes 1916936 | tf_op jit(solution)/shard_map/ppermute | solution.py:594
  4.6 16.9 %collective-permute-start.2 = (f32[1200,128]{1,0:T(8,128)S(1)}, f32[1200,128]{1,0:T(8,128)S(1)}, u32[]{:S(2)}, u32[]{:S(2)}) collective-permute-start(f32[1200,128]{1,0:T(8,128)S(1)} %get-tuple-element.26), channel_id=1, source_target_pairs={{0,4},{4,8},{8,12},{12,16},{16,20},{20,24},{24,28},{28,32},{32,36}... | collective-permute-start | bytes 1843208 | tf_op jit(solution)/shard_map/ppermute | solution.py:594
  4.6 16.8 %collective-permute-start.1 = (f32[24,24,256]{2,1,0:T(8,128)}, f32[24,24,256]{2,1,0:T(8,128)S(1)}, u32[]{:S(2)}, u32[]{:S(2)}) collective-permute-start(f32[24,24,256]{2,1,0:T(8,128)} %get-tuple-element.25), channel_id=1, source_target_pairs={{0,3},{1,0},{2,1},{3,2},{4,7},{5,4},{6,5},{7,6},{8,11},{9,8},{10,9... | collective-permute-start | bytes 1769480 | tf_op jit(solution)/shard_map/ppermute | solution.py:594
  6.2 12.8 %collective-permute-start.3 = (f32[1104,128]{1,0:T(8,128)}, f32[1104,128]{1,0:T(8,128)}, u32[]{:S(2)}, u32[]{:S(2)}) collective-permute-start(f32[1104,128]{1,0:T(8,128)} %get-tuple-element.27), channel_id=1, source_target_pairs={{0,124},{4,0},{8,4},{12,8},{16,12},{20,16},{24,20},{28,24},{32,28}... | collective-permute-start | bytes 1695752 | tf_op jit(solution)/shard_map/ppermute | solution.py:594
  21.7 13.4 %copy-start.1 = (f32[24,24,256]{2,1,0:T(8,128)S(1)}, f32[24,24,256]{2,1,0:T(8,128)}, u32[]{:S(2)}) copy-start(f32[24,24,256]{2,1,0:T(8,128)} %guess.5) | copy-start | bytes 1769476
  21.8 13.4 %copy-start.3 = (f32[24,24,256]{2,1,0:T(8,128)S(1)}, f32[24,24,256]{2,1,0:T(8,128)}, u32[]{:S(2)}) copy-start(f32[24,24,256]{2,1,0:T(8,128)} %load.5) | copy-start | bytes 1769476
  21.9 13.2 %collective-permute-start.4 = (f32[1248,128]{1,0:T(8,128)S(1)}, f32[1248,128]{1,0:T(8,128)S(1)}, u32[]{:S(2)}, u32[]{:S(2)}) collective-permute-start(f32[1248,128]{1,0:T(8,128)S(1)} %get-tuple-element.32), channel_id=1, source_target_pairs={{0,4},{4,8},{8,12},{12,16},{16,20},{20,24},{24,28},{28,32},{32,36}... | collective-permute-start | bytes 1916936 | tf_op jit(solution)/shard_map/ppermute | solution.py:594
  22.5 11.9 %collective-permute-start.5 = (f32[1152,128]{1,0:T(8,128)S(1)}, f32[1152,128]{1,0:T(8,128)S(1)}, u32[]{:S(2)}, u32[]{:S(2)}) collective-permute-start(f32[1152,128]{1,0:T(8,128)S(1)} %get-tuple-element.33), channel_id=1, source_target_pairs={{0,124},{4,0},{8,4},{12,8},{16,12},{20,16},{24,20},{28,24},{32,28}... | collective-permute-start | bytes 1769480 | tf_op jit(solution)/shard_map/ppermute | solution.py:594
  58.5 4.7 %collective-permute-start.6 = (f32[12,12,128]{2,1,0:T(8,128)S(1)}, f32[12,12,128]{2,1,0:T(8,128)S(1)}, u32[]{:S(2)}, u32[]{:S(2)}) collective-permute-start(f32[12,12,128]{2,1,0:T(8,128)S(1)} %get-tuple-element.35), channel_id=1, source_target_pairs={{0,1},{1,2},{2,3},{3,0},{4,5},{5,6},{6,7},{7,4},{8,9},{9,10},{10,1... | collective-permute-start | bytes 221192 | tf_op jit(solution)/shard_map/ppermute | solution.py:594
  59.1 5.8 %collective-permute-start.7 = (f32[12,12,128]{2,1,0:T(8,128)S(1)}, f32[12,12,128]{2,1,0:T(8,128)S(1)}, u32[]{:S(2)}, u32[]{:S(2)}) collective-permute-start(f32[12,12,128]{2,1,0:T(8,128)S(1)} %get-tuple-element.35), channel_id=1, source_target_pairs={{0,3},{1,0},{2,1},{3,2},{4,7},{5,4},{6,5},{7,6},{8,11},{9,8},{10,9... | collective-permute-start | bytes 221192 | tf_op jit(solution)/shard_map/ppermute | solution.py:594
  65.0 9.5 %collective-permute-start.8 = (f32[36,12,128]{2,1,0:T(8,128)S(1)}, f32[36,12,128]{2,1,0:T(8,128)S(1)}, u32[]{:S(2)}, u32[]{:S(2)}) collective-permute-start(f32[36,12,128]{2,1,0:T(8,128)S(1)} %constant_dynamic-update-slice_fusion.own.f1_own), channel_id=1, source_target_pairs={{0,4},{4,8},{8,12},{12,16},{16,20},{20,24},{24,28},{28,32},{32,36}... | collective-permute-start | bytes 663560 | tf_op jit(solution)/shard_map/ppermute | solution.py:594
  65.1 11.6 %collective-permute-start.11 = (f32[36,12,128]{2,1,0:T(8,128)S(1)}, f32[36,12,128]{2,1,0:T(8,128)S(1)}, u32[]{:S(2)}, u32[]{:S(2)}) collective-permute-start(f32[36,12,128]{2,1,0:T(8,128)S(1)} %constant_dynamic-update-slice_fusion.own.f1_own), channel_id=1, source_target_pairs={{0,124},{4,0},{8,4},{12,8},{16,12},{20,16},{24,20},{28,24},{32,28}... | collective-permute-start | bytes 663560 | tf_op jit(solution)/shard_map/ppermute | solution.py:594
  74.5 6.2 %collective-permute-start.9 = (f32[9,24,256]{2,1,0:T(8,128)S(1)}, f32[9,24,256]{2,1,0:T(8,128)S(1)}, u32[]{:S(2)}, u32[]{:S(2)}) collective-permute-start(f32[9,24,256]{2,1,0:T(8,128)S(1)} %get-tuple-element.45), channel_id=1, source_target_pairs={{0,1},{1,2},{2,3},{3,0},{4,5},{5,6},{6,7},{7,4},{8,9},{9,10},{10,1... | collective-permute-start | bytes 663560 | tf_op jit(solution)/shard_map/ppermute | solution.py:594
  74.8 7.1 %collective-permute-start.10 = (f32[9,24,256]{2,1,0:T(8,128)S(1)}, f32[9,24,256]{2,1,0:T(8,128)S(1)}, u32[]{:S(2)}, u32[]{:S(2)}) collective-permute-start(f32[9,24,256]{2,1,0:T(8,128)S(1)} %get-tuple-element.46), channel_id=1, source_target_pairs={{0,3},{1,0},{2,1},{3,2},{4,7},{5,4},{6,5},{7,6},{8,11},{9,8},{10,9... | collective-permute-start | bytes 663560 | tf_op jit(solution)/shard_map/ppermute | solution.py:594
  103.0 2.1 %collective-permute-start.14 = (f32[64,18,128]{2,0,1:T(8,128)S(1)}, f32[64,18,128]{2,0,1:T(8,128)S(1)}, u32[]{:S(2)}, u32[]{:S(2)}) collective-permute-start(f32[64,18,128]{2,0,1:T(8,128)S(1)} %copy.13), channel_id=1, source_target_pairs={{0,4},{4,0},{1,5},{5,1},{2,6},{6,2},{3,7},{7,3},{8,12},{12,8},{9,1... | collective-permute-start | bytes 1769480 | tf_op jit(solution)/shard_map/ppermute | solution.py:708
  103.2 37.2 %collective-permute-start.13 = (f32[42,16,256]{2,1,0:T(8,128)S(1)}, f32[42,16,256]{2,1,0:T(8,128)S(1)}, u32[]{:S(2)}, u32[]{:S(2)}) collective-permute-start(f32[42,16,256]{2,1,0:T(8,128)S(1)} %get-tuple-element.43), channel_id=1, source_target_pairs={{0,124},{4,0},{8,4},{12,8},{16,12},{20,16},{24,20},{28,24},{32,28}... | collective-permute-start | bytes 2064392 | tf_op jit(solution)/shard_map/ppermute | solution.py:594
  104.7 35.8 %collective-permute-start.12 = (f32[42,16,256]{2,1,0:T(8,128)S(1)}, f32[42,16,256]{2,1,0:T(8,128)S(1)}, u32[]{:S(2)}, u32[]{:S(2)}) collective-permute-start(f32[42,16,256]{2,1,0:T(8,128)S(1)} %get-tuple-element.44), channel_id=1, source_target_pairs={{0,4},{4,8},{8,12},{12,16},{16,20},{20,24},{24,28},{28,32},{32,36}... | collective-permute-start | bytes 2064392 | tf_op jit(solution)/shard_map/ppermute | solution.py:594
  129.0 4.7 %collective-permute-start.15 = (f32[9,12,128]{2,1,0:T(8,128)S(1)}, f32[9,12,128]{2,1,0:T(8,128)S(1)}, u32[]{:S(2)}, u32[]{:S(2)}) collective-permute-start(f32[9,12,128]{2,1,0:T(8,128)S(1)} %get-tuple-element.47), channel_id=1, source_target_pairs={{0,1},{1,2},{2,3},{3,0},{4,5},{5,6},{6,7},{7,4},{8,9},{9,10},{10,1... | collective-permute-start | bytes 165896 | tf_op jit(solution)/shard_map/ppermute | solution.py:594
  131.4 5.6 %collective-permute-start.16 = (f32[9,12,128]{2,1,0:T(8,128)S(1)}, f32[9,12,128]{2,1,0:T(8,128)S(1)}, u32[]{:S(2)}, u32[]{:S(2)}) collective-permute-start(f32[9,12,128]{2,1,0:T(8,128)S(1)} %get-tuple-element.48), channel_id=1, source_target_pairs={{0,3},{1,0},{2,1},{3,2},{4,7},{5,4},{6,5},{7,6},{8,11},{9,8},{10,9... | collective-permute-start | bytes 165896 | tf_op jit(solution)/shard_map/ppermute | solution.py:594
  137.0 11.1 %collective-permute-start.18 = (f32[30,9,128]{2,1,0:T(8,128)S(1)}, f32[30,9,128]{2,1,0:T(8,128)S(1)}, u32[]{:S(2)}, u32[]{:S(2)}) collective-permute-start(f32[30,9,128]{2,1,0:T(8,128)S(1)} %bitcast.12), channel_id=1, source_target_pairs={{0,124},{4,0},{8,4},{12,8},{16,12},{20,16},{24,20},{28,24},{32,28}... | collective-permute-start | bytes 414728 | tf_op jit(solution)/shard_map/ppermute | solution.py:594
  140.1 8.0 %collective-permute-start.17 = (f32[30,8,128]{2,1,0:T(8,128)S(1)}, f32[30,8,128]{2,1,0:T(8,128)S(1)}, u32[]{:S(2)}, u32[]{:S(2)}) collective-permute-start(f32[30,8,128]{2,1,0:T(8,128)S(1)} %slice.62), channel_id=1, source_target_pairs={{0,4},{4,8},{8,12},{12,16},{16,20},{20,24},{24,28},{28,32},{32,36}... | collective-permute-start | bytes 368648 | tf_op jit(solution)/shard_map/ppermute | solution.py:594

commit v5 on v4

--- a/solution.py
+++ b/solution.py
@@ -47,13 +47,24 @@
 
 
 def fill_w(w_ref, depth, size, pairs=False):
-    mass = {0: 2416.0, 1: 1192.0, -1: 1192.0, 2: 120.0, -2: 120.0, 3: 1.0, -3: 1.0}
-    low = {1: -1.0, -1: -1.0}
-    stiff = {0: 80.0, 1: -15.0, -1: -15.0, 2: -24.0, -2: -24.0, 3: -1.0, -3: -1.0}
-    for block, table in enumerate((mass, mass, stiff, stiff, low)):
-        w_ref[block * depth : (block + 1) * depth, :] = banded(
-            depth, depth, size, size, table, 1, -1, pairs
-        )
+    i = lax.broadcasted_iota(jnp.int32, (depth, depth), 0)
+    j = lax.broadcasted_iota(jnp.int32, (depth, depth), 1)
+    inside = i >= 0
+    if pairs:
+        inside = (i < 64) == (j < 64)
+        i, j = jnp.where(i < 64, i, i - 64), jnp.where(j < 64, j, j - 64)
+    apart = jnp.where(inside & (i < size) & (j < size), jnp.abs(i - j), 9)
+
+    def table(*taps):
+        out = jnp.zeros((depth, depth), F32)
+        for distance, weight in enumerate(taps):
+            out = jnp.where(apart == distance, weight, out)
+        return out.astype(BF16)
+
+    mass = table(2416.0, 1192.0, 120.0, 1.0)
+    stiff = table(80.0, -15.0, -24.0, -1.0)
+    for block, matrix in enumerate((mass, mass, stiff, stiff, table(0.0, -1.0))):
+        w_ref[block * depth : (block + 1) * depth, :] = matrix
 
 
 def restrict_w(rows, columns, size, pairs=False):
@@ -105,13 +116,14 @@
 
             start = [plane(u0 - 3 + k) for k in range(6)]
             carry = tuple([p for p, _ in start] + [q for _, q in start])
-            groups = nu // 6
+            group = nu // 3 if nu >= 18 else nu
+            groups = nu // group
             if groups > 1:
-                carry = lax.fori_loop(0, groups, lambda g, c: several(6 * g, 6, c), carry)
-            elif groups == 1:
-                carry = several(0, 6, carry)
-            if nu % 6:
-                several(6 * groups, nu % 6, carry)
+                carry = lax.fori_loop(0, groups, lambda g, c: several(group * g, group, c), carry)
+            else:
+                carry = several(0, group, carry)
+            if nu % group:
+                several(group * groups, nu % group, carry)
 
 
 def stencil_pairs(x_ref, l_ref, k0, nk, v0, nv):
@@ -159,7 +171,8 @@
 
 def finish(l_ref, w_ref, nu, nv, use):
     depth = w_ref.shape[1]
-    chunk = max(1, min(nu, 384 // nv))
+    chunk = max(1, min(nu, 1152 // nv))
+    chunk = -(-nu // -(-nu // chunk))
 
     def some(first, count):
         left = l_ref[pl.ds(first, count), 0:nv, :].reshape(count * nv, 4 * depth)
@@ -222,8 +235,8 @@
         plane = 0.125 * (read(-1) + read(1)) + 0.75 * read(0)
     else:
         plane = 0.5 * (read(0) + read(1))
-    tu_ref[0 : plane.shape[0], :] = plane
-    low, mid, high = (tu_ref[k : k + rows, :] for k in range(3))
+    tu_ref[slot, 0 : plane.shape[0], :] = plane
+    low, mid, high = (tu_ref[slot, k : k + rows, :] for k in range(3))
     z_ref[slot, pl.ds(0, rows, stride=2), :] = 0.125 * (low + high) + 0.75 * mid
     z_ref[slot, pl.ds(1, rows, stride=2), :] = 0.5 * (mid + high)
 
@@ -374,11 +387,12 @@
         def read(k):
             return y[0, u // 2 + 12 + k, 6:30, :]
 
-        widen(read, u % 2 == 0, tu_ref, z_ref, 0, 22)
-        fine = dot_split(z_ref[0, 0:48, :], pw)
+        widen(read, u % 2 == 0, tu_ref, z_ref, u + 9, 22)
+    for first in (0, 21):
+        fine = dot_split(z_ref[first : first + 21].reshape(21 * 48, LANES), pw)
         for tile in range(2):
             lanes = slice(tile * LANES, (tile + 1) * LANES)
-            x[tile, u + UB0, 6:50, :] = fine[0:44, lanes]
+            x[tile, first + 5 : first + 26, 6:54, :] = fine[:, lanes].reshape(21, 48, LANES)
     for u in range(42):
         for tile in range(2):
             lanes = slice(tile * LANES, (tile + 1) * LANES)
@@ -440,8 +454,9 @@
         def read(k):
             return e2[coarse + k, 0:24, :]
 
-        widen(read, u % 2 == 0, tu_ref, z_ref, 0, 16)
-        x[0, u + 12, 4:36, :] = dot_split(z_ref[0, 0:32, :], pw)
+        widen(read, u % 2 == 0, tu_ref, z_ref, u + 6, 16)
+    fine = dot_split(z_ref[...].reshape(24 * 32, LANES), pw)
+    x[0, 6:30, 4:36, :] = fine.reshape(24, 32, LANES)
     for u in range(6, 30):
         for row in (6, 18):
             at = slice(row, row + 12)
@@ -531,17 +546,19 @@
 
     def wide(k, _):
         before, own, after = (b_ref[k + i] for i in range(3))
-        tu_ref[0:24, :] = jnp.where(
+        spread = tu_ref.at[pl.ds(24 * k, 24)]
+        spread[...] = jnp.where(
             low_half(24), 0.125 * (before + after) + 0.75 * own, 0.5 * (own + after)
         )
-        first, mid, last = (tu_ref[i : i + 22, :] for i in range(3))
-        z_ref[0, pl.ds(0, 22, stride=2), :] = 0.125 * (first + last) + 0.75 * mid
-        z_ref[0, pl.ds(1, 22, stride=2), :] = 0.5 * (mid + last)
-        fine = dot_split(z_ref[0, 0:48, :], pw)
-        at = (0, k + 2, slice(46, 94), slice(None))
-        x[at] = x[at] + fine
-
-    lax.fori_loop(0, 12, wide, None)
+        first, mid, last = (spread[i : i + 22, :] for i in range(3))
+        z_ref[k, pl.ds(0, 22, stride=2), :] = 0.125 * (first + last) + 0.75 * mid
+        z_ref[k, pl.ds(1, 22, stride=2), :] = 0.5 * (mid + last)
+
+    for k in range(12):
+        wide(k, None)
+    fine = dot_split(z_ref[...].reshape(12 * 48, LANES), pw)
+    at = (0, slice(2, 14), slice(46, 94), slice(None))
+    x[at] = x[at] + fine.reshape(12, 48, LANES)
     smooth(2, 12, x, sf, w_ref, 50, 32)
     smooth(2, 12, x, sf, w_ref, 53, 32)
     smooth(2, 12, x, sf, w_ref, 56, 16)
@@ -715,12 +732,12 @@
             ((12, 128, 512), BF16),
             w1,
             ((14, 112, 128), F32),
-            ((112, 128), F32),
+            ((288, 128), F32),
             ((1, 10, 64, LANES), F32),
             ((1, 10, 64, LANES), F32),
             w1,
             ((14, 24, 128), F32),
-            ((2, 48, 128), F32),
+            ((12, 48, 128), F32),
         ],
         (same, other),
         4 * 10**9,
@@ -728,7 +745,7 @@
     (y,) = call(
         next_post,
         [shape_of(12, 12, 128)],
-        [window1, window1, window1, left1, w1, ((48, 128), F32), ((2, 48, 128), F32)],
+        [window1, window1, window1, left1, w1, ((24, 24, 128), F32), ((24, 32, 128), F32)],
         (f1_own, f1_low, f1_high, mask1, x1, e2),
         10**9,
     )
@@ -744,8 +761,8 @@
             window,
             left0,
             w0,
-            ((48, 128), F32),
-            ((2, 48, 128), F32),
+            ((42, 24, 128), F32),
+            ((42, 48, 128), F32),
             columns,
             window1,
             window1,

time: 165 us -> 161 us (0.976); the launches traced: 164 us -> 158 us
  Pallas kernels: 68.5 us -> 61.1 us
    pallas_call x7, Pallas kernels: 68.5 us -> 61.1 us  [call(): pl.pallas_call(body, out_shape=list(outs), in_specs=[vmem] * len(operands...]
  transfers between devices with their start and end apart: 19 -> 19, of which waited for: 12 -> 13; matrix products, arithmetic and copies ran while one was open for 0% -> 0% of each run, Pallas kernels for 17% -> 15%
where the time goes in v5:
time: 161 us; the launch traced here: 158 us
  Pallas kernels  61.1 us (38%)
  waiting for transfers between devices  41.4 us (26%)
  starting transfers between devices  30.2 us (19%)
  blocking collectives  20.5 us (13%)
  local copies, waits for them, and re-layouts  3.77 us (2%)
    pallas_call x7, Pallas kernels, call(): pl.pallas_call(body, out_shape=list(outs), in_specs=[vmem] * len(operands...  61.1 us
    ppermute x18, waiting for transfers between devices, ring(): return lax.ppermute(value, axes if len(axes) > 1 else axes[0], pairs)  41.2 us
    ppermute x18, starting transfers between devices, ring(): return lax.ppermute(value, axes if len(axes) > 1 else axes[0], pairs)  30.1 us
    all_to_all x1, blocking collectives, on_device(): same = lax.all_to_all(f2, ('pz', 'dir'), 0, 0)  20.5 us
  transfers between devices with their start and end apart: 19, of which 13 were waited for; matrix products, arithmetic and copies ran while one was open for 0% of the time, Pallas kernels for 15%

profile of v5, /device:TPU:6, one launch (start us, length us, event | category | flops | bytes accessed | tf_op | source)
XLA Modules:
  0.0 157.7 jit_solution(8077960405305643924)
XLA Ops:
  0.0 0.8 copy.11
  0.9 1.1 copy-done
  2.0 1.1 copy-done.2
  3.0 1.2 shard_map.46
  4.2 0.4 collective-permute-start
  4.6 1.6 %collective-permute-start.1 = (f32[24,24,256]{2,1,0:T(8,128)}, f32[24,24,256]{2,1,0:T(8,128)S(1)}, u32[]{:S(2)}, u32[]{:S(2)}) collective-permute-start(f32[24,24,256]{2,1,0:T(8,128)} %get-tuple-element.25), channel_id=1, source_target_pairs={{0,3},{1,0},{2,1},{3,2},{4,7},{5,4},{6,5},{7,6},{8,11},{9,8},{10,9... | collective-permute-start | bytes 1769480 | tf_op jit(solution)/shard_map/ppermute | solution.py:611
  6.2 5.4 %collective-permute-start.3 = (f32[1104,128]{1,0:T(8,128)}, f32[1104,128]{1,0:T(8,128)}, u32[]{:S(2)}, u32[]{:S(2)}) collective-permute-start(f32[1104,128]{1,0:T(8,128)} %get-tuple-element.27), channel_id=1, source_target_pairs={{0,124},{4,0},{8,4},{12,8},{16,12},{20,16},{24,20},{28,24},{32,28}... | collective-permute-start | bytes 1695752 | tf_op jit(solution)/shard_map/ppermute | solution.py:611
  11.6 7.4 %collective-permute-done.3.own_down = f32[1104,128]{1,0:T(8,128)} collective-permute-done((f32[1104,128]{1,0:T(8,128)}, f32[1104,128]{1,0:T(8,128)}, u32[]{:S(2)}, u32[]{:S(2)}) %collective-permute-start.3) | collective-permute-done | bytes 565280 | tf_op jit(solution)/shard_map/ppermute | solution.py:611
  19.1 2.4 %collective-permute-done.1.high = f32[24,24,256]{2,1,0:T(8,128)S(1)} collective-permute-done((f32[24,24,256]{2,1,0:T(8,128)}, f32[24,24,256]{2,1,0:T(8,128)S(1)}, u32[]{:S(2)}, u32[]{:S(2)}) %collective-permute-start.1) | collective-permute-done | bytes 589856 | tf_op jit(solution)/shard_map/ppermute | solution.py:611
  21.5 0.1 slice.56
  21.6 0.1 maximum_multiply_fusion.1
  21.7 0.1 maximum_multiply_fusion
  21.8 0.1 shard_map.47
  21.9 0.7 collective-permute-start.4
  22.5 5.0 %collective-permute-start.5 = (f32[1152,128]{1,0:T(8,128)S(1)}, f32[1152,128]{1,0:T(8,128)S(1)}, u32[]{:S(2)}, u32[]{:S(2)}) collective-permute-start(f32[1152,128]{1,0:T(8,128)S(1)} %get-tuple-element.33), channel_id=1, source_target_pairs={{0,124},{4,0},{8,4},{12,8},{16,12},{20,16},{24,20},{28,24},{32,28}... | collective-permute-start | bytes 1769480 | tf_op jit(solution)/shard_map/ppermute | solution.py:611
  27.5 7.4 %collective-permute-done.5.down = f32[1152,128]{1,0:T(8,128)S(1)} collective-permute-done((f32[1152,128]{1,0:T(8,128)S(1)}, f32[1152,128]{1,0:T(8,128)S(1)}, u32[]{:S(2)}, u32[]{:S(2)}) %collective-permute-start.5) | collective-permute-done | bytes 589856 | tf_op jit(solution)/shard_map/ppermute | solution.py:611
  34.9 0.2 collective-permute-done.4.up
  35.1 20.8 %shard_map.48 = (f32[24,24,256]{2,1,0:T(8,128)S(1)}, f32[12,12,128]{2,1,0:T(8,128)S(1)}, f32[40,128]{1,0:T(8,128)S(1)}) custom-call(f32[24,24,256]{2,1,0:T(8,128)S(1)} %copy-done.1, f32[24,24,256]{2,1,0:T(8,128)S(1)} %copy-done.3, f32[26,24,256]{2,1,0:T(8,128)S(1)} %collective-permute-done.low, f32[24,24,256]{2,1,0:T(8,128)S(1)} %collective-permute-done.1.high, ...), custom_call_target="tpu_custom_call" | custom-call | flops 10000000000 | bytes 22474752 | tf_op jit(solution)/shard_map/pallas_call | solution.py:591
  55.9 0.6 collective-permute-start.6
  56.5 1.5 collective-permute-start.7
  58.0 2.6 %collective-permute-done.6 = f32[12,12,128]{2,1,0:T(8,128)S(1)} collective-permute-done((f32[12,12,128]{2,1,0:T(8,128)S(1)}, f32[12,12,128]{2,1,0:T(8,128)S(1)}, u32[]{:S(2)}, u32[]{:S(2)}) %collective-permute-start.6) | collective-permute-done | bytes 73760 | tf_op jit(solution)/shard_map/ppermute | solution.py:611
  60.6 1.7 %collective-permute-done.7 = f32[12,12,128]{2,1,0:T(8,128)S(1)} collective-permute-done((f32[12,12,128]{2,1,0:T(8,128)S(1)}, f32[12,12,128]{2,1,0:T(8,128)S(1)}, u32[]{:S(2)}, u32[]{:S(2)}) %collective-permute-start.7) | collective-permute-done | bytes 73760 | tf_op jit(solution)/shard_map/ppermute | solution.py:611
  62.4 0.1 collective-permute-start.8
  62.4 5.2 %collective-permute-start.11 = (f32[36,12,128]{2,1,0:T(8,128)S(1)}, f32[36,12,128]{2,1,0:T(8,128)S(1)}, u32[]{:S(2)}, u32[]{:S(2)}) collective-permute-start(f32[36,12,128]{2,1,0:T(8,128)S(1)} %constant_dynamic-update-slice_fusion.own.f1_own), channel_id=1, source_target_pairs={{0,124},{4,0},{8,4},{12,8},{16,12},{20,16},{24,20},{28,24},{32,28}... | collective-permute-start | bytes 663560 | tf_op jit(solution)/shard_map/ppermute | solution.py:611
  67.6 4.3 %collective-permute-done.8.low.f1_low = f32[36,12,128]{2,1,0:T(8,128)S(1)} collective-permute-done((f32[36,12,128]{2,1,0:T(8,128)S(1)}, f32[36,12,128]{2,1,0:T(8,128)S(1)}, u32[]{:S(2)}, u32[]{:S(2)}) %collective-permute-start.8) | collective-permute-done | bytes 221216 | tf_op jit(solution)/shard_map/ppermute | solution.py:611
  71.9 0.3 collective-permute-start.9
  72.2 1.8 %collective-permute-start.10 = (f32[9,24,256]{2,1,0:T(8,128)S(1)}, f32[9,24,256]{2,1,0:T(8,128)S(1)}, u32[]{:S(2)}, u32[]{:S(2)}) collective-permute-start(f32[9,24,256]{2,1,0:T(8,128)S(1)} %get-tuple-element.46), channel_id=1, source_target_pairs={{0,3},{1,0},{2,1},{3,2},{4,7},{5,4},{6,5},{7,6},{8,11},{9,8},{10,9... | collective-permute-start | bytes 663560 | tf_op jit(solution)/shard_map/ppermute | solution.py:611
  74.0 3.5 %shard_map.49 = (f32[24,24,128]{2,1,0:T(8,128)S(1)}, f32[64,18,128]{2,1,0:T(8,128)S(1)}) custom-call(f32[36,12,128]{2,1,0:T(8,128)S(1)} %constant_dynamic-update-slice_fusion.own.f1_own, f32[36,12,128]{2,1,0:T(8,128)S(1)} %collective-permute-done.8.low.f1_low, f32[36,12,128]{2,1,0:T(8,128)S(1)} %collective-permute-done.11.high.f1_high, ...), custom_call_target="tpu_custom_call" | custom-call | flops 1000000000 | bytes 6307840 | tf_op jit(solution)/shard_map/pallas_call | solution.py:591
  77.5 0.4 collective-permute-done.9
  77.9 1.4 collective-permute-done.10
  79.3 0.1 pad_maximum_fusion.x_own
  79.4 20.5 %all_to_all.5.same = f32[64,18,128]{2,1,0:T(8,128)S(1)} all-to-all(f32[64,18,128]{2,1,0:T(8,128)S(1)} %get-tuple-element.42), channel_id=1, replica_groups=mesh['pz'=16,'core'=2,'dir'=4] {'pz','dir'}, dimensions={0} | all-to-all | bytes 1179648 | tf_op jit(solution)/shard_map/all_to_all | solution.py:724
  99.9 0.1 copy.13
  100.1 0.1 collective-permute-start.14
  100.1 0.1 fusion.1
  100.3 1.5 collective-permute-start.13
  101.8 0.2 collective-permute-start.12
  102.0 0.2 collective-permute-done.14
  102.1 0.4 copy.14.other
  102.5 18.2 %shard_map.50.e2 = f32[17,24,128]{2,1,0:T(8,128)S(1)} custom-call(f32[64,18,128]{2,1,0:T(8,128)S(1)} %all_to_all.5.same, f32[64,18,128]{2,1,0:T(8,128)S(1)} %copy.14.other), custom_call_target="tpu_custom_call" | custom-call | flops 4000000000 | bytes 8708096 | tf_op jit(solution)/shard_map/pallas_call | solution.py:591
  120.7 1.9 %shard_map.51 = f32[12,12,128]{2,1,0:T(8,128)S(1)} custom-call(f32[36,12,128]{2,1,0:T(8,128)S(1)} %constant_dynamic-update-slice_fusion.own.f1_own, f32[36,12,128]{2,1,0:T(8,128)S(1)} %collective-permute-done.8.low.f1_low, f32[36,12,128]{2,1,0:T(8,128)S(1)} %collective-permute-done.11.high.f1_high, f32[40,128]{1,0:T(8,128)S(1)} %get-tuple-element.38.mask.mask1, ...), custom_call_target="tpu_custom_call" | custom-call | flops 1000000000 | bytes 6168576 | tf_op jit(solution)/shard_map/pallas_call | solution.py:591
  122.6 2.4 %collective-permute-start.15 = (f32[9,12,128]{2,1,0:T(8,128)S(1)}, f32[9,12,128]{2,1,0:T(8,128)S(1)}, u32[]{:S(2)}, u32[]{:S(2)}) collective-permute-start(f32[9,12,128]{2,1,0:T(8,128)S(1)} %get-tuple-element.47), channel_id=1, source_target_pairs={{0,1},{1,2},{2,3},{3,0},{4,5},{5,6},{6,7},{7,4},{8,9},{9,10},{10,1... | collective-permute-start | bytes 165896 | tf_op jit(solution)/shard_map/ppermute | solution.py:611
  125.0 2.5 %collective-permute-done.15 = f32[9,12,128]{2,1,0:T(8,128)S(1)} collective-permute-done((f32[9,12,128]{2,1,0:T(8,128)S(1)}, f32[9,12,128]{2,1,0:T(8,128)S(1)}, u32[]{:S(2)}, u32[]{:S(2)}) %collective-permute-start.15) | collective-permute-done | bytes 55328 | tf_op jit(solution)/shard_map/ppermute | solution.py:611
  127.5 3.3 %collective-permute-done.16 = f32[9,12,128]{2,1,0:T(8,128)S(1)} collective-permute-done((f32[9,12,128]{2,1,0:T(8,128)S(1)}, f32[9,12,128]{2,1,0:T(8,128)S(1)}, u32[]{:S(2)}, u32[]{:S(2)}) %collective-permute-start.16) | collective-permute-done | bytes 55328 | tf_op jit(solution)/shard_map/ppermute | solution.py:611
  130.8 3.2 %collective-permute-start.18 = (f32[30,9,128]{2,1,0:T(8,128)S(1)}, f32[30,9,128]{2,1,0:T(8,128)S(1)}, u32[]{:S(2)}, u32[]{:S(2)}) collective-permute-start(f32[30,9,128]{2,1,0:T(8,128)S(1)} %bitcast.12), channel_id=1, source_target_pairs={{0,124},{4,0},{8,4},{12,8},{16,12},{20,16},{24,20},{28,24},{32,28}... | collective-permute-start | bytes 414728 | tf_op jit(solution)/shard_map/ppermute | solution.py:611
  133.9 0.3 collective-permute-start.17
  134.3 7.6 %collective-permute-done.17.y_low = f32[30,8,128]{2,1,0:T(8,128)S(1)} collective-permute-done((f32[30,8,128]{2,1,0:T(8,128)S(1)}, f32[30,8,128]{2,1,0:T(8,128)S(1)}, u32[]{:S(2)}, u32[]{:S(2)}) %collective-permute-start.17) | collective-permute-done | bytes 122912 | tf_op jit(solution)/shard_map/ppermute | solution.py:611
  141.9 15.5 %shard_map.52 = f32[24,24,256]{2,1,0:T(8,128)} custom-call(f32[24,24,256]{2,1,0:T(8,128)S(1)} %copy-done.1, f32[24,24,256]{2,1,0:T(8,128)S(1)} %copy-done.3, f32[26,24,256]{2,1,0:T(8,128)S(1)} %collective-permute-done.low, f32[24,24,256]{2,1,0:T(8,128)S(1)} %collective-permute-done.1.high, f32[1200,128]{1,0:T(8,128)S(1)} %collective-permute-done.2.own_up, ...), custom_call_target="tpu_custom_call" | custom-call | flops 10000000000 | bytes 31617024 | tf_op jit(solution)/shard_map/pallas_call | solution.py:591
  (34 shorter events, 0.3 us)
Async XLA Ops:
  0.0 0.8 copy-start.4
  0.9 1.1 copy-start
  2.0 1.1 copy-start.2
  4.2 17.2 %collective-permute-start = (f32[26,24,256]{2,1,0:T(8,128)S(1)}, f32[26,24,256]{2,1,0:T(8,128)S(1)}, u32[]{:S(2)}, u32[]{:S(2)}) collective-permute-start(f32[26,24,256]{2,1,0:T(8,128)S(1)} %get-tuple-element.24), channel_id=1, source_target_pairs={{0,1},{1,2},{2,3},{3,0},{4,5},{5,6},{6,7},{7,4},{8,9},{9,10},{10,1... | collective-permute-start | bytes 1916936 | tf_op jit(solution)/shard_map/ppermute | solution.py:611
  4.6 16.9 %collective-permute-start.2 = (f32[1200,128]{1,0:T(8,128)S(1)}, f32[1200,128]{1,0:T(8,128)S(1)}, u32[]{:S(2)}, u32[]{:S(2)}) collective-permute-start(f32[1200,128]{1,0:T(8,128)S(1)} %get-tuple-element.26), channel_id=1, source_target_pairs={{0,4},{4,8},{8,12},{12,16},{16,20},{20,24},{24,28},{28,32},{32,36}... | collective-permute-start | bytes 1843208 | tf_op jit(solution)/shard_map/ppermute | solution.py:611
  4.6 16.8 %collective-permute-start.1 = (f32[24,24,256]{2,1,0:T(8,128)}, f32[24,24,256]{2,1,0:T(8,128)S(1)}, u32[]{:S(2)}, u32[]{:S(2)}) collective-permute-start(f32[24,24,256]{2,1,0:T(8,128)} %get-tuple-element.25), channel_id=1, source_target_pairs={{0,3},{1,0},{2,1},{3,2},{4,7},{5,4},{6,5},{7,6},{8,11},{9,8},{10,9... | collective-permute-start | bytes 1769480 | tf_op jit(solution)/shard_map/ppermute | solution.py:611
  6.2 12.8 %collective-permute-start.3 = (f32[1104,128]{1,0:T(8,128)}, f32[1104,128]{1,0:T(8,128)}, u32[]{:S(2)}, u32[]{:S(2)}) collective-permute-start(f32[1104,128]{1,0:T(8,128)} %get-tuple-element.27), channel_id=1, source_target_pairs={{0,124},{4,0},{8,4},{12,8},{16,12},{20,16},{24,20},{28,24},{32,28}... | collective-permute-start | bytes 1695752 | tf_op jit(solution)/shard_map/ppermute | solution.py:611
  21.7 13.4 %copy-start.1 = (f32[24,24,256]{2,1,0:T(8,128)S(1)}, f32[24,24,256]{2,1,0:T(8,128)}, u32[]{:S(2)}) copy-start(f32[24,24,256]{2,1,0:T(8,128)} %guess.5) | copy-start | bytes 1769476
  21.8 13.4 %copy-start.3 = (f32[24,24,256]{2,1,0:T(8,128)S(1)}, f32[24,24,256]{2,1,0:T(8,128)}, u32[]{:S(2)}) copy-start(f32[24,24,256]{2,1,0:T(8,128)} %load.5) | copy-start | bytes 1769476
  21.9 13.2 %collective-permute-start.4 = (f32[1248,128]{1,0:T(8,128)S(1)}, f32[1248,128]{1,0:T(8,128)S(1)}, u32[]{:S(2)}, u32[]{:S(2)}) collective-permute-start(f32[1248,128]{1,0:T(8,128)S(1)} %get-tuple-element.32), channel_id=1, source_target_pairs={{0,4},{4,8},{8,12},{12,16},{16,20},{20,24},{24,28},{28,32},{32,36}... | collective-permute-start | bytes 1916936 | tf_op jit(solution)/shard_map/ppermute | solution.py:611
  22.5 12.4 %collective-permute-start.5 = (f32[1152,128]{1,0:T(8,128)S(1)}, f32[1152,128]{1,0:T(8,128)S(1)}, u32[]{:S(2)}, u32[]{:S(2)}) collective-permute-start(f32[1152,128]{1,0:T(8,128)S(1)} %get-tuple-element.33), channel_id=1, source_target_pairs={{0,124},{4,0},{8,4},{12,8},{16,12},{20,16},{24,20},{28,24},{32,28}... | collective-permute-start | bytes 1769480 | tf_op jit(solution)/shard_map/ppermute | solution.py:611
  55.9 4.7 %collective-permute-start.6 = (f32[12,12,128]{2,1,0:T(8,128)S(1)}, f32[12,12,128]{2,1,0:T(8,128)S(1)}, u32[]{:S(2)}, u32[]{:S(2)}) collective-permute-start(f32[12,12,128]{2,1,0:T(8,128)S(1)} %get-tuple-element.35), channel_id=1, source_target_pairs={{0,1},{1,2},{2,3},{3,0},{4,5},{5,6},{6,7},{7,4},{8,9},{9,10},{10,1... | collective-permute-start | bytes 221192 | tf_op jit(solution)/shard_map/ppermute | solution.py:611
  56.5 5.8 %collective-permute-start.7 = (f32[12,12,128]{2,1,0:T(8,128)S(1)}, f32[12,12,128]{2,1,0:T(8,128)S(1)}, u32[]{:S(2)}, u32[]{:S(2)}) collective-permute-start(f32[12,12,128]{2,1,0:T(8,128)S(1)} %get-tuple-element.35), channel_id=1, source_target_pairs={{0,3},{1,0},{2,1},{3,2},{4,7},{5,4},{6,5},{7,6},{8,11},{9,8},{10,9... | collective-permute-start | bytes 221192 | tf_op jit(solution)/shard_map/ppermute | solution.py:611
  62.4 9.5 %collective-permute-start.8 = (f32[36,12,128]{2,1,0:T(8,128)S(1)}, f32[36,12,128]{2,1,0:T(8,128)S(1)}, u32[]{:S(2)}, u32[]{:S(2)}) collective-permute-start(f32[36,12,128]{2,1,0:T(8,128)S(1)} %constant_dynamic-update-slice_fusion.own.f1_own), channel_id=1, source_target_pairs={{0,4},{4,8},{8,12},{12,16},{16,20},{20,24},{24,28},{28,32},{32,36}... | collective-permute-start | bytes 663560 | tf_op jit(solution)/shard_map/ppermute | solution.py:611
  62.4 11.6 %collective-permute-start.11 = (f32[36,12,128]{2,1,0:T(8,128)S(1)}, f32[36,12,128]{2,1,0:T(8,128)S(1)}, u32[]{:S(2)}, u32[]{:S(2)}) collective-permute-start(f32[36,12,128]{2,1,0:T(8,128)S(1)} %constant_dynamic-update-slice_fusion.own.f1_own), channel_id=1, source_target_pairs={{0,124},{4,0},{8,4},{12,8},{16,12},{20,16},{24,20},{28,24},{32,28}... | collective-permute-start | bytes 663560 | tf_op jit(solution)/shard_map/ppermute | solution.py:611
  71.9 6.0 %collective-permute-start.9 = (f32[9,24,256]{2,1,0:T(8,128)S(1)}, f32[9,24,256]{2,1,0:T(8,128)S(1)}, u32[]{:S(2)}, u32[]{:S(2)}) collective-permute-start(f32[9,24,256]{2,1,0:T(8,128)S(1)} %get-tuple-element.45), channel_id=1, source_target_pairs={{0,1},{1,2},{2,3},{3,0},{4,5},{5,6},{6,7},{7,4},{8,9},{9,10},{10,1... | collective-permute-start | bytes 663560 | tf_op jit(solution)/shard_map/ppermute | solution.py:611
  72.2 7.1 %collective-permute-start.10 = (f32[9,24,256]{2,1,0:T(8,128)S(1)}, f32[9,24,256]{2,1,0:T(8,128)S(1)}, u32[]{:S(2)}, u32[]{:S(2)}) collective-permute-start(f32[9,24,256]{2,1,0:T(8,128)S(1)} %get-tuple-element.46), channel_id=1, source_target_pairs={{0,3},{1,0},{2,1},{3,2},{4,7},{5,4},{6,5},{7,6},{8,11},{9,8},{10,9... | collective-permute-start | bytes 663560 | tf_op jit(solution)/shard_map/ppermute | solution.py:611
  100.1 2.1 %collective-permute-start.14 = (f32[64,18,128]{2,0,1:T(8,128)S(1)}, f32[64,18,128]{2,0,1:T(8,128)S(1)}, u32[]{:S(2)}, u32[]{:S(2)}) collective-permute-start(f32[64,18,128]{2,0,1:T(8,128)S(1)} %copy.13), channel_id=1, source_target_pairs={{0,4},{4,0},{1,5},{5,1},{2,6},{6,2},{3,7},{7,3},{8,12},{12,8},{9,1... | collective-permute-start | bytes 1769480 | tf_op jit(solution)/shard_map/ppermute | solution.py:725
  100.3 34.0 %collective-permute-start.13 = (f32[42,16,256]{2,1,0:T(8,128)S(1)}, f32[42,16,256]{2,1,0:T(8,128)S(1)}, u32[]{:S(2)}, u32[]{:S(2)}) collective-permute-start(f32[42,16,256]{2,1,0:T(8,128)S(1)} %get-tuple-element.43), channel_id=1, source_target_pairs={{0,124},{4,0},{8,4},{12,8},{16,12},{20,16},{24,20},{28,24},{32,28}... | collective-permute-start | bytes 2064392 | tf_op jit(solution)/shard_map/ppermute | solution.py:611
  101.8 32.5 %collective-permute-start.12 = (f32[42,16,256]{2,1,0:T(8,128)S(1)}, f32[42,16,256]{2,1,0:T(8,128)S(1)}, u32[]{:S(2)}, u32[]{:S(2)}) collective-permute-start(f32[42,16,256]{2,1,0:T(8,128)S(1)} %get-tuple-element.44), channel_id=1, source_target_pairs={{0,4},{4,8},{8,12},{12,16},{16,20},{20,24},{24,28},{28,32},{32,36}... | collective-permute-start | bytes 2064392 | tf_op jit(solution)/shard_map/ppermute | solution.py:611
  122.6 4.9 %collective-permute-start.15 = (f32[9,12,128]{2,1,0:T(8,128)S(1)}, f32[9,12,128]{2,1,0:T(8,128)S(1)}, u32[]{:S(2)}, u32[]{:S(2)}) collective-permute-start(f32[9,12,128]{2,1,0:T(8,128)S(1)} %get-tuple-element.47), channel_id=1, source_target_pairs={{0,1},{1,2},{2,3},{3,0},{4,5},{5,6},{6,7},{7,4},{8,9},{9,10},{10,1... | collective-permute-start | bytes 165896 | tf_op jit(solution)/shard_map/ppermute | solution.py:611
  125.0 5.8 %collective-permute-start.16 = (f32[9,12,128]{2,1,0:T(8,128)S(1)}, f32[9,12,128]{2,1,0:T(8,128)S(1)}, u32[]{:S(2)}, u32[]{:S(2)}) collective-permute-start(f32[9,12,128]{2,1,0:T(8,128)S(1)} %get-tuple-element.48), channel_id=1, source_target_pairs={{0,3},{1,0},{2,1},{3,2},{4,7},{5,4},{6,5},{7,6},{8,11},{9,8},{10,9... | collective-permute-start | bytes 165896 | tf_op jit(solution)/shard_map/ppermute | solution.py:611
  130.8 11.1 %collective-permute-start.18 = (f32[30,9,128]{2,1,0:T(8,128)S(1)}, f32[30,9,128]{2,1,0:T(8,128)S(1)}, u32[]{:S(2)}, u32[]{:S(2)}) collective-permute-start(f32[30,9,128]{2,1,0:T(8,128)S(1)} %bitcast.12), channel_id=1, source_target_pairs={{0,124},{4,0},{8,4},{12,8},{16,12},{20,16},{24,20},{28,24},{32,28}... | collective-permute-start | bytes 414728 | tf_op jit(solution)/shard_map/ppermute | solution.py:611
  133.9 7.9 %collective-permute-start.17 = (f32[30,8,128]{2,1,0:T(8,128)S(1)}, f32[30,8,128]{2,1,0:T(8,128)S(1)}, u32[]{:S(2)}, u32[]{:S(2)}) collective-permute-start(f32[30,8,128]{2,1,0:T(8,128)S(1)} %slice.62), channel_id=1, source_target_pairs={{0,4},{4,8},{8,12},{12,16},{16,20},{20,24},{24,28},{28,32},{32,36}... | collective-permute-start | bytes 368648 | tf_op jit(solution)/shard_map/ppermute | solution.py:611

commit v6 on v5

--- a/solution.py
+++ b/solution.py
@@ -116,14 +116,7 @@
 
             start = [plane(u0 - 3 + k) for k in range(6)]
             carry = tuple([p for p, _ in start] + [q for _, q in start])
-            group = nu // 3 if nu >= 18 else nu
-            groups = nu // group
-            if groups > 1:
-                carry = lax.fori_loop(0, groups, lambda g, c: several(group * g, group, c), carry)
-            else:
-                carry = several(0, group, carry)
-            if nu % group:
-                several(group * groups, nu % group, carry)
+            several(0, nu, carry)
 
 
 def stencil_pairs(x_ref, l_ref, k0, nk, v0, nv):
@@ -163,10 +156,7 @@
             return tuple(value for t in planes for value in t)
 
         carry = tuple(value for i in range(4) for value in plane(k0 - 2 + i))
-        if nk > 6:
-            lax.fori_loop(0, nk // 4, lambda g, c: several(4 * g, 4, c), carry)
-        else:
-            several(0, nk, carry)
+        several(0, nk, carry)
 
 
 def finish(l_ref, w_ref, nu, nv, use):

time: 161 us -> 150 us (0.932)
  Pallas kernels: 61.1 us -> 50 us
    pallas_call x7, Pallas kernels: 61.1 us -> 50 us  [call(): pl.pallas_call(body, out_shape=list(outs), in_specs=[vmem] * len(operands...]
  transfers between devices with their start and end apart: 19 -> 19, of which waited for: 13 -> 13; matrix products, arithmetic and copies ran while one was open for 0% -> 0% of each run, Pallas kernels for 15% -> 11%
where the time goes in v6:
time: 150 us; the launch traced here: 147 us
  Pallas kernels  50 us (33%)
  waiting for transfers between devices  42.2 us (28%)
  starting transfers between devices  29.9 us (20%)
  blocking collectives  20.5 us (14%)
  local copies, waits for them, and re-layouts  3.77 us (3%)
    pallas_call x7, Pallas kernels, call(): pl.pallas_call(body, out_shape=list(outs), in_specs=[vmem] * len(operands...  50 us
    ppermute x18, waiting for transfers between devices, ring(): return lax.ppermute(value, axes if len(axes) > 1 else axes[0], pairs)  42 us
    ppermute x18, starting transfers between devices, ring(): return lax.ppermute(value, axes if len(axes) > 1 else axes[0], pairs)  29.9 us
    all_to_all x1, blocking collectives, on_device(): same = lax.all_to_all(f2, ('pz', 'dir'), 0, 0)  20.5 us
  transfers between devices with their start and end apart: 19, of which 13 were waited for; matrix products, arithmetic and copies ran while one was open for 0% of the time, Pallas kernels for 11%

profile of v6, /device:TPU:6, one launch (start us, length us, event | category | flops | bytes accessed | tf_op | source)
XLA Modules:
  0.0 147.4 jit_solution(3664423227049755010)
XLA Ops:
  0.0 0.8 copy.11
  0.9 1.1 copy-done
  2.0 1.1 copy-done.2
  3.0 1.2 shard_map.46
  4.2 0.4 collective-permute-start
  4.6 1.6 %collective-permute-start.1 = (f32[24,24,256]{2,1,0:T(8,128)}, f32[24,24,256]{2,1,0:T(8,128)S(1)}, u32[]{:S(2)}, u32[]{:S(2)}) collective-permute-start(f32[24,24,256]{2,1,0:T(8,128)} %get-tuple-element.25), channel_id=1, source_target_pairs={{0,3},{1,0},{2,1},{3,2},{4,7},{5,4},{6,5},{7,6},{8,11},{9,8},{10,9... | collective-permute-start | bytes 1769480 | tf_op jit(solution)/shard_map/ppermute | solution.py:601
  6.2 5.4 %collective-permute-start.3 = (f32[1104,128]{1,0:T(8,128)}, f32[1104,128]{1,0:T(8,128)}, u32[]{:S(2)}, u32[]{:S(2)}) collective-permute-start(f32[1104,128]{1,0:T(8,128)} %get-tuple-element.27), channel_id=1, source_target_pairs={{0,124},{4,0},{8,4},{12,8},{16,12},{20,16},{24,20},{28,24},{32,28}... | collective-permute-start | bytes 1695752 | tf_op jit(solution)/shard_map/ppermute | solution.py:601
  11.6 7.4 %collective-permute-done.3.own_down = f32[1104,128]{1,0:T(8,128)} collective-permute-done((f32[1104,128]{1,0:T(8,128)}, f32[1104,128]{1,0:T(8,128)}, u32[]{:S(2)}, u32[]{:S(2)}) %collective-permute-start.3) | collective-permute-done | bytes 565280 | tf_op jit(solution)/shard_map/ppermute | solution.py:601
  19.1 2.4 %collective-permute-done.1.high = f32[24,24,256]{2,1,0:T(8,128)S(1)} collective-permute-done((f32[24,24,256]{2,1,0:T(8,128)}, f32[24,24,256]{2,1,0:T(8,128)S(1)}, u32[]{:S(2)}, u32[]{:S(2)}) %collective-permute-start.1) | collective-permute-done | bytes 589856 | tf_op jit(solution)/shard_map/ppermute | solution.py:601
  21.5 0.1 slice.56
  21.6 0.1 maximum_multiply_fusion.1
  21.7 0.1 maximum_multiply_fusion
  21.8 0.1 shard_map.47
  21.9 0.7 collective-permute-start.4
  22.5 4.9 %collective-permute-start.5 = (f32[1152,128]{1,0:T(8,128)S(1)}, f32[1152,128]{1,0:T(8,128)S(1)}, u32[]{:S(2)}, u32[]{:S(2)}) collective-permute-start(f32[1152,128]{1,0:T(8,128)S(1)} %get-tuple-element.33), channel_id=1, source_target_pairs={{0,124},{4,0},{8,4},{12,8},{16,12},{20,16},{24,20},{28,24},{32,28}... | collective-permute-start | bytes 1769480 | tf_op jit(solution)/shard_map/ppermute | solution.py:601
  27.5 7.4 %collective-permute-done.5.down = f32[1152,128]{1,0:T(8,128)S(1)} collective-permute-done((f32[1152,128]{1,0:T(8,128)S(1)}, f32[1152,128]{1,0:T(8,128)S(1)}, u32[]{:S(2)}, u32[]{:S(2)}) %collective-permute-start.5) | collective-permute-done | bytes 589856 | tf_op jit(solution)/shard_map/ppermute | solution.py:601
  34.9 0.2 collective-permute-done.4.up
  35.1 18.2 %shard_map.48 = (f32[24,24,256]{2,1,0:T(8,128)S(1)}, f32[12,12,128]{2,1,0:T(8,128)S(1)}, f32[40,128]{1,0:T(8,128)S(1)}) custom-call(f32[24,24,256]{2,1,0:T(8,128)S(1)} %copy-done.1, f32[24,24,256]{2,1,0:T(8,128)S(1)} %copy-done.3, f32[26,24,256]{2,1,0:T(8,128)S(1)} %collective-permute-done.low, f32[24,24,256]{2,1,0:T(8,128)S(1)} %collective-permute-done.1.high, ...), custom_call_target="tpu_custom_call" | custom-call | flops 10000000000 | bytes 22474752 | tf_op jit(solution)/shard_map/pallas_call | solution.py:581
  53.3 0.6 collective-permute-start.6
  53.9 1.5 %collective-permute-start.7 = (f32[12,12,128]{2,1,0:T(8,128)S(1)}, f32[12,12,128]{2,1,0:T(8,128)S(1)}, u32[]{:S(2)}, u32[]{:S(2)}) collective-permute-start(f32[12,12,128]{2,1,0:T(8,128)S(1)} %get-tuple-element.35), channel_id=1, source_target_pairs={{0,3},{1,0},{2,1},{3,2},{4,7},{5,4},{6,5},{7,6},{8,11},{9,8},{10,9... | collective-permute-start | bytes 221192 | tf_op jit(solution)/shard_map/ppermute | solution.py:601
  55.4 2.6 %collective-permute-done.6 = f32[12,12,128]{2,1,0:T(8,128)S(1)} collective-permute-done((f32[12,12,128]{2,1,0:T(8,128)S(1)}, f32[12,12,128]{2,1,0:T(8,128)S(1)}, u32[]{:S(2)}, u32[]{:S(2)}) %collective-permute-start.6) | collective-permute-done | bytes 73760 | tf_op jit(solution)/shard_map/ppermute | solution.py:601
  58.1 1.7 %collective-permute-done.7 = f32[12,12,128]{2,1,0:T(8,128)S(1)} collective-permute-done((f32[12,12,128]{2,1,0:T(8,128)S(1)}, f32[12,12,128]{2,1,0:T(8,128)S(1)}, u32[]{:S(2)}, u32[]{:S(2)}) %collective-permute-start.7) | collective-permute-done | bytes 73760 | tf_op jit(solution)/shard_map/ppermute | solution.py:601
  59.8 0.1 collective-permute-start.8
  59.9 5.1 %collective-permute-start.11 = (f32[36,12,128]{2,1,0:T(8,128)S(1)}, f32[36,12,128]{2,1,0:T(8,128)S(1)}, u32[]{:S(2)}, u32[]{:S(2)}) collective-permute-start(f32[36,12,128]{2,1,0:T(8,128)S(1)} %constant_dynamic-update-slice_fusion.own.f1_own), channel_id=1, source_target_pairs={{0,124},{4,0},{8,4},{12,8},{16,12},{20,16},{24,20},{28,24},{32,28}... | collective-permute-start | bytes 663560 | tf_op jit(solution)/shard_map/ppermute | solution.py:601
  64.9 4.4 %collective-permute-done.8.low.f1_low = f32[36,12,128]{2,1,0:T(8,128)S(1)} collective-permute-done((f32[36,12,128]{2,1,0:T(8,128)S(1)}, f32[36,12,128]{2,1,0:T(8,128)S(1)}, u32[]{:S(2)}, u32[]{:S(2)}) %collective-permute-start.8) | collective-permute-done | bytes 221216 | tf_op jit(solution)/shard_map/ppermute | solution.py:601
  69.4 0.3 collective-permute-start.9
  69.6 1.8 %collective-permute-start.10 = (f32[9,24,256]{2,1,0:T(8,128)S(1)}, f32[9,24,256]{2,1,0:T(8,128)S(1)}, u32[]{:S(2)}, u32[]{:S(2)}) collective-permute-start(f32[9,24,256]{2,1,0:T(8,128)S(1)} %get-tuple-element.46), channel_id=1, source_target_pairs={{0,3},{1,0},{2,1},{3,2},{4,7},{5,4},{6,5},{7,6},{8,11},{9,8},{10,9... | collective-permute-start | bytes 663560 | tf_op jit(solution)/shard_map/ppermute | solution.py:601
  71.5 2.8 %shard_map.49 = (f32[24,24,128]{2,1,0:T(8,128)S(1)}, f32[64,18,128]{2,1,0:T(8,128)S(1)}) custom-call(f32[36,12,128]{2,1,0:T(8,128)S(1)} %constant_dynamic-update-slice_fusion.own.f1_own, f32[36,12,128]{2,1,0:T(8,128)S(1)} %collective-permute-done.8.low.f1_low, f32[36,12,128]{2,1,0:T(8,128)S(1)} %collective-permute-done.11.high.f1_high, ...), custom_call_target="tpu_custom_call" | custom-call | flops 1000000000 | bytes 6307840 | tf_op jit(solution)/shard_map/pallas_call | solution.py:581
  74.3 1.0 collective-permute-done.9
  75.4 1.4 collective-permute-done.10
  76.8 0.1 pad_maximum_fusion.x_own
  76.9 20.5 %all_to_all.5.same = f32[64,18,128]{2,1,0:T(8,128)S(1)} all-to-all(f32[64,18,128]{2,1,0:T(8,128)S(1)} %get-tuple-element.42), channel_id=1, replica_groups=mesh['pz'=16,'core'=2,'dir'=4] {'pz','dir'}, dimensions={0} | all-to-all | bytes 1179648 | tf_op jit(solution)/shard_map/all_to_all | solution.py:714
  97.4 0.1 copy.13
  97.5 0.1 collective-permute-start.14
  97.6 0.1 fusion.1
  97.7 1.5 collective-permute-start.13
  99.2 0.2 collective-permute-start.12
  99.4 0.2 collective-permute-done.14
  99.6 0.4 copy.14.other
  99.9 11.8 %shard_map.50.e2 = f32[17,24,128]{2,1,0:T(8,128)S(1)} custom-call(f32[64,18,128]{2,1,0:T(8,128)S(1)} %all_to_all.5.same, f32[64,18,128]{2,1,0:T(8,128)S(1)} %copy.14.other), custom_call_target="tpu_custom_call" | custom-call | flops 4000000000 | bytes 8708096 | tf_op jit(solution)/shard_map/pallas_call | solution.py:581
  111.8 1.6 %shard_map.51 = f32[12,12,128]{2,1,0:T(8,128)S(1)} custom-call(f32[36,12,128]{2,1,0:T(8,128)S(1)} %constant_dynamic-update-slice_fusion.own.f1_own, f32[36,12,128]{2,1,0:T(8,128)S(1)} %collective-permute-done.8.low.f1_low, f32[36,12,128]{2,1,0:T(8,128)S(1)} %collective-permute-done.11.high.f1_high, f32[40,128]{1,0:T(8,128)S(1)} %get-tuple-element.38.mask.mask1, ...), custom_call_target="tpu_custom_call" | custom-call | flops 1000000000 | bytes 6168576 | tf_op jit(solution)/shard_map/pallas_call | solution.py:581
  113.3 2.4 %collective-permute-start.15 = (f32[9,12,128]{2,1,0:T(8,128)S(1)}, f32[9,12,128]{2,1,0:T(8,128)S(1)}, u32[]{:S(2)}, u32[]{:S(2)}) collective-permute-start(f32[9,12,128]{2,1,0:T(8,128)S(1)} %get-tuple-element.47), channel_id=1, source_target_pairs={{0,1},{1,2},{2,3},{3,0},{4,5},{5,6},{6,7},{7,4},{8,9},{9,10},{10,1... | collective-permute-start | bytes 165896 | tf_op jit(solution)/shard_map/ppermute | solution.py:601
  115.7 2.5 %collective-permute-done.15 = f32[9,12,128]{2,1,0:T(8,128)S(1)} collective-permute-done((f32[9,12,128]{2,1,0:T(8,128)S(1)}, f32[9,12,128]{2,1,0:T(8,128)S(1)}, u32[]{:S(2)}, u32[]{:S(2)}) %collective-permute-start.15) | collective-permute-done | bytes 55328 | tf_op jit(solution)/shard_map/ppermute | solution.py:601
  118.2 3.3 %collective-permute-done.16 = f32[9,12,128]{2,1,0:T(8,128)S(1)} collective-permute-done((f32[9,12,128]{2,1,0:T(8,128)S(1)}, f32[9,12,128]{2,1,0:T(8,128)S(1)}, u32[]{:S(2)}, u32[]{:S(2)}) %collective-permute-start.16) | collective-permute-done | bytes 55328 | tf_op jit(solution)/shard_map/ppermute | solution.py:601
  121.5 3.2 %collective-permute-start.18 = (f32[30,9,128]{2,1,0:T(8,128)S(1)}, f32[30,9,128]{2,1,0:T(8,128)S(1)}, u32[]{:S(2)}, u32[]{:S(2)}) collective-permute-start(f32[30,9,128]{2,1,0:T(8,128)S(1)} %bitcast.12), channel_id=1, source_target_pairs={{0,124},{4,0},{8,4},{12,8},{16,12},{20,16},{24,20},{28,24},{32,28}... | collective-permute-start | bytes 414728 | tf_op jit(solution)/shard_map/ppermute | solution.py:601
  124.7 0.3 collective-permute-start.17
  125.1 7.6 %collective-permute-done.17.y_low = f32[30,8,128]{2,1,0:T(8,128)S(1)} collective-permute-done((f32[30,8,128]{2,1,0:T(8,128)S(1)}, f32[30,8,128]{2,1,0:T(8,128)S(1)}, u32[]{:S(2)}, u32[]{:S(2)}) %collective-permute-start.17) | collective-permute-done | bytes 122912 | tf_op jit(solution)/shard_map/ppermute | solution.py:601
  132.7 14.3 %shard_map.52 = f32[24,24,256]{2,1,0:T(8,128)} custom-call(f32[24,24,256]{2,1,0:T(8,128)S(1)} %copy-done.1, f32[24,24,256]{2,1,0:T(8,128)S(1)} %copy-done.3, f32[26,24,256]{2,1,0:T(8,128)S(1)} %collective-permute-done.low, f32[24,24,256]{2,1,0:T(8,128)S(1)} %collective-permute-done.1.high, f32[1200,128]{1,0:T(8,128)S(1)} %collective-permute-done.2.own_up, ...), custom_call_target="tpu_custom_call" | custom-call | flops 10000000000 | bytes 31617024 | tf_op jit(solution)/shard_map/pallas_call | solution.py:581
  (34 shorter events, 0.3 us)
Async XLA Ops:
  0.0 0.8 copy-start.4
  0.9 1.1 copy-start
  2.0 1.1 copy-start.2
  4.2 17.2 %collective-permute-start = (f32[26,24,256]{2,1,0:T(8,128)S(1)}, f32[26,24,256]{2,1,0:T(8,128)S(1)}, u32[]{:S(2)}, u32[]{:S(2)}) collective-permute-start(f32[26,24,256]{2,1,0:T(8,128)S(1)} %get-tuple-element.24), channel_id=1, source_target_pairs={{0,1},{1,2},{2,3},{3,0},{4,5},{5,6},{6,7},{7,4},{8,9},{9,10},{10,1... | collective-permute-start | bytes 1916936 | tf_op jit(solution)/shard_map/ppermute | solution.py:601
  4.6 16.9 %collective-permute-start.2 = (f32[1200,128]{1,0:T(8,128)S(1)}, f32[1200,128]{1,0:T(8,128)S(1)}, u32[]{:S(2)}, u32[]{:S(2)}) collective-permute-start(f32[1200,128]{1,0:T(8,128)S(1)} %get-tuple-element.26), channel_id=1, source_target_pairs={{0,4},{4,8},{8,12},{12,16},{16,20},{20,24},{24,28},{28,32},{32,36}... | collective-permute-start | bytes 1843208 | tf_op jit(solution)/shard_map/ppermute | solution.py:601
  4.6 16.8 %collective-permute-start.1 = (f32[24,24,256]{2,1,0:T(8,128)}, f32[24,24,256]{2,1,0:T(8,128)S(1)}, u32[]{:S(2)}, u32[]{:S(2)}) collective-permute-start(f32[24,24,256]{2,1,0:T(8,128)} %get-tuple-element.25), channel_id=1, source_target_pairs={{0,3},{1,0},{2,1},{3,2},{4,7},{5,4},{6,5},{7,6},{8,11},{9,8},{10,9... | collective-permute-start | bytes 1769480 | tf_op jit(solution)/shard_map/ppermute | solution.py:601
  6.2 12.8 %collective-permute-start.3 = (f32[1104,128]{1,0:T(8,128)}, f32[1104,128]{1,0:T(8,128)}, u32[]{:S(2)}, u32[]{:S(2)}) collective-permute-start(f32[1104,128]{1,0:T(8,128)} %get-tuple-element.27), channel_id=1, source_target_pairs={{0,124},{4,0},{8,4},{12,8},{16,12},{20,16},{24,20},{28,24},{32,28}... | collective-permute-start | bytes 1695752 | tf_op jit(solution)/shard_map/ppermute | solution.py:601
  21.7 13.4 %copy-start.1 = (f32[24,24,256]{2,1,0:T(8,128)S(1)}, f32[24,24,256]{2,1,0:T(8,128)}, u32[]{:S(2)}) copy-start(f32[24,24,256]{2,1,0:T(8,128)} %guess.5) | copy-start | bytes 1769476
  21.8 13.4 %copy-start.3 = (f32[24,24,256]{2,1,0:T(8,128)S(1)}, f32[24,24,256]{2,1,0:T(8,128)}, u32[]{:S(2)}) copy-start(f32[24,24,256]{2,1,0:T(8,128)} %load.5) | copy-start | bytes 1769476
  21.9 13.2 %collective-permute-start.4 = (f32[1248,128]{1,0:T(8,128)S(1)}, f32[1248,128]{1,0:T(8,128)S(1)}, u32[]{:S(2)}, u32[]{:S(2)}) collective-permute-start(f32[1248,128]{1,0:T(8,128)S(1)} %get-tuple-element.32), channel_id=1, source_target_pairs={{0,4},{4,8},{8,12},{12,16},{16,20},{20,24},{24,28},{28,32},{32,36}... | collective-permute-start | bytes 1916936 | tf_op jit(solution)/shard_map/ppermute | solution.py:601
  22.5 12.3 %collective-permute-start.5 = (f32[1152,128]{1,0:T(8,128)S(1)}, f32[1152,128]{1,0:T(8,128)S(1)}, u32[]{:S(2)}, u32[]{:S(2)}) collective-permute-start(f32[1152,128]{1,0:T(8,128)S(1)} %get-tuple-element.33), channel_id=1, source_target_pairs={{0,124},{4,0},{8,4},{12,8},{16,12},{20,16},{24,20},{28,24},{32,28}... | collective-permute-start | bytes 1769480 | tf_op jit(solution)/shard_map/ppermute | solution.py:601
  53.3 4.7 %collective-permute-start.6 = (f32[12,12,128]{2,1,0:T(8,128)S(1)}, f32[12,12,128]{2,1,0:T(8,128)S(1)}, u32[]{:S(2)}, u32[]{:S(2)}) collective-permute-start(f32[12,12,128]{2,1,0:T(8,128)S(1)} %get-tuple-element.35), channel_id=1, source_target_pairs={{0,1},{1,2},{2,3},{3,0},{4,5},{5,6},{6,7},{7,4},{8,9},{9,10},{10,1... | collective-permute-start | bytes 221192 | tf_op jit(solution)/shard_map/ppermute | solution.py:601
  53.9 5.8 %collective-permute-start.7 = (f32[12,12,128]{2,1,0:T(8,128)S(1)}, f32[12,12,128]{2,1,0:T(8,128)S(1)}, u32[]{:S(2)}, u32[]{:S(2)}) collective-permute-start(f32[12,12,128]{2,1,0:T(8,128)S(1)} %get-tuple-element.35), channel_id=1, source_target_pairs={{0,3},{1,0},{2,1},{3,2},{4,7},{5,4},{6,5},{7,6},{8,11},{9,8},{10,9... | collective-permute-start | bytes 221192 | tf_op jit(solution)/shard_map/ppermute | solution.py:601
  59.8 9.5 %collective-permute-start.8 = (f32[36,12,128]{2,1,0:T(8,128)S(1)}, f32[36,12,128]{2,1,0:T(8,128)S(1)}, u32[]{:S(2)}, u32[]{:S(2)}) collective-permute-start(f32[36,12,128]{2,1,0:T(8,128)S(1)} %constant_dynamic-update-slice_fusion.own.f1_own), channel_id=1, source_target_pairs={{0,4},{4,8},{8,12},{12,16},{16,20},{20,24},{24,28},{28,32},{32,36}... | collective-permute-start | bytes 663560 | tf_op jit(solution)/shard_map/ppermute | solution.py:601
  59.9 11.6 %collective-permute-start.11 = (f32[36,12,128]{2,1,0:T(8,128)S(1)}, f32[36,12,128]{2,1,0:T(8,128)S(1)}, u32[]{:S(2)}, u32[]{:S(2)}) collective-permute-start(f32[36,12,128]{2,1,0:T(8,128)S(1)} %constant_dynamic-update-slice_fusion.own.f1_own), channel_id=1, source_target_pairs={{0,124},{4,0},{8,4},{12,8},{16,12},{20,16},{24,20},{28,24},{32,28}... | collective-permute-start | bytes 663560 | tf_op jit(solution)/shard_map/ppermute | solution.py:601
  69.4 6.0 %collective-permute-start.9 = (f32[9,24,256]{2,1,0:T(8,128)S(1)}, f32[9,24,256]{2,1,0:T(8,128)S(1)}, u32[]{:S(2)}, u32[]{:S(2)}) collective-permute-start(f32[9,24,256]{2,1,0:T(8,128)S(1)} %get-tuple-element.45), channel_id=1, source_target_pairs={{0,1},{1,2},{2,3},{3,0},{4,5},{5,6},{6,7},{7,4},{8,9},{9,10},{10,1... | collective-permute-start | bytes 663560 | tf_op jit(solution)/shard_map/ppermute | solution.py:601
  69.6 7.1 %collective-permute-start.10 = (f32[9,24,256]{2,1,0:T(8,128)S(1)}, f32[9,24,256]{2,1,0:T(8,128)S(1)}, u32[]{:S(2)}, u32[]{:S(2)}) collective-permute-start(f32[9,24,256]{2,1,0:T(8,128)S(1)} %get-tuple-element.46), channel_id=1, source_target_pairs={{0,3},{1,0},{2,1},{3,2},{4,7},{5,4},{6,5},{7,6},{8,11},{9,8},{10,9... | collective-permute-start | bytes 663560 | tf_op jit(solution)/shard_map/ppermute | solution.py:601
  97.5 2.1 %collective-permute-start.14 = (f32[64,18,128]{2,0,1:T(8,128)S(1)}, f32[64,18,128]{2,0,1:T(8,128)S(1)}, u32[]{:S(2)}, u32[]{:S(2)}) collective-permute-start(f32[64,18,128]{2,0,1:T(8,128)S(1)} %copy.13), channel_id=1, source_target_pairs={{0,4},{4,0},{1,5},{5,1},{2,6},{6,2},{3,7},{7,3},{8,12},{12,8},{9,1... | collective-permute-start | bytes 1769480 | tf_op jit(solution)/shard_map/ppermute | solution.py:715
  97.7 27.3 %collective-permute-start.13 = (f32[42,16,256]{2,1,0:T(8,128)S(1)}, f32[42,16,256]{2,1,0:T(8,128)S(1)}, u32[]{:S(2)}, u32[]{:S(2)}) collective-permute-start(f32[42,16,256]{2,1,0:T(8,128)S(1)} %get-tuple-element.43), channel_id=1, source_target_pairs={{0,124},{4,0},{8,4},{12,8},{16,12},{20,16},{24,20},{28,24},{32,28}... | collective-permute-start | bytes 2064392 | tf_op jit(solution)/shard_map/ppermute | solution.py:601
  99.2 25.9 %collective-permute-start.12 = (f32[42,16,256]{2,1,0:T(8,128)S(1)}, f32[42,16,256]{2,1,0:T(8,128)S(1)}, u32[]{:S(2)}, u32[]{:S(2)}) collective-permute-start(f32[42,16,256]{2,1,0:T(8,128)S(1)} %get-tuple-element.44), channel_id=1, source_target_pairs={{0,4},{4,8},{8,12},{12,16},{16,20},{20,24},{24,28},{28,32},{32,36}... | collective-permute-start | bytes 2064392 | tf_op jit(solution)/shard_map/ppermute | solution.py:601
  113.3 4.9 %collective-permute-start.15 = (f32[9,12,128]{2,1,0:T(8,128)S(1)}, f32[9,12,128]{2,1,0:T(8,128)S(1)}, u32[]{:S(2)}, u32[]{:S(2)}) collective-permute-start(f32[9,12,128]{2,1,0:T(8,128)S(1)} %get-tuple-element.47), channel_id=1, source_target_pairs={{0,1},{1,2},{2,3},{3,0},{4,5},{5,6},{6,7},{7,4},{8,9},{9,10},{10,1... | collective-permute-start | bytes 165896 | tf_op jit(solution)/shard_map/ppermute | solution.py:601
  115.7 5.8 %collective-permute-start.16 = (f32[9,12,128]{2,1,0:T(8,128)S(1)}, f32[9,12,128]{2,1,0:T(8,128)S(1)}, u32[]{:S(2)}, u32[]{:S(2)}) collective-permute-start(f32[9,12,128]{2,1,0:T(8,128)S(1)} %get-tuple-element.48), channel_id=1, source_target_pairs={{0,3},{1,0},{2,1},{3,2},{4,7},{5,4},{6,5},{7,6},{8,11},{9,8},{10,9... | collective-permute-start | bytes 165896 | tf_op jit(solution)/shard_map/ppermute | solution.py:601
  121.5 11.1 %collective-permute-start.18 = (f32[30,9,128]{2,1,0:T(8,128)S(1)}, f32[30,9,128]{2,1,0:T(8,128)S(1)}, u32[]{:S(2)}, u32[]{:S(2)}) collective-permute-start(f32[30,9,128]{2,1,0:T(8,128)S(1)} %bitcast.12), channel_id=1, source_target_pairs={{0,124},{4,0},{8,4},{12,8},{16,12},{20,16},{24,20},{28,24},{32,28}... | collective-permute-start | bytes 414728 | tf_op jit(solution)/shard_map/ppermute | solution.py:601
  124.7 7.9 %collective-permute-start.17 = (f32[30,8,128]{2,1,0:T(8,128)S(1)}, f32[30,8,128]{2,1,0:T(8,128)S(1)}, u32[]{:S(2)}, u32[]{:S(2)}) collective-permute-start(f32[30,8,128]{2,1,0:T(8,128)S(1)} %slice.62), channel_id=1, source_target_pairs={{0,4},{4,8},{8,12},{12,16},{16,20},{20,24},{24,28},{28,32},{32,36}... | collective-permute-start | bytes 368648 | tf_op jit(solution)/shard_map/ppermute | solution.py:601
